TPU v7x, 128 devices: a whole 4x4x4 slice. The times are simulated.
128 devices in a mesh: section: 8 (over x, core), tensor: 16 (over z, y).
Axes of the slice: x: 4, y: 4, z: 4, core: 2. Of those that a mesh axis runs over, the one named last changes fastest.
Arguments:
- token_ids: int32 [4, 32], replicated, may hold values from 0 to 511
- block_types: int32 [8], P('section'), may hold values from 0 to 1
- embed_table: bfloat16 [512, 8192], P('section'), may hold values from -6 to 6
- proj_weights: bfloat16 [8, 8192, 4096], P('section', None, 'tensor'), may hold values from -0.0625 to 0.0625
- norm_gains: float32 [8, 8192], P('section'), may hold values from 0.25 to 1.75
- conv_filters: bfloat16 [8, 128, 4096], P('section', None, 'tensor'), may hold values from -0.59765625 to 0.59765625
- conv_caches: bfloat16 [8, 32, 127, 4096], P('section', None, None, 'tensor'), may hold values from -6 to 6
- final_gain: float32 [8192], replicated, may hold values from 0.25 to 1.75
- unembed: bfloat16 [8192, 512], P(None, 'section'), may hold values from -0.1875 to 0.1875
Outputs:
- logits: float32 [4, 32, 512], P(None, None, 'section')
All inputs are finite; a program needn't handle non-finite values.
Results may differ from a plain program's by a relative error of at most 0.02.
Values may be sent and summed in bfloat16 or wider, within the bound.
No kernel may reach another device: no remote copies, remote signals or barrier semaphores. Data moves between devices by JAX's collectives and lax.ppermute only.
A program may use at most 64 MiB of HBM per device.

v0:
```python
import jax
import jax.numpy as jnp
from jax import lax
from jax.sharding import PartitionSpec as P

SHORT = 7
GROUPS = 2


def as_sent(array):
    return jax.tree.map(lambda a: a.astype(jnp.bfloat16) if a.dtype == jnp.float32 else a, array)


def from_behind(block, axis, distance):
    devices = range(lax.axis_size(axis))
    route = [(i - distance, i) for i in devices if i - distance in devices]
    return lax.ppermute(block, axis, route)


def broadcast(block, axis, holder):
    block = jnp.where(lax.axis_index(axis) == holder, block, jnp.zeros_like(block))
    return lax.psum(block, axis)


def rms_scale(values, scale_row):
    values = values.astype(jnp.float32)
    mean_square = jnp.mean(values * values, axis=-1, keepdims=True)
    return values * lax.rsqrt(mean_square + 1e-06) * scale_row


def on_device(
    token_ids,
    block_types,
    embed_table,
    proj_weights,
    norm_gains,
    conv_filters,
    conv_caches,
    final_gain,
    unembed,
):
    section_count = lax.axis_size("section")
    section_index = lax.axis_index("section")
    steps_total, requests = token_ids.shape
    group_count = GROUPS
    step_block = 1
    rows_each = requests // group_count
    item_rows = step_block * rows_each
    items_total = steps_total // step_block * group_count
    vocab_local = embed_table.shape[0]
    model_width = embed_table.shape[1]
    chan_local = proj_weights.shape[2]
    tap_total = conv_filters.shape[1]
    vocab_ids = section_index * vocab_local + jnp.arange(vocab_local, dtype=jnp.int32)
    one_hot = (token_ids[:, :, None] == vocab_ids).astype(jnp.bfloat16)
    partial_embed = jnp.einsum(
        "srv,vd->srd", one_hot, embed_table, preferred_element_type=jnp.float32
    )
    embedded = lax.psum(partial_embed.astype(jnp.bfloat16), "section")
    embedded = embedded.reshape(items_total, item_rows, model_width)
    block_kind = block_types[0]
    tap_mask = jnp.where(block_kind == 1, 1.0, (jnp.arange(tap_total) < SHORT).astype(jnp.float32))
    tap_rows = (conv_filters[0].astype(jnp.float32) * tap_mask[:, None]).astype(jnp.bfloat16)
    flipped = tap_rows[::-1]
    history = conv_caches[0]
    history_len = history.shape[1]
    shifted = jnp.stack(
        [
            jnp.concatenate(
                [jnp.zeros((moment, chan_local), jnp.bfloat16), flipped[: history_len - moment]], 0
            )
            for moment in range(steps_total)
        ]
    )
    cache_terms = jnp.einsum("krc,brc->kbc", shifted, history, preferred_element_type=jnp.float32)
    cache_terms = cache_terms.reshape(items_total, item_rows, chan_local)
    weight = proj_weights[0]
    full_gain = norm_gains[0]

    def convolve(signal, item_index, recent_rows):
        block_start = item_index // group_count * step_block
        group_index = item_index % group_count
        recent_rows = lax.dynamic_update_slice(
            recent_rows,
            signal.reshape(step_block, 1, rows_each, chan_local),
            (block_start, group_index, 0, 0),
        )
        base = lax.dynamic_index_in_dim(cache_terms, item_index, 0, keepdims=False).reshape(
            step_block, rows_each, chan_local
        )
        moment = block_start + 0
        summed = base[0]
        for lag_index in range(steps_total):
            source = jnp.maximum(moment - lag_index, 0)
            earlier = lax.dynamic_slice(
                recent_rows, (source, group_index, 0, 0), (1, 1, rows_each, chan_local)
            )[0, 0]
            summed = summed + jnp.where(
                moment >= lag_index,
                tap_rows[lag_index].astype(jnp.float32) * earlier.astype(jnp.float32),
                0.0,
            )
        outputs = [summed]
        return (jnp.concatenate(outputs, 0), recent_rows)

    empty_partial = jnp.zeros((item_rows, model_width), jnp.float32)

    def skip_section(operands):
        full_rows, carried, recent_rows, item_index = operands
        return (carried, recent_rows, empty_partial)

    def even_section(operands):
        full_rows, carried, recent_rows, item_index = operands
        normed = rms_scale(full_rows, full_gain).astype(jnp.bfloat16)
        projected = jnp.dot(normed, weight, preferred_element_type=jnp.float32).astype(jnp.bfloat16)
        convolved, recent_rows = convolve(projected, item_index, recent_rows)
        return (convolved.astype(jnp.bfloat16), recent_rows, empty_partial)

    def odd_section(operands):
        full_rows, carried, recent_rows, item_index = operands
        mixed_rows, recent_rows = convolve(carried, item_index, recent_rows)
        gated_rows = (carried.astype(jnp.float32) * mixed_rows).astype(jnp.bfloat16)
        partial_value = lax.dot_general(
            gated_rows, weight, (((1,), (1,)), ((), ())), preferred_element_type=jnp.float32
        )
        return (carried, recent_rows, partial_value)

    def one_tick(tick_index, state):
        outgoing, recent_rows, final_rows = state
        received = from_behind(as_sent(outgoing), "section", 1).astype(outgoing.dtype)
        start_item = jnp.minimum(tick_index, items_total - 1)
        fed = lax.dynamic_index_in_dim(embedded, start_item, 0, keepdims=False)
        fed_full = jnp.concatenate([fed, jnp.zeros((item_rows, chan_local), jnp.bfloat16)], 1)
        incoming = jnp.where(section_index == 0, fed_full, received)
        residual = incoming[:, :model_width]
        carried = incoming[:, model_width:]
        item_index = tick_index - section_index
        valid = (item_index >= 0) & (item_index < items_total)
        safe_item = jnp.clip(item_index, 0, items_total - 1)
        full_rows = residual
        branch_index = jnp.where(valid, 1 + section_index % 2, 0)
        carried, recent_rows, partial_value = lax.switch(
            branch_index,
            [skip_section, even_section, odd_section],
            (full_rows, carried, recent_rows, safe_item),
        )
        summed = jax.tree.map(
            lambda part: part.astype(jnp.float32), lax.psum(as_sent(partial_value), "tensor")
        )
        updated_rows = (residual.astype(jnp.float32) + full_gain * summed).astype(jnp.bfloat16)
        residual = jnp.where(valid & (section_index % 2 == 1), updated_rows, residual)
        finished = valid & (section_index == section_count - 1)
        updated = lax.dynamic_update_slice(final_rows, residual[None], (safe_item, 0, 0))
        final_rows = jnp.where(finished, updated, final_rows)
        outgoing = jnp.concatenate([residual, carried], 1)
        return (outgoing, recent_rows, final_rows)

    def two_ticks(turn_index, state):
        state = one_tick(2 * turn_index, state)
        return one_tick(2 * turn_index + 1, state)

    initial = (
        jnp.zeros((item_rows, model_width + chan_local), jnp.bfloat16),
        jnp.zeros((steps_total, group_count, rows_each, chan_local), jnp.bfloat16),
        jnp.zeros((items_total, item_rows, model_width), jnp.bfloat16),
    )
    turn_total = (section_count + items_total) // 2
    outgoing, recent_rows, final_rows = lax.fori_loop(0, turn_total, two_ticks, initial)
    shared_final = broadcast(final_rows, "section", section_count - 1)
    final_seq = shared_final.reshape(steps_total, requests, model_width)
    normed = rms_scale(final_seq, final_gain).astype(jnp.bfloat16)
    return jnp.einsum("srd,dv->srv", normed, unembed, preferred_element_type=jnp.float32)


def solution(mesh):
    placed = (
        P(),
        P("section"),
        P("section", None),
        P("section", None, "tensor"),
        P("section", None),
        P("section", None, "tensor"),
        P("section", None, None, "tensor"),
        P(),
        P(None, "section"),
    )
    return jax.shard_map(
        on_device, mesh=mesh, in_specs=placed, out_specs=P(None, None, "section"), check_vma=False
    )
```

profile of v0, /device:TPU:0, one launch (start us, length us, event | category | flops | bytes accessed | tf_op | source)
XLA Modules:
  0.0 1704.8 jit_solution(7064602011570122457)
XLA Ops:
  14.5 4.4 copy.48
  18.9 3.0 convolution_bitcast_fusion
  23.2 55.6 %all-reduce.10.cloned.1.call-done = bf16[8,16,8192]{2,1,0:T(8,128)(2,1)} async-done(((bf16[8,16,8192]{2,1,0:T(8,128)(2,1)}), bf16[8,16,8192]{2,1,0:T(8,128)(2,1)}) %all-reduce.10.cloned.1.call-update) | async-done | bytes 2097168 | tf_op jit(solution)/shard_map/psum | solution.py:59
  80.3 1544.2 %while.19 = (s32[]{:T(128)}, bf16[16,8448]{1,0:T(8,128)(2,1)S(1)}, bf16[4,2,16,256]{3,2,1,0:T(8,128)(2,1)S(1)}, bf16[8,16,8192]{2,1,0:T(8,128)(2,1)}, s32[]{:T(1...) while((s32[]{:T(128)}, bf16[16,8448]{1,0:T(8,128)(2,1)S(1)}, ...), condition=%wide.region_12.13_spmd, body=%wide.region_1.12_spmd.sunk | while | flops 139651168 | bytes 25092300 | solution.py:168
  83.0 3.2 conditional.4
  87.0 85.2 %all-reduce.14.cloned.1.call-done = bf16[16,8192]{1,0:T(8,128)(2,1)} async-done(((bf16[16,8192]{1,0:T(8,128)(2,1)}), bf16[16,8192]{1,0:T(8,128)(2,1)}) %all-reduce.14.cloned.1.call-update) | async-done | bytes 262160 | tf_op jit(solution)/shard_map/while/body/eval_jaxpr/psum | solution.py:148
  176.6 3.2 conditional.5
  176.9 2.9 fusion.49
  180.6 85.9 %all-reduce.16.cloned.1.call-done = bf16[16,8192]{1,0:T(8,128)(2,1)} async-done(((bf16[16,8192]{1,0:T(8,128)(2,1)}), bf16[16,8192]{1,0:T(8,128)(2,1)}) %all-reduce.16.cloned.1.call-update) | async-done | bytes 262160 | tf_op jit(solution)/shard_map/while/body/eval_jaxpr/psum | solution.py:148
  271.1 3.2 conditional.4
  275.1 87.6 %all-reduce.14.cloned.1.call-done = bf16[16,8192]{1,0:T(8,128)(2,1)} async-done(((bf16[16,8192]{1,0:T(8,128)(2,1)}), bf16[16,8192]{1,0:T(8,128)(2,1)}) %all-reduce.14.cloned.1.call-update) | async-done | bytes 262160 | tf_op jit(solution)/shard_map/while/body/eval_jaxpr/psum | solution.py:148
  367.1 3.2 conditional.5
  367.4 2.9 fusion.49
  371.1 87.6 %all-reduce.16.cloned.1.call-done = bf16[16,8192]{1,0:T(8,128)(2,1)} async-done(((bf16[16,8192]{1,0:T(8,128)(2,1)}), bf16[16,8192]{1,0:T(8,128)(2,1)}) %all-reduce.16.cloned.1.call-update) | async-done | bytes 262160 | tf_op jit(solution)/shard_map/while/body/eval_jaxpr/psum | solution.py:148
  463.2 3.2 conditional.4
  467.2 89.1 %all-reduce.14.cloned.1.call-done = bf16[16,8192]{1,0:T(8,128)(2,1)} async-done(((bf16[16,8192]{1,0:T(8,128)(2,1)}), bf16[16,8192]{1,0:T(8,128)(2,1)}) %all-reduce.14.cloned.1.call-update) | async-done | bytes 262160 | tf_op jit(solution)/shard_map/while/body/eval_jaxpr/psum | solution.py:148
  560.7 3.2 conditional.5
  561.0 2.9 fusion.49
  564.7 89.1 %all-reduce.16.cloned.1.call-done = bf16[16,8192]{1,0:T(8,128)(2,1)} async-done(((bf16[16,8192]{1,0:T(8,128)(2,1)}), bf16[16,8192]{1,0:T(8,128)(2,1)}) %all-reduce.16.cloned.1.call-update) | async-done | bytes 262160 | tf_op jit(solution)/shard_map/while/body/eval_jaxpr/psum | solution.py:148
  658.4 3.2 conditional.4
  662.4 89.1 %all-reduce.14.cloned.1.call-done = bf16[16,8192]{1,0:T(8,128)(2,1)} async-done(((bf16[16,8192]{1,0:T(8,128)(2,1)}), bf16[16,8192]{1,0:T(8,128)(2,1)}) %all-reduce.14.cloned.1.call-update) | async-done | bytes 262160 | tf_op jit(solution)/shard_map/while/body/eval_jaxpr/psum | solution.py:148
  755.9 3.2 conditional.5
  759.9 89.1 %all-reduce.16.cloned.1.call-done = bf16[16,8192]{1,0:T(8,128)(2,1)} async-done(((bf16[16,8192]{1,0:T(8,128)(2,1)}), bf16[16,8192]{1,0:T(8,128)(2,1)}) %all-reduce.16.cloned.1.call-update) | async-done | bytes 262160 | tf_op jit(solution)/shard_map/while/body/eval_jaxpr/psum | solution.py:148
  854.4 92.2 %all-reduce.14.cloned.1.call-done = bf16[16,8192]{1,0:T(8,128)(2,1)} async-done(((bf16[16,8192]{1,0:T(8,128)(2,1)}), bf16[16,8192]{1,0:T(8,128)(2,1)}) %all-reduce.14.cloned.1.call-update) | async-done | bytes 262160 | tf_op jit(solution)/shard_map/while/body/eval_jaxpr/psum | solution.py:148
  951.8 92.3 %all-reduce.16.cloned.1.call-done = bf16[16,8192]{1,0:T(8,128)(2,1)} async-done(((bf16[16,8192]{1,0:T(8,128)(2,1)}), bf16[16,8192]{1,0:T(8,128)(2,1)}) %all-reduce.16.cloned.1.call-update) | async-done | bytes 262160 | tf_op jit(solution)/shard_map/while/body/eval_jaxpr/psum | solution.py:148
  1049.5 92.2 %all-reduce.14.cloned.1.call-done = bf16[16,8192]{1,0:T(8,128)(2,1)} async-done(((bf16[16,8192]{1,0:T(8,128)(2,1)}), bf16[16,8192]{1,0:T(8,128)(2,1)}) %all-reduce.14.cloned.1.call-update) | async-done | bytes 262160 | tf_op jit(solution)/shard_map/while/body/eval_jaxpr/psum | solution.py:148
  1147.0 92.3 %all-reduce.16.cloned.1.call-done = bf16[16,8192]{1,0:T(8,128)(2,1)} async-done(((bf16[16,8192]{1,0:T(8,128)(2,1)}), bf16[16,8192]{1,0:T(8,128)(2,1)}) %all-reduce.16.cloned.1.call-update) | async-done | bytes 262160 | tf_op jit(solution)/shard_map/while/body/eval_jaxpr/psum | solution.py:148
  1244.6 91.9 %all-reduce.14.cloned.1.call-done = bf16[16,8192]{1,0:T(8,128)(2,1)} async-done(((bf16[16,8192]{1,0:T(8,128)(2,1)}), bf16[16,8192]{1,0:T(8,128)(2,1)}) %all-reduce.14.cloned.1.call-update) | async-done | bytes 262160 | tf_op jit(solution)/shard_map/while/body/eval_jaxpr/psum | solution.py:148
  1341.8 92.1 %all-reduce.16.cloned.1.call-done = bf16[16,8192]{1,0:T(8,128)(2,1)} async-done(((bf16[16,8192]{1,0:T(8,128)(2,1)}), bf16[16,8192]{1,0:T(8,128)(2,1)}) %all-reduce.16.cloned.1.call-update) | async-done | bytes 262160 | tf_op jit(solution)/shard_map/while/body/eval_jaxpr/psum | solution.py:148
  1439.2 89.0 %all-reduce.14.cloned.1.call-done = bf16[16,8192]{1,0:T(8,128)(2,1)} async-done(((bf16[16,8192]{1,0:T(8,128)(2,1)}), bf16[16,8192]{1,0:T(8,128)(2,1)}) %all-reduce.14.cloned.1.call-update) | async-done | bytes 262160 | tf_op jit(solution)/shard_map/while/body/eval_jaxpr/psum | solution.py:148
  1533.5 89.1 %all-reduce.16.cloned.1.call-done = bf16[16,8192]{1,0:T(8,128)(2,1)} async-done(((bf16[16,8192]{1,0:T(8,128)(2,1)}), bf16[16,8192]{1,0:T(8,128)(2,1)}) %all-reduce.16.cloned.1.call-update) | async-done | bytes 262160 | tf_op jit(solution)/shard_map/while/body/eval_jaxpr/psum | solution.py:148
  1626.1 66.2 %all-reduce.12.cloned.1.call-done = bf16[8,16,8192]{2,1,0:T(8,128)(2,1)} async-done(((bf16[8,16,8192]{2,1,0:T(8,128)(2,1)}), bf16[8,16,8192]{2,1,0:T(8,128)(2,1)}) %all-reduce.12.cloned.1.call-update) | async-done | bytes 2097168 | tf_op jit(solution)/shard_map/psum | solution.py:22
  (291 shorter events, 116.4 us)
Async XLA Ops:
  6.5 72.2 %all-reduce.10.cloned.1.call-start = ((), (), s32[]{:S(2)}) async-start(), calls=%async_computation | async-start | bytes 4194304 | tf_op jit(solution)/shard_map/psum | solution.py:59
  80.3 91.8 %all-reduce.14.cloned.1.call-start = ((), (), s32[]{:S(2)}) async-start(), calls=%async_computation.2 | async-start | bytes 524288 | tf_op jit(solution)/shard_map/while/body/eval_jaxpr/psum | solution.py:148
  80.4 2.5 collective-permute-start
  86.9 179.6 %all-reduce.16.cloned.1.call-start = ((), (), s32[]{:S(2)}) async-start(), calls=%async_computation.3 | async-start | bytes 524288 | tf_op jit(solution)/shard_map/while/body/eval_jaxpr/psum | solution.py:148
  174.1 2.5 collective-permute-start.1
  268.5 94.2 %all-reduce.14.cloned.1.call-start = ((), (), s32[]{:S(2)}) async-start(), calls=%async_computation.2 | async-start | bytes 524288 | tf_op jit(solution)/shard_map/while/body/eval_jaxpr/psum | solution.py:148
  268.5 2.5 collective-permute-start
  275.0 183.7 %all-reduce.16.cloned.1.call-start = ((), (), s32[]{:S(2)}) async-start(), calls=%async_computation.3 | async-start | bytes 524288 | tf_op jit(solution)/shard_map/while/body/eval_jaxpr/psum | solution.py:148
  364.6 2.5 collective-permute-start.1
  460.6 95.7 %all-reduce.14.cloned.1.call-start = ((), (), s32[]{:S(2)}) async-start(), calls=%async_computation.2 | async-start | bytes 524288 | tf_op jit(solution)/shard_map/while/body/eval_jaxpr/psum | solution.py:148
  460.7 2.5 collective-permute-start
  467.2 186.7 %all-reduce.16.cloned.1.call-start = ((), (), s32[]{:S(2)}) async-start(), calls=%async_computation.3 | async-start | bytes 524288 | tf_op jit(solution)/shard_map/while/body/eval_jaxpr/psum | solution.py:148
  558.2 2.5 collective-permute-start.1
  655.8 95.7 %all-reduce.14.cloned.1.call-start = ((), (), s32[]{:S(2)}) async-start(), calls=%async_computation.2 | async-start | bytes 524288 | tf_op jit(solution)/shard_map/while/body/eval_jaxpr/psum | solution.py:148
  655.8 2.5 collective-permute-start
  662.3 186.7 %all-reduce.16.cloned.1.call-start = ((), (), s32[]{:S(2)}) async-start(), calls=%async_computation.3 | async-start | bytes 524288 | tf_op jit(solution)/shard_map/while/body/eval_jaxpr/psum | solution.py:148
  753.3 2.5 collective-permute-start.1
  850.9 95.7 %all-reduce.14.cloned.1.call-start = ((), (), s32[]{:S(2)}) async-start(), calls=%async_computation.2 | async-start | bytes 524288 | tf_op jit(solution)/shard_map/while/body/eval_jaxpr/psum | solution.py:148
  851.0 2.5 collective-permute-start
  854.3 189.8 %all-reduce.16.cloned.1.call-start = ((), (), s32[]{:S(2)}) async-start(), calls=%async_computation.3 | async-start | bytes 524288 | tf_op jit(solution)/shard_map/while/body/eval_jaxpr/psum | solution.py:148
  948.5 2.5 collective-permute-start.1
  1046.0 95.7 %all-reduce.14.cloned.1.call-start = ((), (), s32[]{:S(2)}) async-start(), calls=%async_computation.2 | async-start | bytes 524288 | tf_op jit(solution)/shard_map/while/body/eval_jaxpr/psum | solution.py:148
  1046.1 2.5 collective-permute-start
  1049.4 189.8 %all-reduce.16.cloned.1.call-start = ((), (), s32[]{:S(2)}) async-start(), calls=%async_computation.3 | async-start | bytes 524288 | tf_op jit(solution)/shard_map/while/body/eval_jaxpr/psum | solution.py:148
  1143.6 2.5 collective-permute-start.1
  1241.2 95.4 %all-reduce.14.cloned.1.call-start = ((), (), s32[]{:S(2)}) async-start(), calls=%async_computation.2 | async-start | bytes 524288 | tf_op jit(solution)/shard_map/while/body/eval_jaxpr/psum | solution.py:148
  1241.2 2.5 collective-permute-start
  1244.6 189.3 %all-reduce.16.cloned.1.call-start = ((), (), s32[]{:S(2)}) async-start(), calls=%async_computation.3 | async-start | bytes 524288 | tf_op jit(solution)/shard_map/while/body/eval_jaxpr/psum | solution.py:148
  1435.7 92.5 %all-reduce.14.cloned.1.call-start = ((), (), s32[]{:S(2)}) async-start(), calls=%async_computation.2 | async-start | bytes 524288 | tf_op jit(solution)/shard_map/while/body/eval_jaxpr/psum | solution.py:148
  1435.8 2.5 collective-permute-start
  1439.1 183.5 %all-reduce.16.cloned.1.call-start = ((), (), s32[]{:S(2)}) async-start(), calls=%async_computation.3 | async-start | bytes 524288 | tf_op jit(solution)/shard_map/while/body/eval_jaxpr/psum | solution.py:148
  1624.5 67.8 %all-reduce.12.cloned.1.call-start = ((), (), s32[]{:S(2)}) async-start(), calls=%async_computation.1 | async-start | bytes 4194304 | tf_op jit(solution)/shard_map/psum | solution.py:22
  (24 other events, 83.5 us)
Sparse Core Ops, SparseCore 0:
  10.7 68.0 all-reduce.9
  87.0 85.1 all-reduce.13
  180.7 85.7 all-reduce.15
  275.2 87.4 all-reduce.13
  371.2 87.4 all-reduce.15
  467.3 88.9 all-reduce.13
  564.8 88.9 all-reduce.15
  662.4 88.9 all-reduce.13
  760.0 88.9 all-reduce.15
  854.6 91.9 all-reduce.13
  951.9 92.1 all-reduce.15
  1049.8 91.9 all-reduce.13
  1147.1 92.1 all-reduce.15
  1244.9 91.6 all-reduce.13
  1341.9 91.8 all-reduce.15
  1439.4 88.7 all-reduce.13
  1533.6 88.9 all-reduce.15
  1627.4 64.8 all-reduce.11
where the time goes:
time: 1710 us; the launch traced here: 1700 us
  waiting for transfers between devices  1570 us (92%)
  other arithmetic  37.9 us (2%)
  local copies, waits for them, and re-layouts  32.9 us (2%)
  matrix products  30.3 us (2%)
  starting transfers between devices  21.6 us (1%)
    psum x16, waiting for transfers between devices, one_tick(): lax.psum(as_sent(partial_value), 'tensor')  1430 us
    psum x1, waiting for transfers between devices, broadcast(): return lax.psum(block, axis)  66.2 us
    psum x1, waiting for transfers between devices, on_device(): embedded = lax.psum(partial_embed.astype(jnp.bfloat16), 'section')  55.6 us
  transfers between devices with their start and end apart: 34, of which 26 were waited for; matrix products, arithmetic and copies ran while one was open for 1% of the time, Pallas kernels for 0%

commit v1 on v0

v1 whole, which is shorter than its diff:
```python
import jax
import jax.numpy as jnp
from jax import lax
from jax.sharding import PartitionSpec as P

SHORT = 7
CORES = 2


def swap_cores(block):
    devices = range(lax.axis_size("section"))
    return lax.ppermute(block, "section", [(i, i ^ 1) for i in devices])


def to_plane(block, source, target):
    route = [(CORES * source + core, CORES * target + core) for core in range(CORES)]
    return lax.ppermute(block, "section", route)


def exchange(blocks):
    return lax.all_to_all(blocks, "tensor", 0, 0)


def gather(block):
    return exchange(jnp.broadcast_to(block, (lax.axis_size("tensor"),) + block.shape))


def on_device(
    token_ids,
    block_types,
    embed_table,
    proj_weights,
    norm_gains,
    conv_filters,
    conv_caches,
    final_gain,
    unembed,
):
    f32, bf16 = jnp.float32, jnp.bfloat16
    planes = lax.axis_size("section") // CORES
    section = lax.axis_index("section")
    plane, core = section // CORES, section % CORES
    groups = lax.axis_size("tensor")
    group = lax.axis_index("tensor")
    steps, requests = token_ids.shape
    own = requests // CORES
    rows = steps * own
    vocab_local, width = embed_table.shape
    part = width // groups
    chan = proj_weights.shape[2]
    taps = conv_filters.shape[1]

    def pair(mine):
        other = swap_cores(mine)
        even = jnp.where(core == 0, mine, other)
        odd = jnp.where(core == 0, other, mine)
        return even, odd

    ids = token_ids.reshape(steps, CORES, own).transpose(1, 0, 2).reshape(CORES, rows)
    vocab_ids = section * vocab_local + jnp.arange(vocab_local, dtype=jnp.int32)
    one_hot = (ids[:, :, None] == vocab_ids).astype(bf16)
    table_part = lax.dynamic_slice_in_dim(embed_table, group * part, part, 1)
    found = jnp.einsum("crv,vd->crd", one_hot, table_part, preferred_element_type=f32).astype(bf16)
    kept = lax.dynamic_index_in_dim(found, core, 0, keepdims=False)
    given = lax.dynamic_index_in_dim(found, 1 - core, 0, keepdims=False)
    on_chip = kept + swap_cores(given)
    chunk = on_chip
    for source in range(1, planes):
        chunk = chunk + to_plane(on_chip, source, 0)

    weight_in, weight_out = pair(proj_weights[0])
    gain_in, gain_out = pair(norm_gains[0])
    weight_in = weight_in.reshape(groups, part, chan)
    weight_out = weight_out.reshape(groups, part, chan)
    gain_in = gain_in.reshape(groups, 1, part)
    gain_out = lax.dynamic_slice_in_dim(gain_out, group * part, part, 0)

    mask = jnp.where(block_types[0] == 1, 1.0, (jnp.arange(taps) < SHORT).astype(f32))
    filt = (conv_filters[0].astype(f32) * mask[:, None]).astype(bf16)
    flipped = filt[::-1]
    history = conv_caches[0]
    length = history.shape[1]
    shifted = jnp.stack(
        [
            jnp.concatenate([jnp.zeros((k, chan), bf16), flipped[: length - k]], 0)
            for k in range(steps)
        ]
    )
    terms = jnp.einsum("krc,brc->kbc", shifted, history, preferred_element_type=f32)
    terms = terms.reshape(steps, CORES, own, chan).transpose(1, 0, 2, 3)
    terms_kept = lax.dynamic_index_in_dim(terms, core, 0, keepdims=False)
    terms_given = lax.dynamic_index_in_dim(terms, 1 - core, 0, keepdims=False)
    terms_other = swap_cores(terms_given)
    base_in = jnp.where(core == 0, terms_kept, terms_other)
    base_out = jnp.where(core == 0, terms_other, terms_kept)
    lags_in, lags_out = pair(filt[:steps].astype(f32))

    def convolve(signal, base, lags):
        signal = signal.astype(f32).reshape(steps, own, chan)
        results = []
        for k in range(steps):
            total = base[k]
            for lag in range(k + 1):
                total = total + lags[lag] * signal[k - lag]
            results.append(total)
        return jnp.stack(results).reshape(rows, chan)

    for layer in range(planes):
        full = gather(chunk).astype(f32)
        mean_square = jnp.sum(full * full, axis=(0, 2), keepdims=True) / width
        normed = (full * lax.rsqrt(mean_square + 1e-06) * gain_in).astype(bf16)
        a = jnp.einsum("trk,tkc->rc", normed, weight_in, preferred_element_type=f32).astype(bf16)
        z = convolve(a, base_in, lags_in).astype(bf16)
        g = (z.astype(f32) * convolve(z, base_out, lags_out)).astype(bf16)
        partial = jnp.einsum("rc,tkc->trk", g, weight_out, preferred_element_type=f32)
        summed = jnp.sum(exchange(partial.astype(bf16)).astype(f32), axis=0)
        chunk = (chunk.astype(f32) + gain_out * summed).astype(bf16)
        if layer < planes - 1:
            chunk = to_plane(chunk, layer, layer + 1)

    last = planes - 1
    shared = jnp.where(plane == last, chunk, jnp.zeros_like(chunk))
    for target in range(last):
        shared = shared + to_plane(chunk, last, target)
    other = swap_cores(shared)
    both = jnp.where(core == 0, jnp.stack([shared, other]), jnp.stack([other, shared]))
    both = both.reshape(CORES * rows, part).astype(f32)
    gain_part = lax.dynamic_slice_in_dim(final_gain, group * part, part, 0)
    head_part = lax.dynamic_slice_in_dim(unembed, group * part, part, 0)
    squares = jnp.sum(both * both, axis=1, keepdims=True)
    scores = jnp.dot((both * gain_part).astype(bf16), head_part, preferred_element_type=f32)
    packed = jnp.concatenate([scores, squares], 1)
    totals = jnp.sum(gather(packed), axis=0)
    cols = unembed.shape[1]
    logits = totals[:, :cols] * lax.rsqrt(totals[:, cols:] / width + 1e-06)
    return logits.reshape(CORES, steps, own, cols).transpose(1, 0, 2, 3).reshape(steps, requests, cols)


def solution(mesh):
    placed = (
        P(),
        P("section"),
        P("section", None),
        P("section", None, "tensor"),
        P("section", None),
        P("section", None, "tensor"),
        P("section", None, None, "tensor"),
        P(),
        P(None, "section"),
    )
    return jax.shard_map(
        on_device, mesh=mesh, in_specs=placed, out_specs=P(None, None, "section"), check_vma=False
    )
```

time: 1710 us -> 238 us (0.14)
  waiting for transfers between devices: 1570 us -> 51.6 us
  blocking collectives: 0 us -> 117 us
  other arithmetic: 37.9 us -> 8.86 us
    psum x18 -> x0, waiting for transfers between devices: 1560 us -> none  [the longest x16 1430 us: one_tick(): lax.psum(as_sent(partial_value), 'tensor')]
    all_to_all x0 -> x7, blocking collectives: none -> 117 us  [exchange(): return lax.all_to_all(blocks, 'tensor', 0, 0)]
    all_to_all x0 -> x2, waiting for transfers between devices: none -> 31 us  [exchange(): return lax.all_to_all(blocks, 'tensor', 0, 0)]
    select_n x34 -> x6, other arithmetic: 32.4 us -> 4.57 us  [the longest x2 3.79 us: pair(): even = jnp.where(core == 0, mine, other)]
  transfers between devices with their start and end apart: 34 -> 17, of which waited for: 26 -> 8; matrix products, arithmetic and copies ran while one was open for 1% -> 9% of each run, Pallas kernels for 0% -> 0%
where the time goes in v1:
time: 238 us; the launch traced here: 237 us
  blocking collectives  117 us (49%)
  waiting for transfers between devices  51.6 us (22%)
  starting transfers between devices  23.4 us (10%)
  local copies, waits for them, and re-layouts  20.5 us (9%)
  matrix products  14.4 us (6%)
  other arithmetic  8.86 us (4%)
    all_to_all x7, blocking collectives, exchange(): return lax.all_to_all(blocks, 'tensor', 0, 0)  117 us
    all_to_all x2, waiting for transfers between devices, exchange(): return lax.all_to_all(blocks, 'tensor', 0, 0)  31 us
    ppermute x9, waiting for transfers between devices, to_plane(): return lax.ppermute(block, 'section', route)  19 us
    all_to_all x2, starting transfers between devices, exchange(): return lax.all_to_all(blocks, 'tensor', 0, 0)  11.8 us
    ppermute x9, starting transfers between devices, to_plane(): return lax.ppermute(block, 'section', route)  10.9 us
    dot_general x4, matrix products, on_device(): jnp.einsum('rc,tkc->trk', g, weight_out, preferred_element_type=f32)  6.57 us
  transfers between devices with their start and end apart: 17, of which 8 were waited for; matrix products, arithmetic and copies ran while one was open for 9% of the time, Pallas kernels for 0%

profile of v1, /device:TPU:0, one launch (start us, length us, event | category | flops | bytes accessed | tf_op | source)
XLA Modules:
  0.0 236.8 jit_solution(12193511925718710807)
XLA Ops:
  5.6 4.4 %copy.74 = bf16[32,127,256]{1,0,2:T(8,128)(2,1)S(1)} copy(bf16[32,127,256]{2,0,1:T(8,128)(2,1)} %bitcast.417) | data formatting | bytes 4161536 | tf_op jit(solution)/shard_map/squeeze | solution.py:81
  10.6 1.5 slice.404
  15.4 3.0 %convolution_bitcast_fusion = f32[4,32,256]{1,0,2:T(4,128)} fusion(bf16[32,127,256]{1,0,2:T(8,128)(2,1)S(1)} %copy.74, bf16[1,127,256]{1,0,2:T(2,128)(2,1)S(1)} %copy.73, bf16[1,127,256]{1,0,2:T(2,128)(2,1)S(1)} %copy.72, bf16[1,127,256]{1,0,2:T(2,128)(2,1)} %copy.71, bf16[1,127,256]{1,0,2:T(2,128)(2,1)} %copy.70), kind=kOutput, calls=%fused_computation.34 | convolution fusion | flops 9363456 | bytes 2471936 | tf_op jit(solution)/shard_map/krc,brc->kbc/dot_general | solution.py:89
  19.2 1.3 collective-permute-start.3
  20.5 1.3 collective-permute-start.2
  21.8 1.3 collective-permute-start.1
  23.1 1.2 copy.75
  24.4 2.2 collective-permute-done.3
  26.6 1.6 collective-permute-done.2
  29.3 8.1 %all-to-all-start = ((bf16[16,64,512]{2,1,0:T(8,128)(2,1)}), bf16[16,64,512]{2,1,0:T(8,128)(2,1)S(1)}, u32[]{:S(2)}, u32[]{:S(2)}) async-start(bf16[16,64,512]{2,1,0:T(8,128)(2,1)} %broadcast_in_dim.19), calls=%async_computation | async-start | bytes 2097152 | tf_op jit(solution)/shard_map/all_to_all | solution.py:21
  37.6 1.1 collective-permute-done.6
  38.8 15.2 %all-to-all-done = bf16[16,64,512]{2,1,0:T(8,128)(2,1)S(1)} async-done(((bf16[16,64,512]{2,1,0:T(8,128)(2,1)}), bf16[16,64,512]{2,1,0:T(8,128)(2,1)S(1)}, u32[]{:S(2)}, u32[]{:S(2)}) %all-to-all-start) | async-done | bytes 1048608 | tf_op jit(solution)/shard_map/all_to_all | solution.py:21
  54.3 3.8 %broadcast_select_fusion = (bf16[8192,256]{1,0:T(8,128)(2,1)S(1)}, bf16[8192,256]{1,0:T(8,128)(2,1)S(1)}) fusion(bf16[8192,256]{1,0:T(8,128)(2,1)} %collective-permute-done.5, pred[]{:T(512)S(6)} %eq.19, bf16[1,8192,256]{2,1,0:T(8,128)(2,1)} %param.12), kind=kLoop, calls=%fused_computation | loop fusion | flops 4194304 | bytes 16777216 | tf_op jit(solution)/shard_map/jit(_where)/select_n | solution.py:55
  58.1 2.0 copy-done.3
  61.3 2.4 %fusion.12 = bf16[16,64,512]{2,1,0:T(8,128)(2,1)} fusion(bf16[16,512,256]{2,1,0:T(8,128)(2,1)S(1)} %bitcast.408, bf16[64,256,1]{1,0,2:T(8,128)(2,1)S(1)} %bitcast.426), kind=kOutput, calls=%fused_computation.30 | convolution fusion | flops 268959744 | bytes 5275648 | tf_op jit(solution)/shard_map/rc,tkc->trk/dot_general | solution.py:115
  63.7 3.7 %all-to-all-start.1 = ((bf16[16,64,512]{2,1,0:T(8,128)(2,1)}), bf16[16,64,512]{2,1,0:T(8,128)(2,1)S(1)}, u32[]{:S(2)}, u32[]{:S(2)}) async-start(bf16[16,64,512]{2,1,0:T(8,128)(2,1)} %fusion.12), calls=%async_computation.1 | async-start | bytes 2097152 | tf_op jit(solution)/shard_map/all_to_all | solution.py:21
  68.2 15.8 %all-to-all-done.1 = bf16[16,64,512]{2,1,0:T(8,128)(2,1)S(1)} async-done(((bf16[16,64,512]{2,1,0:T(8,128)(2,1)}), bf16[16,64,512]{2,1,0:T(8,128)(2,1)S(1)}, u32[]{:S(2)}, u32[]{:S(2)}) %all-to-all-start.1) | async-done | bytes 1048608 | tf_op jit(solution)/shard_map/all_to_all | solution.py:21
  84.1 3.1 %collective-permute-start.8 = (bf16[64,512]{1,0:T(8,128)(2,1)S(1)}, bf16[64,512]{1,0:T(8,128)(2,1)S(1)}, u32[]{:S(2)}, u32[]{:S(2)}) collective-permute-start(bf16[64,512]{1,0:T(8,128)(2,1)S(1)} %add_convert_fusion.3), channel_id=1, source_target_pairs={{0,32},{16,48},{1,33},{17,49},{2,34},{18,50},{3,35},{19,51},{4,36}... | collective-permute-start | bytes 196616 | tf_op jit(solution)/shard_map/ppermute | solution.py:17
  87.3 1.9 collective-permute-done.8
  89.2 18.9 %all_to_all.45 = bf16[16,64,512]{2,1,0:T(8,128)(2,1)S(1)} all-to-all(bf16[16,64,512]{2,1,0:T(8,128)(2,1)S(1)} %broadcast_in_dim.20), channel_id=1, replica_groups=mesh['section'=8,'tensor'=16] {'tensor'}, dimensions={0} | all-to-all | bytes 2097152 | tf_op jit(solution)/shard_map/all_to_all | solution.py:21
  109.5 1.2 copy-done.2
  110.6 1.4 fusion.13
  112.0 17.9 %all_to_all.46 = bf16[16,64,512]{2,1,0:T(8,128)(2,1)S(1)} all-to-all(bf16[16,64,512]{2,1,0:T(8,128)(2,1)S(1)} %fusion.13), channel_id=1, replica_groups=mesh['section'=8,'tensor'=16] {'tensor'}, dimensions={0} | all-to-all | bytes 2097152 | tf_op jit(solution)/shard_map/all_to_all | solution.py:21
  130.9 16.8 %all_to_all.47 = bf16[16,64,512]{2,1,0:T(8,128)(2,1)S(1)} all-to-all(bf16[16,64,512]{2,1,0:T(8,128)(2,1)S(1)} %broadcast_in_dim.21), channel_id=1, replica_groups=mesh['section'=8,'tensor'=16] {'tensor'}, dimensions={0} | all-to-all | bytes 2097152 | tf_op jit(solution)/shard_map/all_to_all | solution.py:21
  148.9 1.4 fusion.14
  150.3 16.0 %all_to_all.48 = bf16[16,64,512]{2,1,0:T(8,128)(2,1)S(1)} all-to-all(bf16[16,64,512]{2,1,0:T(8,128)(2,1)S(1)} %fusion.14), channel_id=1, replica_groups=mesh['section'=8,'tensor'=16] {'tensor'}, dimensions={0} | all-to-all | bytes 2097152 | tf_op jit(solution)/shard_map/all_to_all | solution.py:21
  167.2 15.9 %all_to_all.49 = bf16[16,64,512]{2,1,0:T(8,128)(2,1)S(1)} all-to-all(bf16[16,64,512]{2,1,0:T(8,128)(2,1)S(1)} %broadcast_in_dim.22), channel_id=1, replica_groups=mesh['section'=8,'tensor'=16] {'tensor'}, dimensions={0} | all-to-all | bytes 2097152 | tf_op jit(solution)/shard_map/all_to_all | solution.py:21
  184.4 1.4 fusion.15
  185.8 15.9 %all_to_all.50 = bf16[16,64,512]{2,1,0:T(8,128)(2,1)S(1)} all-to-all(bf16[16,64,512]{2,1,0:T(8,128)(2,1)S(1)} %fusion.15), channel_id=1, replica_groups=mesh['section'=8,'tensor'=16] {'tensor'}, dimensions={0} | all-to-all | bytes 2097152 | tf_op jit(solution)/shard_map/all_to_all | solution.py:21
  203.2 1.3 collective-permute-start.11
  204.6 13.2 %collective-permute-done.11 = bf16[64,512]{1,0:T(8,128)(2,1)S(1)} collective-permute-done((bf16[64,512]{1,0:T(8,128)(2,1)S(1)}, bf16[64,512]{1,0:T(8,128)(2,1)S(1)}, u32[]{:S(2)}, u32[]{:S(2)}) %collective-permute-start.11) | collective-permute-done | bytes 65568 | tf_op jit(solution)/shard_map/ppermute | solution.py:17
  220.5 15.5 %all_to_all.51 = f32[16,128,65]{1,2,0:T(8,128)S(1)} all-to-all(f32[16,128,65]{1,2,0:T(8,128)S(1)} %broadcast_in_dim.46), channel_id=1, replica_groups=mesh['section'=8,'tensor'=16] {'tensor'}, dimensions={0} | all-to-all | bytes 1064960 | tf_op jit(solution)/shard_map/all_to_all | solution.py:21
  (118 shorter events, 24.1 us)
Async XLA Ops:
  0.0 1.2 copy-start
  0.0 54.3 %collective-permute-start.5 = (bf16[8192,256]{1,0:T(8,128)(2,1)}, bf16[8192,256]{1,0:T(8,128)(2,1)}, u32[]{:S(2)}, u32[]{:S(2)}) collective-permute-start(bf16[8192,256]{1,0:T(8,128)(2,1)} %bitcast.416), channel_id=1, source_target_pairs={{0,16},{16,0},{32,48},{48,32},{64,80},{80,64},{96,112},{112,96},{1... | collective-permute-start | bytes 12582920 | tf_op jit(solution)/shard_map/ppermute | solution.py:12
  1.5 4.1 %copy-start.5 = (bf16[2,64,512]{2,1,0:T(8,128)(2,1)}, bf16[2,64,512]{2,1,0:T(8,128)(2,1)S(1)}, u32[]{:S(2)}) copy-start(bf16[2,64,512]{2,1,0:T(8,128)(2,1)S(1)} %convolution_convert_fusion.4) | copy-start | bytes 393220
  2.1 16.2 %collective-permute-start = (bf16[64,512]{1,0:T(8,128)(2,1)}, bf16[64,512]{1,0:T(8,128)(2,1)}, u32[]{:S(2)}, u32[]{:S(2)}) collective-permute-start(bf16[64,512]{1,0:T(8,128)(2,1)} %dynamic-slice_bitcast_fusion.1), channel_id=1, source_target_pairs={{0,16},{16,0},{32,48},{48,32},{64,80},{80,64},{96,112},{112,96},{1... | collective-permute-start | bytes 196616 | tf_op jit(solution)/shard_map/ppermute | solution.py:12
  2.3 35.3 %collective-permute-start.4 = (f32[8192]{0:T(1024)}, f32[8192]{0:T(1024)}, u32[]{:S(2)}, u32[]{:S(2)}) collective-permute-start(f32[8192]{0:T(1024)} %bitcast.430), channel_id=1, source_target_pairs={{0,16},{16,0},{32,48},{48,32},{64,80},{80,64},{96,112},{112,96},{1... | collective-permute-start | bytes 98312 | tf_op jit(solution)/shard_map/ppermute | solution.py:12
  19.2 7.4 %collective-permute-start.3 = (bf16[64,512]{1,0:T(8,128)(2,1)S(1)}, bf16[64,512]{1,0:T(8,128)(2,1)S(1)}, u32[]{:S(2)}, u32[]{:S(2)}) collective-permute-start(bf16[64,512]{1,0:T(8,128)(2,1)S(1)} %bitcast_add_fusion), channel_id=1, source_target_pairs={{96,0},{112,16},{97,1},{113,17},{98,2},{114,18},{99,3},{115,19},{1... | collective-permute-start | bytes 196616 | tf_op jit(solution)/shard_map/ppermute | solution.py:17
  20.5 7.7 %collective-permute-start.2 = (bf16[64,512]{1,0:T(8,128)(2,1)S(1)}, bf16[64,512]{1,0:T(8,128)(2,1)S(1)}, u32[]{:S(2)}, u32[]{:S(2)}) collective-permute-start(bf16[64,512]{1,0:T(8,128)(2,1)S(1)} %bitcast_add_fusion), channel_id=1, source_target_pairs={{64,0},{80,16},{65,1},{81,17},{66,2},{82,18},{67,3},{83,19},{68,4}... | collective-permute-start | bytes 196616 | tf_op jit(solution)/shard_map/ppermute | solution.py:17
  21.8 6.4 %collective-permute-start.1 = (bf16[64,512]{1,0:T(8,128)(2,1)S(1)}, bf16[64,512]{1,0:T(8,128)(2,1)S(1)}, u32[]{:S(2)}, u32[]{:S(2)}) collective-permute-start(bf16[64,512]{1,0:T(8,128)(2,1)S(1)} %bitcast_add_fusion), channel_id=1, source_target_pairs={{32,0},{48,16},{33,1},{49,17},{34,2},{50,18},{35,3},{51,19},{36,4}... | collective-permute-start | bytes 196616 | tf_op jit(solution)/shard_map/ppermute | solution.py:17
  23.1 14.5 %copy-start.6 = (f32[1,8192]{1,0:T(1,128)S(1)}, f32[1,8192]{1,0:T(1,128)}, u32[]{:S(2)}) copy-start(f32[1,8192]{1,0:T(1,128)} %param.13) | copy-start | bytes 98308
  26.6 10.9 %collective-permute-start.7 = (f32[4,256]{1,0:T(4,128)S(1)}, f32[4,256]{1,0:T(4,128)S(1)}, u32[]{:S(2)}, u32[]{:S(2)}) collective-permute-start(f32[4,256]{1,0:T(4,128)S(1)} %slice_convert_fusion), channel_id=1, source_target_pairs={{0,16},{16,0},{32,48},{48,32},{64,80},{80,64},{96,112},{112,96},{1... | collective-permute-start | bytes 12296 | tf_op jit(solution)/shard_map/ppermute | solution.py:12
  29.3 24.7 %all-to-all-start = ((bf16[16,64,512]{2,1,0:T(8,128)(2,1)}), bf16[16,64,512]{2,1,0:T(8,128)(2,1)S(1)}, u32[]{:S(2)}, u32[]{:S(2)}) async-start(bf16[16,64,512]{2,1,0:T(8,128)(2,1)} %broadcast_in_dim.19), calls=%async_computation | async-start | bytes 2097152 | tf_op jit(solution)/shard_map/all_to_all | solution.py:21
  37.4 1.3 collective-permute-start.6
  58.1 2.0 copy-start.3
  58.1 3.2 %copy-start.1 = (bf16[8192,256]{1,0:T(8,128)(2,1)}, bf16[8192,256]{1,0:T(8,128)(2,1)S(1)}, u32[]{:S(2)}) copy-start(bf16[8192,256]{1,0:T(8,128)(2,1)S(1)} %get-tuple-element.6) | copy-start | bytes 12582916
  63.7 20.2 %all-to-all-start.1 = ((bf16[16,64,512]{2,1,0:T(8,128)(2,1)}), bf16[16,64,512]{2,1,0:T(8,128)(2,1)S(1)}, u32[]{:S(2)}, u32[]{:S(2)}) async-start(bf16[16,64,512]{2,1,0:T(8,128)(2,1)} %fusion.12), calls=%async_computation.1 | async-start | bytes 2097152 | tf_op jit(solution)/shard_map/all_to_all | solution.py:21
  84.1 24.3 %copy-start.4 = (bf16[8192,256]{1,0:T(8,128)(2,1)S(1)}, bf16[8192,256]{1,0:T(8,128)(2,1)}, u32[]{:S(2)}) copy-start(bf16[8192,256]{1,0:T(8,128)(2,1)} %copy-done.3) | copy-start | bytes 12582916
  84.1 5.0 %collective-permute-start.8 = (bf16[64,512]{1,0:T(8,128)(2,1)S(1)}, bf16[64,512]{1,0:T(8,128)(2,1)S(1)}, u32[]{:S(2)}, u32[]{:S(2)}) collective-permute-start(bf16[64,512]{1,0:T(8,128)(2,1)S(1)} %add_convert_fusion.3), channel_id=1, source_target_pairs={{0,32},{16,48},{1,33},{17,49},{2,34},{18,50},{3,35},{19,51},{4,36}... | collective-permute-start | bytes 196616 | tf_op jit(solution)/shard_map/ppermute | solution.py:17
  108.5 2.2 copy-start.2
  130.1 0.7 collective-permute-start.9
  166.5 0.7 collective-permute-start.10
  201.9 2.7 %collective-permute-start.13 = (bf16[64,512]{1,0:T(8,128)(2,1)S(1)}, bf16[64,512]{1,0:T(8,128)(2,1)S(1)}, u32[]{:S(2)}, u32[]{:S(2)}) collective-permute-start(bf16[64,512]{1,0:T(8,128)(2,1)S(1)} %add_convert_fusion), channel_id=1, source_target_pairs={{96,64},{112,80},{97,65},{113,81},{98,66},{114,82},{99,67},{115,83... | collective-permute-start | bytes 196616 | tf_op jit(solution)/shard_map/ppermute | solution.py:17
  202.5 2.0 collective-permute-start.12
  203.2 14.6 %collective-permute-start.11 = (bf16[64,512]{1,0:T(8,128)(2,1)S(1)}, bf16[64,512]{1,0:T(8,128)(2,1)S(1)}, u32[]{:S(2)}, u32[]{:S(2)}) collective-permute-start(bf16[64,512]{1,0:T(8,128)(2,1)S(1)} %add_convert_fusion), channel_id=1, source_target_pairs={{96,0},{112,16},{97,1},{113,17},{98,2},{114,18},{99,3},{115,19},{1... | collective-permute-start | bytes 196616 | tf_op jit(solution)/shard_map/ppermute | solution.py:17
  217.8 1.3 collective-permute-start.14

commit v2 on v1

v2 whole, which is shorter than its diff:
```python
import jax
import jax.numpy as jnp
from jax import lax
from jax.experimental import pallas as pl
from jax.experimental.pallas import tpu as pltpu
from jax.sharding import PartitionSpec as P

SHORT = 7
CORES = 2
RECUT = 2
LEAD = 8
EXTRA = 8


def swap_cores(block):
    devices = range(lax.axis_size("section"))
    return lax.ppermute(block, "section", [(i, i ^ 1) for i in devices])


def to_plane(block, source, target):
    route = [(CORES * source + core, CORES * target + core) for core in range(CORES)]
    return lax.ppermute(block, "section", route)


def exchange(blocks):
    return lax.all_to_all(blocks, "tensor", 0, 0)


def copies(block):
    return jnp.broadcast_to(block, (lax.axis_size("tensor"),) + block.shape)


def unset(like):
    return pl.pallas_call(
        lambda out: None,
        out_shape=jax.ShapeDtypeStruct(like.shape, like.dtype),
        out_specs=pl.BlockSpec(memory_space=pl.ANY),
    )()


def terms_kernel(filt_ref, history_ref, out_ref, shifted):
    steps = out_ref.shape[0]
    length = history_ref.shape[1]
    for k in range(steps):
        shifted[k] = filt_ref[LEAD - k : LEAD - k + length, :]

    def one_request(b, carry):
        rows = history_ref[b].astype(jnp.float32)
        for k in range(steps):
            out_ref[k, pl.ds(b, 1), :] = jnp.sum(shifted[k] * rows, axis=0, keepdims=True)
        return carry

    lax.fori_loop(0, history_ref.shape[0], one_request, 0)


def cache_terms(filt, history, steps):
    requests, length, chan = history.shape
    padded = jnp.pad(filt[::-1].astype(jnp.float32), ((LEAD, 0), (0, 0)))
    return pl.pallas_call(
        terms_kernel,
        out_shape=jax.ShapeDtypeStruct((steps, requests, chan), jnp.float32),
        in_specs=[pl.BlockSpec(memory_space=pltpu.VMEM)] * 2,
        out_specs=pl.BlockSpec(memory_space=pltpu.VMEM),
        scratch_shapes=[pltpu.VMEM((steps, length, chan), jnp.float32)],
        compiler_params=pltpu.CompilerParams(vmem_limit_bytes=24 << 20),
        cost_estimate=pl.CostEstimate(
            flops=2 * steps * requests * length * chan,
            bytes_accessed=2 * requests * length * chan,
            transcendentals=0,
        ),
    )(padded, history)


def as_row_pair(column, width):
    row = jnp.pad(column.reshape(1, -1), ((0, 0), (0, width - column.shape[0])))
    high = row.astype(jnp.bfloat16)
    low = (row - high.astype(jnp.float32)).astype(jnp.bfloat16)
    return jnp.pad(jnp.concatenate([high, low], 0), ((0, EXTRA - 2), (0, 0)))


def on_device(
    token_ids,
    block_types,
    embed_table,
    proj_weights,
    norm_gains,
    conv_filters,
    conv_caches,
    final_gain,
    unembed,
):
    f32, bf16 = jnp.float32, jnp.bfloat16
    planes = lax.axis_size("section") // CORES
    section = lax.axis_index("section")
    plane, core = section // CORES, section % CORES
    groups = lax.axis_size("tensor")
    group = lax.axis_index("tensor")
    steps, requests = token_ids.shape
    own = requests // CORES
    rows = steps * own
    vocab_local, width = embed_table.shape
    part = width // groups
    chan = proj_weights.shape[2]
    taps = conv_filters.shape[1]
    cols = unembed.shape[1]

    ids = token_ids.reshape(steps, CORES, own).transpose(1, 0, 2).reshape(CORES, rows)
    vocab_ids = section * vocab_local + jnp.arange(vocab_local, dtype=jnp.int32)
    table_part = lax.dynamic_slice_in_dim(embed_table, group * part, part, 1)

    def find(half):
        half_ids = lax.dynamic_index_in_dim(ids, half, 0, keepdims=False)
        one_hot = (half_ids[:, None] == vocab_ids).astype(bf16)
        return jnp.dot(one_hot, table_part, preferred_element_type=f32).astype(bf16)

    on_chip = find(core) + swap_cores(find(1 - core))
    on_chip, mine, small = lax.optimization_barrier(
        (on_chip, proj_weights[0], (norm_gains[0], unembed))
    )
    my_gain, unembed = small

    def pair(mine):
        other = swap_cores(mine)
        even = jnp.where(core == 0, mine, other)
        odd = jnp.where(core == 0, other, mine)
        return even, odd

    chunk = on_chip
    for source in range(1, planes):
        chunk = chunk + to_plane(on_chip, source, 0)
    blocks, filters, history = lax.optimization_barrier(
        (copies(chunk), conv_filters[0], conv_caches[0])
    )
    gathered = exchange(blocks)

    mask = jnp.where(block_types[0] == 1, 1.0, (jnp.arange(taps) < SHORT).astype(f32))
    filt = filters.astype(f32) * mask[:, None]
    terms = cache_terms(filt, history, steps).reshape(steps, CORES, own, chan)
    terms_kept = lax.dynamic_index_in_dim(terms, core, 1, keepdims=False)
    terms_given = lax.dynamic_index_in_dim(terms, 1 - core, 1, keepdims=False)
    terms_other = swap_cores(terms_given)
    base_in = jnp.where(core == 0, terms_kept, terms_other)
    base_out = jnp.where(core == 0, terms_other, terms_kept)
    lags_in, lags_out = pair(filt[:steps])
    weight_in, weight_out = pair(mine.reshape(groups, part, chan))
    gain_in, gain_out = pair(my_gain)
    gain_in_all = gain_in.reshape(groups, 1, part)
    gain_in = lax.dynamic_slice_in_dim(gain_in, group * part, part, 0)
    gain_out = lax.dynamic_slice_in_dim(gain_out, group * part, part, 0)
    head = pair(lax.dynamic_slice_in_dim(unembed, group * part, part, 0))
    head = jnp.concatenate(head, 1)
    head_gain = lax.dynamic_slice_in_dim(final_gain, group * part, part, 0)

    def convolve(signal, base, lags):
        signal = signal.astype(f32).reshape(steps, own, chan)
        results = []
        for k in range(steps):
            total = base[k]
            for lag in range(k + 1):
                total = total + lags[lag] * signal[k - lag]
            results.append(total)
        return jnp.stack(results).reshape(rows, chan)

    def gate(a):
        z = convolve(a.astype(bf16), base_in, lags_in).astype(bf16)
        return (z.astype(f32) * convolve(z, base_out, lags_out)).astype(bf16)

    def native(chunk, gathered):
        full = gathered.astype(f32)
        mean_square = jnp.sum(full * full, axis=(0, 2), keepdims=True) / width
        normed = (full * lax.rsqrt(mean_square + 1e-06) * gain_in_all).astype(bf16)
        g = gate(jnp.einsum("trk,tkc->rc", normed, weight_in, preferred_element_type=f32))
        partial = jnp.einsum("rc,tkc->trk", g, weight_out, preferred_element_type=f32)
        summed = jnp.sum(exchange(partial.astype(bf16)).astype(f32), axis=0)
        return (chunk.astype(f32) + gain_out * summed).astype(bf16)

    def recut(chunk, cut_in, cut_out):
        values = chunk.astype(f32)
        squares = jnp.sum(values * values, axis=1, keepdims=True)
        scaled = (values * gain_in).astype(bf16)
        partial = jnp.einsum("rk,tkc->trc", scaled, cut_in, preferred_element_type=f32)
        packed = jnp.concatenate([partial.astype(bf16), copies(as_row_pair(squares, chan))], 1)
        totals = jnp.sum(exchange(packed).astype(f32), axis=0)
        square = (totals[rows] + totals[rows + 1])[:rows, None]
        g = gate(totals[:rows] * lax.rsqrt(square / width + 1e-06))
        whole = exchange(copies(g))
        summed = jnp.einsum("trc,tkc->rk", whole, cut_out, preferred_element_type=f32)
        return (values + gain_out * summed).astype(bf16)

    def cut(mine):
        return pair(exchange(mine))

    cut_in, cut_out = lax.cond(
        plane >= RECUT,
        cut,
        lambda mine: (unset(mine), unset(mine)),
        mine.reshape(groups, part, chan),
    )
    chunk = lax.cond(plane == 0, native, lambda chunk, gathered: chunk, chunk, gathered)
    for layer in range(1, planes):
        chunk = to_plane(chunk, layer - 1, layer)
        if layer < RECUT:
            chunk = lax.cond(
                plane == layer, lambda c: native(c, exchange(copies(c))), lambda c: c, chunk
            )
            if layer == RECUT - 1:
                chunk, cut_in, cut_out = lax.optimization_barrier((chunk, cut_in, cut_out))
        else:
            chunk = lax.cond(
                plane == layer, recut, lambda c, cut_in, cut_out: c, chunk, cut_in, cut_out
            )

    last = planes - 1
    shared = jnp.where(plane == last, chunk, jnp.zeros_like(chunk))
    for target in range(last):
        shared = shared + to_plane(chunk, last, target)
    shared = shared.astype(f32)
    squares = jnp.sum(shared * shared, axis=1, keepdims=True)
    scores = jnp.dot((shared * head_gain).astype(bf16), head, preferred_element_type=f32)
    packed = jnp.concatenate([scores.astype(bf16), as_row_pair(squares, CORES * cols)], 0)
    totals = jnp.sum(exchange(copies(packed)).astype(f32), axis=0)
    square = (totals[rows] + totals[rows + 1])[:rows, None]
    logits = totals[:rows] * lax.rsqrt(square / width + 1e-06)
    kept = jnp.where(core == 0, logits[:, :cols], logits[:, cols:])
    other = swap_cores(jnp.where(core == 0, logits[:, cols:], logits[:, :cols]))
    both = jnp.where(core == 0, jnp.stack([kept, other]), jnp.stack([other, kept]))
    return both.reshape(CORES, steps, own, cols).transpose(1, 0, 2, 3).reshape(steps, requests, cols)


def solution(mesh):
    placed = (
        P(),
        P("section"),
        P("section", None),
        P("section", None, "tensor"),
        P("section", None),
        P("section", None, "tensor"),
        P("section", None, None, "tensor"),
        P(),
        P(None, "section"),
    )
    return jax.shard_map(
        on_device, mesh=mesh, in_specs=placed, out_specs=P(None, None, "section"), check_vma=False
    )
```

time: 238 us -> 223 us (0.937)
  waiting for transfers between devices: 51.6 us -> 146 us
  blocking collectives: 117 us -> 31.9 us
  local copies, waits for them, and re-layouts: 20.5 us -> 7.58 us
  matrix products: 14.4 us -> 5.19 us
  starting transfers between devices: 23.4 us -> 18.7 us
    ppermute x9, waiting for transfers between devices: 19 us -> 131 us  [to_plane(): return lax.ppermute(block, 'section', route)]
    all_to_all x7 -> x2, blocking collectives: 117 us -> 31.9 us  [exchange(): return lax.all_to_all(blocks, 'tensor', 0, 0)]
    all_to_all x2 -> x1, waiting for transfers between devices: 31 us -> 12 us  [exchange(): return lax.all_to_all(blocks, 'tensor', 0, 0)]
    dot_general x11 -> x5, matrix products: 14.4 us -> 5.19 us  [the longest x1 3.24 us: native(): jnp.einsum('trk,tkc->rc', normed, weight_in, preferred_element_type=f32)]
    select_n x2 -> x3, other arithmetic: 0.77 us -> 5.86 us  [pair(): odd = jnp.where(core == 0, other, mine)]
    squeeze x3 -> x1, local copies, waits for them, and re-layouts: 5.07 us -> 0.01 us  [on_device(): terms_given = lax.dynamic_index_in_dim(terms, 1 - core, 1, keepdims=False)]
    slice x8 -> x1, local copies, waits for them, and re-layouts: 3.92 us -> 0.01 us  [on_device(): lags_in, lags_out = pair(filt[:steps])]
    all_to_all x2 -> x1, starting transfers between devices: 11.8 us -> 8.13 us  [exchange(): return lax.all_to_all(blocks, 'tensor', 0, 0)]
  transfers between devices with their start and end apart: 17 -> 17, of which waited for: 8 -> 8; matrix products, arithmetic and copies ran while one was open for 9% -> 6% of each run, Pallas kernels for 0% -> 1%
where the time goes in v2:
time: 223 us; the launch traced here: 221 us
  waiting for transfers between devices  146 us (65%)
  blocking collectives  31.9 us (14%)
  starting transfers between devices  18.7 us (8%)
  other arithmetic  8.63 us (4%)
  local copies, waits for them, and re-layouts  7.58 us (3%)
  matrix products  5.19 us (2%)
    ppermute x9, waiting for transfers between devices, to_plane(): return lax.ppermute(block, 'section', route)  131 us
    all_to_all x2, blocking collectives, exchange(): return lax.all_to_all(blocks, 'tensor', 0, 0)  31.9 us
    all_to_all x1, waiting for transfers between devices, exchange(): return lax.all_to_all(blocks, 'tensor', 0, 0)  12 us
    ppermute x9, starting transfers between devices, to_plane(): return lax.ppermute(block, 'section', route)  9.09 us
    all_to_all x1, starting transfers between devices, exchange(): return lax.all_to_all(blocks, 'tensor', 0, 0)  8.13 us
    select_n x3, other arithmetic, pair(): odd = jnp.where(core == 0, other, mine)  5.86 us
  transfers between devices with their start and end apart: 17, of which 8 were waited for; matrix products, arithmetic and copies ran while one was open for 6% of the time, Pallas kernels for 1%

profile of v2, /device:TPU:0, one launch (start us, length us, event | category | flops | bytes accessed | tf_op | source)
XLA Modules:
  0.0 220.6 jit_solution(6406936385079355647)
XLA Ops:
  0.0 0.9 reshape.212
  1.5 1.2 collective-permute-done.1
  4.3 2.8 %copy.20 = bf16[1,32,127,256]{3,2,1,0:T(8,128)(2,1)S(1)} copy(bf16[1,32,127,256]{3,1,2,0:T(8,128)(2,1)} %param.25) | data formatting | bytes 4161536 | tf_op args[6]
  7.1 1.3 collective-permute-start.2
  8.4 1.3 collective-permute-start.3
  9.7 1.3 collective-permute-start.4
  11.1 2.1 collective-permute-done.2
  13.2 2.9 %collective-permute-done.3 = bf16[64,512]{1,0:T(8,128)(2,1)S(1)} collective-permute-done((bf16[64,512]{1,0:T(8,128)(2,1)S(1)}, bf16[64,512]{1,0:T(8,128)(2,1)S(1)}, u32[]{:S(2)}, u32[]{:S(2)}) %collective-permute-start.3) | collective-permute-done | bytes 65568 | tf_op jit(solution)/shard_map/ppermute | solution.py:22
  16.1 1.5 collective-permute-done.4
  17.6 0.9 add_add_fusion.1
  18.4 1.1 broadcast_in_dim.35
  19.8 2.0 shard_map.91
  22.4 8.1 %all-to-all-start.8 = ((bf16[16,64,512]{2,1,0:T(8,128)(2,1)}), bf16[16,64,512]{2,1,0:T(8,128)(2,1)S(1)}, u32[]{:S(2)}, u32[]{:S(2)}) async-start(bf16[16,64,512]{2,1,0:T(8,128)(2,1)} %broadcast_in_dim.35), calls=%async_computation.8 | async-start | bytes 2097152 | tf_op jit(solution)/shard_map/all_to_all | solution.py:26
  30.6 5.8 %broadcast_select_fusion.2 = (bf16[16,512,256]{2,1,0:T(8,128)(2,1)}, bf16[16,512,256]{2,1,0:T(8,128)(2,1)}) fusion(bf16[16,512,256]{2,1,0:T(8,128)(2,1)} %collective-permute-done.8, bf16[16,512,256]{2,1,0:T(8,128)(2,1)} %bitcast.541, pred[]{:T(512)S(6)} %eq.35), kind=kLoop, calls=%fused_computation.248 | loop fusion | flops 4194304 | bytes 16777216 | tf_op jit(solution)/shard_map/jit(_where)/select_n | solution.py:125
  36.4 12.0 %all-to-all-done.8 = bf16[16,64,512]{2,1,0:T(8,128)(2,1)S(1)} async-done(((bf16[16,64,512]{2,1,0:T(8,128)(2,1)}), bf16[16,64,512]{2,1,0:T(8,128)(2,1)S(1)}, u32[]{:S(2)}, u32[]{:S(2)}) %all-to-all-start.8) | async-done | bytes 1048608 | tf_op jit(solution)/shard_map/all_to_all | solution.py:26
  48.4 25.3 %conditional.5 = (bf16[64,512]{1,0:T(8,128)(2,1)S(1)}) conditional(s32[]{:T(128)} %convert_element_type.241, bf16[64,512]{1,0:T(8,128)(2,1)S(1)} %add_add_fusion.1, (bf16[64,512]{1,0:T(8,128)(2,1)S(1)}, f32[512]{0:T(512)S(1)}, f32[4,16,256]{2,1,0:T(8,128)S(1)}, f32[4,256]{1,0:T(4,128)S(1)}, bf16[16,64,512]{2,1,0:T(8,128)(2,1)S(1)}, ...), branch_computations={%region_0.1_spmd, %region_1.4_spmd} | conditional | flops 542638144 | bytes 32599076 | solution.py:199
  48.7 3.2 %fusion.5 = f32[64,256]{1,0:T(8,128)S(1)} fusion(bf16[16,512,256]{2,1,0:T(8,128)(2,1)} %get-tuple-element.105, bf16[16,64,512]{2,1,0:T(8,128)(2,1)S(1)} %get-tuple-element.103, f32[16,512]{1,0:T(8,128)S(1)} %bitcast.543, f32[64]{0:T(128)S(1)} %add_rsqrt_fusion), kind=kOutput, calls=%fused_computation.10 | convolution fusion | flops 270565376 | bytes 5341440 | tf_op jit(solution)/shard_map/cond/branch_1_fun/trk,tkc->rc/dot_general | solution.py:172
  52.0 1.4 fusion.3
  53.4 20.1 %all_to_all.42 = bf16[16,64,512]{2,1,0:T(8,128)(2,1)S(1)} all-to-all(bf16[16,64,512]{2,1,0:T(8,128)(2,1)S(1)} %fusion.3), channel_id=1, replica_groups=mesh['section'=8,'tensor'=16] {'tensor'}, dimensions={0} | all-to-all | bytes 2097152 | tf_op jit(solution)/shard_map/cond/branch_1_fun/all_to_all | solution.py:26
  73.7 1.3 collective-permute-start.9
  75.0 1.8 collective-permute-done.9
  76.9 0.7 collective-permute-start.10
  77.6 0.7 collective-permute-start.11
  78.3 0.9 constant_dynamic-slice_fusion
  79.2 0.8 dynamic_slice.36
  79.9 1.3 collective-permute-start.12
  81.2 0.7 collective-permute-start.13
  81.9 0.7 collective-permute-start.14
  82.6 0.9 broadcast_select_fusion.5
  83.4 122.8 %collective-permute-done.12 = bf16[64,512]{1,0:T(8,128)(2,1)S(1)} collective-permute-done((bf16[64,512]{1,0:T(8,128)(2,1)S(1)}, bf16[64,512]{1,0:T(8,128)(2,1)S(1)}, u32[]{:S(2)}, u32[]{:S(2)}) %collective-permute-start.12) | collective-permute-done | bytes 65568 | tf_op jit(solution)/shard_map/ppermute | solution.py:22
  206.7 11.8 %all_to_all.47 = bf16[16,72,128]{2,1,0:T(8,128)(2,1)S(1)} all-to-all(bf16[16,72,128]{2,1,0:T(8,128)(2,1)S(1)} %broadcast_in_dim.44), channel_id=1, replica_groups=mesh['section'=8,'tensor'=16] {'tensor'}, dimensions={0} | all-to-all | bytes 589824 | tf_op jit(solution)/shard_map/all_to_all | solution.py:26
  218.8 1.2 collective-permute-done.16
  (71 shorter events, 4.5 us)
Async XLA Ops:
  0.0 1.2 copy-start
  0.0 11.0 %copy-start.4 = (f32[1,8192]{1,0:T(1,128)S(1)}, f32[1,8192]{1,0:T(1,128)}, u32[]{:S(2)}) copy-start(f32[1,8192]{1,0:T(1,128)} %param.23) | copy-start | bytes 98308
  0.0 19.5 %copy-start.3 = (bf16[1,128,256]{2,1,0:T(8,128)(2,1)S(1)}, bf16[1,128,256]{2,1,0:T(8,128)(2,1)}, u32[]{:S(2)}) copy-start(bf16[1,128,256]{2,1,0:T(8,128)(2,1)} %param.24) | copy-start | bytes 196612
  1.4 1.3 collective-permute-start.1
  3.0 27.7 %collective-permute-start.8 = (bf16[16,512,256]{2,1,0:T(8,128)(2,1)}, bf16[16,512,256]{2,1,0:T(8,128)(2,1)}, u32[]{:S(2)}, u32[]{:S(2)}) collective-permute-start(bf16[16,512,256]{2,1,0:T(8,128)(2,1)} %bitcast.540), channel_id=1, source_target_pairs={{0,16},{16,0},{32,48},{48,32},{64,80},{80,64},{96,112},{112,96},{1... | collective-permute-start | bytes 12582920 | tf_op jit(solution)/shard_map/ppermute | solution.py:17
  3.9 7.1 %collective-permute-start.5 = (f32[8192]{0:T(1024)}, f32[8192]{0:T(1024)S(1)}, u32[]{:S(2)}, u32[]{:S(2)}) collective-permute-start(f32[8192]{0:T(1024)} %bitcast.551), channel_id=1, source_target_pairs={{0,16},{16,0},{32,48},{48,32},{64,80},{80,64},{96,112},{112,96},{1... | collective-permute-start | bytes 98312 | tf_op jit(solution)/shard_map/ppermute | solution.py:17
  7.1 6.2 %collective-permute-start.2 = (bf16[64,512]{1,0:T(8,128)(2,1)S(1)}, bf16[64,512]{1,0:T(8,128)(2,1)S(1)}, u32[]{:S(2)}, u32[]{:S(2)}) collective-permute-start(bf16[64,512]{1,0:T(8,128)(2,1)S(1)} %fusion.160), channel_id=1, source_target_pairs={{32,0},{48,16},{33,1},{49,17},{34,2},{50,18},{35,3},{51,19},{36,4}... | collective-permute-start | bytes 196616 | tf_op jit(solution)/shard_map/ppermute | solution.py:22
  8.4 7.7 %collective-permute-start.3 = (bf16[64,512]{1,0:T(8,128)(2,1)S(1)}, bf16[64,512]{1,0:T(8,128)(2,1)S(1)}, u32[]{:S(2)}, u32[]{:S(2)}) collective-permute-start(bf16[64,512]{1,0:T(8,128)(2,1)S(1)} %fusion.160), channel_id=1, source_target_pairs={{64,0},{80,16},{65,1},{81,17},{66,2},{82,18},{67,3},{83,19},{68,4}... | collective-permute-start | bytes 196616 | tf_op jit(solution)/shard_map/ppermute | solution.py:22
  9.7 7.9 %collective-permute-start.4 = (bf16[64,512]{1,0:T(8,128)(2,1)S(1)}, bf16[64,512]{1,0:T(8,128)(2,1)}, u32[]{:S(2)}, u32[]{:S(2)}) collective-permute-start(bf16[64,512]{1,0:T(8,128)(2,1)S(1)} %fusion.160), channel_id=1, source_target_pairs={{96,0},{112,16},{97,1},{113,17},{98,2},{114,18},{99,3},{115,19},{1... | collective-permute-start | bytes 196616 | tf_op jit(solution)/shard_map/ppermute | solution.py:22
  19.7 10.9 %collective-permute-start.7 = (f32[4,256]{1,0:T(4,128)S(1)}, f32[4,256]{1,0:T(4,128)S(1)}, u32[]{:S(2)}, u32[]{:S(2)}) collective-permute-start(f32[4,256]{1,0:T(4,128)S(1)} %slice.563), channel_id=1, source_target_pairs={{0,16},{16,0},{32,48},{48,32},{64,80},{80,64},{96,112},{112,96},{1... | collective-permute-start | bytes 12296 | tf_op jit(solution)/shard_map/ppermute | solution.py:17
  21.9 8.7 %collective-permute-start.6 = (f32[4,16,256]{2,1,0:T(8,128)S(1)}, f32[4,16,256]{2,1,0:T(8,128)S(1)}, u32[]{:S(2)}, u32[]{:S(2)}) collective-permute-start(f32[4,16,256]{2,1,0:T(8,128)S(1)} %dynamic-slice_bitcast_fusion), channel_id=1, source_target_pairs={{0,16},{16,0},{32,48},{48,32},{64,80},{80,64},{96,112},{112,96},{1... | collective-permute-start | bytes 196616 | tf_op jit(solution)/shard_map/ppermute | solution.py:17
  22.4 25.9 %all-to-all-start.8 = ((bf16[16,64,512]{2,1,0:T(8,128)(2,1)}), bf16[16,64,512]{2,1,0:T(8,128)(2,1)S(1)}, u32[]{:S(2)}, u32[]{:S(2)}) async-start(bf16[16,64,512]{2,1,0:T(8,128)(2,1)} %broadcast_in_dim.35), calls=%async_computation.8 | async-start | bytes 2097152 | tf_op jit(solution)/shard_map/all_to_all | solution.py:26
  48.4 3.7 %copy-start.1 = (bf16[16,512,256]{2,1,0:T(8,128)(2,1)S(1)}, bf16[16,512,256]{2,1,0:T(8,128)(2,1)}, u32[]{:S(2)}) copy-start(bf16[16,512,256]{2,1,0:T(8,128)(2,1)} %get-tuple-element.108) | copy-start | bytes 12582916 | tf_op jit(solution)/shard_map/cond
  73.7 3.2 %collective-permute-start.9 = (bf16[64,512]{1,0:T(8,128)(2,1)S(1)}, bf16[64,512]{1,0:T(8,128)(2,1)S(1)}, u32[]{:S(2)}, u32[]{:S(2)}) collective-permute-start(bf16[64,512]{1,0:T(8,128)(2,1)S(1)} %get-tuple-element.266), channel_id=1, source_target_pairs={{0,32},{16,48},{1,33},{17,49},{2,34},{18,50},{3,35},{19,51},{4,36}... | collective-permute-start | bytes 196616 | tf_op jit(solution)/shard_map/ppermute | solution.py:22
  76.9 0.7 collective-permute-start.10
  77.6 2.3 %collective-permute-start.11 = (bf16[64,512]{1,0:T(8,128)(2,1)S(1)}, bf16[64,512]{1,0:T(8,128)(2,1)S(1)}, u32[]{:S(2)}, u32[]{:S(2)}) collective-permute-start(bf16[64,512]{1,0:T(8,128)(2,1)S(1)} %get-tuple-element.268), channel_id=1, source_target_pairs={{64,96},{80,112},{65,97},{81,113},{66,98},{82,114},{67,99},{83,115... | collective-permute-start | bytes 196616 | tf_op jit(solution)/shard_map/ppermute | solution.py:22
  79.2 3.4 %collective-permute-start.15 = (bf16[512,64]{0,1:T(8,128)(2,1)S(1)}, bf16[512,64]{0,1:T(8,128)(2,1)S(1)}, u32[]{:S(2)}, u32[]{:S(2)}) collective-permute-start(bf16[512,64]{0,1:T(8,128)(2,1)S(1)} %constant_dynamic-slice_fusion), channel_id=1, source_target_pairs={{0,16},{16,0},{32,48},{48,32},{64,80},{80,64},{96,112},{112,96},{1... | collective-permute-start | bytes 196616 | tf_op jit(solution)/shard_map/ppermute | solution.py:17
  79.9 126.3 %collective-permute-start.12 = (bf16[64,512]{1,0:T(8,128)(2,1)S(1)}, bf16[64,512]{1,0:T(8,128)(2,1)S(1)}, u32[]{:S(2)}, u32[]{:S(2)}) collective-permute-start(bf16[64,512]{1,0:T(8,128)(2,1)S(1)} %get-tuple-element.269), channel_id=1, source_target_pairs={{96,0},{112,16},{97,1},{113,17},{98,2},{114,18},{99,3},{115,19},{1... | collective-permute-start | bytes 196616 | tf_op jit(solution)/shard_map/ppermute | solution.py:22
  81.2 125.1 %collective-permute-start.13 = (bf16[64,512]{1,0:T(8,128)(2,1)S(1)}, bf16[64,512]{1,0:T(8,128)(2,1)S(1)}, u32[]{:S(2)}, u32[]{:S(2)}) collective-permute-start(bf16[64,512]{1,0:T(8,128)(2,1)S(1)} %get-tuple-element.269), channel_id=1, source_target_pairs={{96,32},{112,48},{97,33},{113,49},{98,34},{114,50},{99,35},{115,51... | collective-permute-start | bytes 196616 | tf_op jit(solution)/shard_map/ppermute | solution.py:22
  81.9 124.4 %collective-permute-start.14 = (bf16[64,512]{1,0:T(8,128)(2,1)S(1)}, bf16[64,512]{1,0:T(8,128)(2,1)S(1)}, u32[]{:S(2)}, u32[]{:S(2)}) collective-permute-start(bf16[64,512]{1,0:T(8,128)(2,1)S(1)} %get-tuple-element.269), channel_id=1, source_target_pairs={{96,64},{112,80},{97,65},{113,81},{98,66},{114,82},{99,67},{115,83... | collective-permute-start | bytes 196616 | tf_op jit(solution)/shard_map/ppermute | solution.py:22
  218.7 1.3 collective-permute-start.16

commit v3 on v2

--- a/solution.py
+++ b/solution.py
@@ -7,7 +7,6 @@
 
 SHORT = 7
 CORES = 2
-RECUT = 2
 LEAD = 8
 EXTRA = 8
 
@@ -41,8 +40,11 @@
 def terms_kernel(filt_ref, history_ref, out_ref, shifted):
     steps = out_ref.shape[0]
     length = history_ref.shape[1]
-    for k in range(steps):
-        shifted[k] = filt_ref[LEAD - k : LEAD - k + length, :]
+
+    @pl.when(pl.program_id(0) == 0)
+    def _():
+        for k in range(steps):
+            shifted[k] = filt_ref[LEAD - k : LEAD - k + length, :]
 
     def one_request(b, carry):
         rows = history_ref[b].astype(jnp.float32)
@@ -56,11 +58,16 @@
 def cache_terms(filt, history, steps):
     requests, length, chan = history.shape
     padded = jnp.pad(filt[::-1].astype(jnp.float32), ((LEAD, 0), (0, 0)))
+    block = LEAD
     return pl.pallas_call(
         terms_kernel,
+        grid=(requests // block,),
         out_shape=jax.ShapeDtypeStruct((steps, requests, chan), jnp.float32),
-        in_specs=[pl.BlockSpec(memory_space=pltpu.VMEM)] * 2,
-        out_specs=pl.BlockSpec(memory_space=pltpu.VMEM),
+        in_specs=[
+            pl.BlockSpec(padded.shape, lambda i: (0, 0)),
+            pl.BlockSpec((block, length, chan), lambda i: (i, 0, 0)),
+        ],
+        out_specs=pl.BlockSpec((steps, block, chan), lambda i: (0, i, 0)),
         scratch_shapes=[pltpu.VMEM((steps, length, chan), jnp.float32)],
         compiler_params=pltpu.CompilerParams(vmem_limit_bytes=24 << 20),
         cost_estimate=pl.CostEstimate(
@@ -69,6 +76,42 @@
             transcendentals=0,
         ),
     )(padded, history)
+
+
+def fetch_kernel(choice_ref, *refs):
+    count = (len(refs) - 2) // 2
+    sources, out_ref, sem = refs[: 2 * count], refs[-2], refs[-1]
+    depth = out_ref.shape[1] // count
+    for pick in range(2):
+
+        @pl.when(choice_ref[0] == pick)
+        def _():
+            moves = [
+                pltpu.make_async_copy(
+                    sources[pick * count + n], out_ref.at[:, pl.ds(n * depth, depth)], sem.at[n]
+                )
+                for n in range(count)
+            ]
+            for move in moves:
+                move.start()
+            for move in moves:
+                move.wait()
+
+
+def fetch(choice, first, second):
+    count = len(first)
+    groups, depth, chan = first[0].shape
+    size = groups * depth * count * chan
+    return pl.pallas_call(
+        fetch_kernel,
+        out_shape=jax.ShapeDtypeStruct((groups, depth * count, chan), first[0].dtype),
+        in_specs=[pl.BlockSpec(memory_space=pltpu.SMEM)]
+        + [pl.BlockSpec(memory_space=pl.ANY)] * (2 * count),
+        out_specs=pl.BlockSpec(memory_space=pltpu.VMEM),
+        scratch_shapes=[pltpu.SemaphoreType.DMA((count,))],
+        compiler_params=pltpu.CompilerParams(vmem_limit_bytes=24 << 20),
+        cost_estimate=pl.CostEstimate(flops=0, bytes_accessed=4 * size, transcendentals=0),
+    )(choice.reshape(1), *first, *second)
 
 
 def as_row_pair(column, width):
@@ -104,18 +147,17 @@
     taps = conv_filters.shape[1]
     cols = unembed.shape[1]
 
-    ids = token_ids.reshape(steps, CORES, own).transpose(1, 0, 2).reshape(CORES, rows)
     vocab_ids = section * vocab_local + jnp.arange(vocab_local, dtype=jnp.int32)
     table_part = lax.dynamic_slice_in_dim(embed_table, group * part, part, 1)
 
     def find(half):
-        half_ids = lax.dynamic_index_in_dim(ids, half, 0, keepdims=False)
-        one_hot = (half_ids[:, None] == vocab_ids).astype(bf16)
+        ids = lax.dynamic_slice_in_dim(token_ids, half * own, own, 1)
+        one_hot = (ids[:, :, None] == vocab_ids).astype(bf16).reshape(rows, vocab_local)
         return jnp.dot(one_hot, table_part, preferred_element_type=f32).astype(bf16)
 
     on_chip = find(core) + swap_cores(find(1 - core))
     on_chip, mine, small = lax.optimization_barrier(
-        (on_chip, proj_weights[0], (norm_gains[0], unembed))
+        (on_chip, proj_weights[0].reshape(groups, part, chan), (norm_gains[0], unembed))
     )
     my_gain, unembed = small
 
@@ -128,28 +170,22 @@
     chunk = on_chip
     for source in range(1, planes):
         chunk = chunk + to_plane(on_chip, source, 0)
-    blocks, filters, history = lax.optimization_barrier(
-        (copies(chunk), conv_filters[0], conv_caches[0])
-    )
-    gathered = exchange(blocks)
-
-    mask = jnp.where(block_types[0] == 1, 1.0, (jnp.arange(taps) < SHORT).astype(f32))
-    filt = filters.astype(f32) * mask[:, None]
-    terms = cache_terms(filt, history, steps).reshape(steps, CORES, own, chan)
-    terms_kept = lax.dynamic_index_in_dim(terms, core, 1, keepdims=False)
-    terms_given = lax.dynamic_index_in_dim(terms, 1 - core, 1, keepdims=False)
-    terms_other = swap_cores(terms_given)
-    base_in = jnp.where(core == 0, terms_kept, terms_other)
-    base_out = jnp.where(core == 0, terms_other, terms_kept)
-    lags_in, lags_out = pair(filt[:steps])
-    weight_in, weight_out = pair(mine.reshape(groups, part, chan))
     gain_in, gain_out = pair(my_gain)
     gain_in_all = gain_in.reshape(groups, 1, part)
     gain_in = lax.dynamic_slice_in_dim(gain_in, group * part, part, 0)
     gain_out = lax.dynamic_slice_in_dim(gain_out, group * part, part, 0)
-    head = pair(lax.dynamic_slice_in_dim(unembed, group * part, part, 0))
-    head = jnp.concatenate(head, 1)
-    head_gain = lax.dynamic_slice_in_dim(final_gain, group * part, part, 0)
+
+    def setup(filters, history):
+        mask = jnp.where(block_types[0] == 1, 1.0, (jnp.arange(taps) < SHORT).astype(f32))
+        filt = filters.astype(f32) * mask[:, None]
+        terms = cache_terms(filt, history, steps).reshape(steps, CORES, own, chan)
+        terms_kept = lax.dynamic_index_in_dim(terms, core, 1, keepdims=False)
+        terms_given = lax.dynamic_index_in_dim(terms, 1 - core, 1, keepdims=False)
+        terms_other = swap_cores(terms_given)
+        base_in = jnp.where(core == 0, terms_kept, terms_other)
+        base_out = jnp.where(core == 0, terms_other, terms_kept)
+        lags_in, lags_out = pair(filt[:steps])
+        return base_in, lags_in, base_out, lags_out
 
     def convolve(signal, base, lags):
         signal = signal.astype(f32).reshape(steps, own, chan)
@@ -161,20 +197,37 @@
             results.append(total)
         return jnp.stack(results).reshape(rows, chan)
 
-    def gate(a):
+    def gate(a, conv):
+        base_in, lags_in, base_out, lags_out = conv
         z = convolve(a.astype(bf16), base_in, lags_in).astype(bf16)
         return (z.astype(f32) * convolve(z, base_out, lags_out)).astype(bf16)
 
-    def native(chunk, gathered):
+    def first_layer(chunk, mine, filters, history):
+        blocks, mine_now, filters, history = lax.optimization_barrier(
+            (copies(chunk), mine, filters, history)
+        )
+        gathered = exchange(blocks)
+        conv = setup(filters, history)
+        other = swap_cores(mine_now)
+        weight_in = fetch(core, [mine_now], [other])
+        weight_out = fetch(1 - core, [mine_now], [other])
         full = gathered.astype(f32)
         mean_square = jnp.sum(full * full, axis=(0, 2), keepdims=True) / width
         normed = (full * lax.rsqrt(mean_square + 1e-06) * gain_in_all).astype(bf16)
-        g = gate(jnp.einsum("trk,tkc->rc", normed, weight_in, preferred_element_type=f32))
+        a = jnp.einsum("trk,tkc->rc", normed, weight_in, preferred_element_type=f32)
+        g = gate(a, conv)
         partial = jnp.einsum("rc,tkc->trk", g, weight_out, preferred_element_type=f32)
         summed = jnp.sum(exchange(partial.astype(bf16)).astype(f32), axis=0)
-        return (chunk.astype(f32) + gain_out * summed).astype(bf16)
-
-    def recut(chunk, cut_in, cut_out):
+        chunk = (chunk.astype(f32) + gain_out * summed).astype(bf16)
+        half = mine[:, : part // 2]
+        return chunk, conv, [unset(half)] * 2, [unset(half)] * 2
+
+    def prepare(chunk, mine, filters, history):
+        cut = [exchange(mine[:, : part // 2]), exchange(mine[:, part // 2 :])]
+        other = [swap_cores(piece) for piece in cut]
+        return chunk, setup(filters, history), cut, other
+
+    def later_layer(chunk, conv, cut_in, cut_out):
         values = chunk.astype(f32)
         squares = jnp.sum(values * values, axis=1, keepdims=True)
         scaled = (values * gain_in).astype(bf16)
@@ -182,33 +235,22 @@
         packed = jnp.concatenate([partial.astype(bf16), copies(as_row_pair(squares, chan))], 1)
         totals = jnp.sum(exchange(packed).astype(f32), axis=0)
         square = (totals[rows] + totals[rows + 1])[:rows, None]
-        g = gate(totals[:rows] * lax.rsqrt(square / width + 1e-06))
+        g = gate(totals[:rows] * lax.rsqrt(square / width + 1e-06), conv)
         whole = exchange(copies(g))
         summed = jnp.einsum("trc,tkc->rk", whole, cut_out, preferred_element_type=f32)
         return (values + gain_out * summed).astype(bf16)
 
-    def cut(mine):
-        return pair(exchange(mine))
-
-    cut_in, cut_out = lax.cond(
-        plane >= RECUT,
-        cut,
-        lambda mine: (unset(mine), unset(mine)),
-        mine.reshape(groups, part, chan),
-    )
-    chunk = lax.cond(plane == 0, native, lambda chunk, gathered: chunk, chunk, gathered)
+    chunk, conv, cut, other = lax.cond(
+        plane == 0, first_layer, prepare, chunk, mine, conv_filters[0], conv_caches[0]
+    )
+    cut_in = fetch(core, cut, other)
+    cut_out = fetch(1 - core, cut, other)
+    head = pair(lax.dynamic_slice_in_dim(unembed, group * part, part, 0))
+    head = jnp.concatenate(head, 1)
+    head_gain = lax.dynamic_slice_in_dim(final_gain, group * part, part, 0)
     for layer in range(1, planes):
         chunk = to_plane(chunk, layer - 1, layer)
-        if layer < RECUT:
-            chunk = lax.cond(
-                plane == layer, lambda c: native(c, exchange(copies(c))), lambda c: c, chunk
-            )
-            if layer == RECUT - 1:
-                chunk, cut_in, cut_out = lax.optimization_barrier((chunk, cut_in, cut_out))
-        else:
-            chunk = lax.cond(
-                plane == layer, recut, lambda c, cut_in, cut_out: c, chunk, cut_in, cut_out
-            )
+        chunk = later_layer(chunk, conv, cut_in, cut_out)
 
     last = planes - 1
     shared = jnp.where(plane == last, chunk, jnp.zeros_like(chunk))

time: 223 us -> 241 us (1.081)
  waiting for transfers between devices: 146 us -> 68 us
  starting transfers between devices: 18.7 us -> 53.6 us
  blocking collectives: 31.9 us -> 53.5 us
  local copies, waits for them, and re-layouts: 7.58 us -> 22.9 us
  matrix products: 5.19 us -> 16.5 us
  Pallas kernels: 2.03 us -> 10.4 us
  other arithmetic: 8.63 us -> 11.1 us
    ppermute x9, waiting for transfers between devices: 131 us -> 14.1 us  [to_plane(): return lax.ppermute(block, 'section', route)]
    all_to_all x1 -> x5, waiting for transfers between devices: 12 us -> 50.8 us  [exchange(): return lax.all_to_all(blocks, 'tensor', 0, 0)]
    all_to_all x2 -> x4, blocking collectives: 31.9 us -> 53.5 us  [exchange(): return lax.all_to_all(blocks, 'tensor', 0, 0)]
    ppermute x9, starting transfers between devices: 9.09 us -> 28 us  [to_plane(): return lax.ppermute(block, 'section', route)]
    all_to_all x1 -> x5, starting transfers between devices: 8.13 us -> 24.6 us  [exchange(): return lax.all_to_all(blocks, 'tensor', 0, 0)]
    dot_general x2 -> x8, matrix products: 4.62 us -> 16 us  [the longest x3 8.81 us: later_layer(): jnp.einsum('trc,tkc->rk', whole, cut_out, preferred_element_type=f32)]
    pallas_call x1 -> x5, Pallas kernels: 2.02 us -> 10.4 us  [the longest x4 8.26 us: fetch(): pl.pallas_call(fetch_kernel, out_shape=jax.ShapeDtypeStruct((groups, dept...]
    cond x2 -> x20, local copies, waits for them, and re-layouts: 0.01 us -> 7.11 us
  transfers between devices with their start and end apart: 17 -> 21, of which waited for: 8 -> 12; matrix products, arithmetic and copies ran while one was open for 6% -> 9% of each run, Pallas kernels for 1% -> 3%
where the time goes in v3:
time: 241 us; the launch traced here: 238 us
  waiting for transfers between devices  68 us (28%)
  starting transfers between devices  53.6 us (22%)
  blocking collectives  53.5 us (22%)
  local copies, waits for them, and re-layouts  22.9 us (10%)
  matrix products  16.5 us (7%)
  other arithmetic  11.1 us (5%)
  Pallas kernels  10.4 us (4%)
    all_to_all x4, blocking collectives, exchange(): return lax.all_to_all(blocks, 'tensor', 0, 0)  53.5 us
    all_to_all x5, waiting for transfers between devices, exchange(): return lax.all_to_all(blocks, 'tensor', 0, 0)  50.8 us
    ppermute x9, starting transfers between devices, to_plane(): return lax.ppermute(block, 'section', route)  28 us
    all_to_all x5, starting transfers between devices, exchange(): return lax.all_to_all(blocks, 'tensor', 0, 0)  24.6 us
    ppermute x9, waiting for transfers between devices, to_plane(): return lax.ppermute(block, 'section', route)  14.1 us
    dot_general x3, matrix products, later_layer(): jnp.einsum('trc,tkc->rk', whole, cut_out, preferred_element_type=f32)  8.81 us
    unnamed x37, local copies, waits for them, and re-layouts  8.65 us
    pallas_call x4, Pallas kernels, fetch(): pl.pallas_call(fetch_kernel, out_shape=jax.ShapeDtypeStruct((groups, dept...  8.26 us
  transfers between devices with their start and end apart: 21, of which 12 were waited for; matrix products, arithmetic and copies ran while one was open for 9% of the time, Pallas kernels for 3%

profile of v3, /device:TPU:0, one launch (start us, length us, event | category | flops | bytes accessed | tf_op | source)
XLA Modules:
  0.0 237.7 jit_solution(10435989931530101492)
XLA Ops:
  3.2 4.1 %copy.18 = bf16[1,32,127,256]{3,2,1,0:T(8,128)(2,1)} copy(bf16[1,32,127,256]{3,1,2,0:T(8,128)(2,1)} %param.17) | data formatting | bytes 4161536 | tf_op args[6]
  12.6 2.3 collective-permute-done.10
  14.9 2.8 %collective-permute-done.9 = bf16[64,512]{1,0:T(8,128)(2,1)S(1)} collective-permute-done((bf16[64,512]{1,0:T(8,128)(2,1)S(1)}, bf16[64,512]{1,0:T(8,128)(2,1)S(1)}, u32[]{:S(2)}, u32[]{:S(2)}) %collective-permute-start.9) | collective-permute-done | bytes 65568 | tf_op jit(solution)/shard_map/ppermute | solution.py:21
  17.8 61.5 %conditional.1 = (bf16[64,512]{1,0:T(8,128)(2,1)S(1)}, bf16[16,256,256]{2,1,0:T(8,128)(2,1)}, bf16[16,256,256]{2,1,0:T(8,128)(2,1)S(1)}, bf16[16,256,256]{2,1,0:...) conditional(s32[]{:T(128)} %convert_element_type.245, ...), branch_computations={%region_0.1_spmd, %region_1.4_spmd} | conditional | flops 551061952 | bytes 92445312 | solution.py:243
  20.3 8.2 %all-to-all-start.2 = ((bf16[16,64,512]{2,1,0:T(8,128)(2,1)}), bf16[16,64,512]{2,1,0:T(8,128)(2,1)}, u32[]{:S(2)}, u32[]{:S(2)}) async-start(bf16[16,64,512]{2,1,0:T(8,128)(2,1)} %broadcast_in_dim.11), calls=%async_computation.2 | async-start | bytes 2097152 | tf_op jit(solution)/shard_map/cond/branch_1_fun/all_to_all | solution.py:25
  28.6 2.1 branch_1_fun.6
  34.5 11.8 %all-to-all-done.2 = bf16[16,64,512]{2,1,0:T(8,128)(2,1)} async-done(((bf16[16,64,512]{2,1,0:T(8,128)(2,1)}), bf16[16,64,512]{2,1,0:T(8,128)(2,1)}, u32[]{:S(2)}, u32[]{:S(2)}) %all-to-all-start.2) | async-done | bytes 1048608 | tf_op jit(solution)/shard_map/cond/branch_1_fun/all_to_all | solution.py:25
  47.9 2.2 branch_1_fun.7
  50.1 2.3 fusion.5
  52.6 2.2 branch_1_fun.5
  54.8 2.4 fusion.3
  57.1 4.3 %all-to-all-start.3 = ((bf16[16,64,512]{2,1,0:T(8,128)(2,1)}), bf16[16,64,512]{2,1,0:T(8,128)(2,1)}, u32[]{:S(2)}, u32[]{:S(2)}) async-start(bf16[16,64,512]{2,1,0:T(8,128)(2,1)} %fusion.3), calls=%async_computation.3 | async-start | bytes 2097152 | tf_op jit(solution)/shard_map/cond/branch_1_fun/all_to_all | solution.py:25
  61.5 1.6 copy.38
  63.1 3.1 %copy.40 = bf16[16,256,256]{2,1,0:T(8,128)(2,1)} copy(bf16[16,256,256]{2,1,0:T(8,128)(2,1)} %branch_1_fun.9) | data formatting | bytes 4194304 | tf_op jit(solution)/shard_map/cond
  66.3 9.8 %all-to-all-done.3 = bf16[16,64,512]{2,1,0:T(8,128)(2,1)} async-done(((bf16[16,64,512]{2,1,0:T(8,128)(2,1)}), bf16[16,64,512]{2,1,0:T(8,128)(2,1)}, u32[]{:S(2)}, u32[]{:S(2)}) %all-to-all-start.3) | async-done | bytes 1048608 | tf_op jit(solution)/shard_map/cond/branch_1_fun/all_to_all | solution.py:25
  80.4 20.1 %collective-permute-start.12 = (bf16[64,512]{1,0:T(8,128)(2,1)S(1)}, bf16[64,512]{1,0:T(8,128)(2,1)S(1)}, u32[]{:S(2)}, u32[]{:S(2)}) collective-permute-start(bf16[64,512]{1,0:T(8,128)(2,1)S(1)} %get-tuple-element.87), channel_id=1, source_target_pairs={{0,32},{16,48},{1,33},{17,49},{2,34},{18,50},{3,35},{19,51},{4,36}... | collective-permute-start | bytes 196616 | tf_op jit(solution)/shard_map/ppermute | solution.py:21
  101.3 1.6 shard_map.91
  105.9 4.2 %all-to-all-start.4 = ((bf16[16,72,256]{2,1,0:T(8,128)(2,1)}), bf16[16,72,256]{2,1,0:T(8,128)(2,1)}, u32[]{:S(2)}, u32[]{:S(2)}) async-start(bf16[16,72,256]{2,1,0:T(8,128)(2,1)} %pad_maximum_fusion), calls=%async_computation.4 | async-start | bytes 1179648 | tf_op jit(solution)/shard_map/all_to_all | solution.py:25
  110.3 13.2 %all-to-all-done.4 = bf16[16,72,256]{2,1,0:T(8,128)(2,1)} async-done(((bf16[16,72,256]{2,1,0:T(8,128)(2,1)}), bf16[16,72,256]{2,1,0:T(8,128)(2,1)}, u32[]{:S(2)}, u32[]{:S(2)}) %all-to-all-start.4) | async-done | bytes 589856 | tf_op jit(solution)/shard_map/all_to_all | solution.py:25
  125.7 4.2 %all-to-all-start.5 = ((bf16[16,64,256]{2,1,0:T(8,128)(2,1)}), bf16[16,64,256]{2,1,0:T(8,128)(2,1)}, u32[]{:S(2)}, u32[]{:S(2)}) async-start(bf16[16,64,256]{2,1,0:T(8,128)(2,1)} %broadcast_in_dim.31), calls=%async_computation.5 | async-start | bytes 1048576 | tf_op jit(solution)/shard_map/all_to_all | solution.py:25
  129.9 2.3 shard_map.92
  132.2 2.0 copy-done.3
  134.2 7.5 %all-to-all-done.5 = bf16[16,64,256]{2,1,0:T(8,128)(2,1)} async-done(((bf16[16,64,256]{2,1,0:T(8,128)(2,1)}), bf16[16,64,256]{2,1,0:T(8,128)(2,1)}, u32[]{:S(2)}, u32[]{:S(2)}) %all-to-all-start.5) | async-done | bytes 524320 | tf_op jit(solution)/shard_map/all_to_all | solution.py:25
  141.7 3.9 %fusion.52 = bf16[64,512]{1,0:T(8,128)(2,1)S(1)} fusion(bf16[16,64,256]{2,1,0:T(8,128)(2,1)} %all-to-all-done.5, bf16[16,512,256]{2,1,0:T(8,128)(2,1)} %copy-done.3, bf16[64,512]{1,0:T(8,128)(2,1)S(1)} %collective-permute-done.12, f32[512]{0:T(512)S(1)} %copy-done.13), kind=kOutput, calls=%fused_computation.93 | convolution fusion | flops 268566528 | bytes 4851712 | tf_op jit(solution)/shard_map/trc,tkc->rk/dot_general | solution.py:240
  147.3 14.9 %all_to_all.52 = bf16[16,72,256]{2,1,0:T(8,128)(2,1)S(1)} all-to-all(bf16[16,72,256]{2,1,0:T(8,128)(2,1)S(1)} %pad_maximum_fusion.1), channel_id=1, replica_groups=mesh['section'=8,'tensor'=16] {'tensor'}, dimensions={0} | all-to-all | bytes 1179648 | tf_op jit(solution)/shard_map/all_to_all | solution.py:25
  162.5 13.3 %all_to_all.53 = bf16[16,64,256]{2,1,0:T(8,128)(2,1)S(1)} all-to-all(bf16[16,64,256]{2,1,0:T(8,128)(2,1)S(1)} %broadcast_in_dim.33), channel_id=1, replica_groups=mesh['section'=8,'tensor'=16] {'tensor'}, dimensions={0} | all-to-all | bytes 1048576 | tf_op jit(solution)/shard_map/all_to_all | solution.py:25
  179.0 13.5 %all_to_all.54 = bf16[16,72,256]{2,1,0:T(8,128)(2,1)S(1)} all-to-all(bf16[16,72,256]{2,1,0:T(8,128)(2,1)S(1)} %pad_maximum_fusion.2), channel_id=1, replica_groups=mesh['section'=8,'tensor'=16] {'tensor'}, dimensions={0} | all-to-all | bytes 1179648 | tf_op jit(solution)/shard_map/all_to_all | solution.py:25
  193.6 3.6 %all-to-all-start.9 = ((bf16[16,64,256]{2,1,0:T(8,128)(2,1)}), bf16[16,64,256]{2,1,0:T(8,128)(2,1)S(1)}, u32[]{:S(2)}, u32[]{:S(2)}) async-start(bf16[16,64,256]{2,1,0:T(8,128)(2,1)} %broadcast_in_dim.58), calls=%async_computation.9 | async-start | bytes 1048576 | tf_op jit(solution)/shard_map/all_to_all | solution.py:25
  198.8 8.5 %all-to-all-done.9 = bf16[16,64,256]{2,1,0:T(8,128)(2,1)S(1)} async-done(((bf16[16,64,256]{2,1,0:T(8,128)(2,1)}), bf16[16,64,256]{2,1,0:T(8,128)(2,1)S(1)}, u32[]{:S(2)}, u32[]{:S(2)}) %all-to-all-start.9) | async-done | bytes 524320 | tf_op jit(solution)/shard_map/all_to_all | solution.py:25
  207.3 3.6 %fusion.54 = bf16[64,512]{1,0:T(8,128)(2,1)S(1)} fusion(bf16[16,64,256]{2,1,0:T(8,128)(2,1)S(1)} %all-to-all-done.9, bf16[16,512,256]{2,1,0:T(8,128)(2,1)} %copy-done.3, bf16[64,512]{1,0:T(8,128)(2,1)S(1)} %collective-permute-done.14, f32[512]{0:T(512)S(1)} %copy-done.13), kind=kOutput, calls=%fused_computation.95 | convolution fusion | flops 268566528 | bytes 4851712 | tf_op jit(solution)/shard_map/trc,tkc->rk/dot_general | solution.py:240
  214.4 8.9 %collective-permute-done.15 = bf16[64,512]{1,0:T(8,128)(2,1)S(1)} collective-permute-done((bf16[64,512]{1,0:T(8,128)(2,1)S(1)}, bf16[64,512]{1,0:T(8,128)(2,1)S(1)}, u32[]{:S(2)}, u32[]{:S(2)}) %collective-permute-start.15) | collective-permute-done | bytes 65568 | tf_op jit(solution)/shard_map/ppermute | solution.py:21
  223.8 11.8 %all_to_all.55 = bf16[16,72,128]{2,1,0:T(8,128)(2,1)S(1)} all-to-all(bf16[16,72,128]{2,1,0:T(8,128)(2,1)S(1)} %broadcast_in_dim.60), channel_id=1, replica_groups=mesh['section'=8,'tensor'=16] {'tensor'}, dimensions={0} | all-to-all | bytes 589824 | tf_op jit(solution)/shard_map/all_to_all | solution.py:25
  (186 shorter events, 39.7 us)
Async XLA Ops:
  1.5 1.3 collective-permute-start.7
  3.0 8.3 %collective-permute-start.11 = (f32[8192]{0:T(1024)}, f32[8192]{0:T(1024)S(1)}, u32[]{:S(2)}, u32[]{:S(2)}) collective-permute-start(f32[8192]{0:T(1024)} %bitcast.503), channel_id=1, source_target_pairs={{0,16},{16,0},{32,48},{48,32},{64,80},{80,64},{96,112},{112,96},{1... | collective-permute-start | bytes 98312 | tf_op jit(solution)/shard_map/ppermute | solution.py:16
  3.2 14.5 %copy-start.7 = (bf16[1,128,256]{2,1,0:T(8,128)(2,1)S(1)}, bf16[1,128,256]{2,1,0:T(8,128)(2,1)}, u32[]{:S(2)}) copy-start(bf16[1,128,256]{2,1,0:T(8,128)(2,1)} %param.16) | copy-start | bytes 196612
  7.4 7.4 %collective-permute-start.10 = (bf16[64,512]{1,0:T(8,128)(2,1)S(1)}, bf16[64,512]{1,0:T(8,128)(2,1)S(1)}, u32[]{:S(2)}, u32[]{:S(2)}) collective-permute-start(bf16[64,512]{1,0:T(8,128)(2,1)S(1)} %fusion.55), channel_id=1, source_target_pairs={{96,0},{112,16},{97,1},{113,17},{98,2},{114,18},{99,3},{115,19},{1... | collective-permute-start | bytes 196616 | tf_op jit(solution)/shard_map/ppermute | solution.py:21
  8.7 6.2 %collective-permute-start.8 = (bf16[64,512]{1,0:T(8,128)(2,1)S(1)}, bf16[64,512]{1,0:T(8,128)(2,1)S(1)}, u32[]{:S(2)}, u32[]{:S(2)}) collective-permute-start(bf16[64,512]{1,0:T(8,128)(2,1)S(1)} %fusion.55), channel_id=1, source_target_pairs={{32,0},{48,16},{33,1},{49,17},{34,2},{50,18},{35,3},{51,19},{36,4}... | collective-permute-start | bytes 196616 | tf_op jit(solution)/shard_map/ppermute | solution.py:21
  10.0 7.7 %collective-permute-start.9 = (bf16[64,512]{1,0:T(8,128)(2,1)S(1)}, bf16[64,512]{1,0:T(8,128)(2,1)S(1)}, u32[]{:S(2)}, u32[]{:S(2)}) collective-permute-start(bf16[64,512]{1,0:T(8,128)(2,1)S(1)} %fusion.55), channel_id=1, source_target_pairs={{64,0},{80,16},{65,1},{81,17},{66,2},{82,18},{67,3},{83,19},{68,4}... | collective-permute-start | bytes 196616 | tf_op jit(solution)/shard_map/ppermute | solution.py:21
  17.8 10.8 %copy-start.6 = (bf16[32,127,256]{2,1,0:T(8,128)(2,1)S(1)}, bf16[32,127,256]{2,1,0:T(8,128)(2,1)}, u32[]{:S(2)}) copy-start(bf16[32,127,256]{2,1,0:T(8,128)(2,1)} %get-tuple-element.66.history_ref) | copy-start | bytes 6242308 | tf_op jit(solution)/shard_map/cond
  18.9 29.0 %collective-permute-start.4 = (bf16[16,512,256]{2,1,0:T(8,128)(2,1)}, bf16[16,512,256]{2,1,0:T(8,128)(2,1)}, u32[]{:S(2)}, u32[]{:S(2)}) collective-permute-start(bf16[16,512,256]{2,1,0:T(8,128)(2,1)} %get-tuple-element.63.refs_0_), channel_id=1, source_target_pairs={{0,16},{16,0},{32,48},{48,32},{64,80},{80,64},{96,112},{112,96},{1... | collective-permute-start | bytes 12582920 | tf_op jit(solution)/shard_map/cond/branch_1_fun/ppermute | solution.py:16
  19.6 41.8 %copy-start.17 = (f32[4,256]{1,0:T(4,128)}, f32[4,256]{1,0:T(4,128)S(1)}, u32[]{:S(2)}) copy-start(f32[4,256]{1,0:T(4,128)S(1)} %slice.544) | copy-start | bytes 12292 | tf_op jit(solution)/shard_map/cond
  19.7 11.1 %copy-start.12 = (f32[8192]{0:T(1024)S(1)}, f32[8192]{0:T(1024)}, u32[]{:S(2)}) copy-start(f32[8192]{0:T(1024)} %get-tuple-element.68) | copy-start | bytes 98308 | tf_op jit(solution)/shard_map/cond
  19.7 11.2 %collective-permute-start.6 = (f32[4,256]{1,0:T(4,128)S(1)}, f32[4,256]{1,0:T(4,128)S(1)}, u32[]{:S(2)}, u32[]{:S(2)}) collective-permute-start(f32[4,256]{1,0:T(4,128)S(1)} %slice.544), channel_id=1, source_target_pairs={{0,16},{16,0},{32,48},{48,32},{64,80},{80,64},{96,112},{112,96},{1... | collective-permute-start | bytes 12296 | tf_op jit(solution)/shard_map/cond/branch_1_fun/ppermute | solution.py:16
  20.3 26.0 %all-to-all-start.2 = ((bf16[16,64,512]{2,1,0:T(8,128)(2,1)}), bf16[16,64,512]{2,1,0:T(8,128)(2,1)}, u32[]{:S(2)}, u32[]{:S(2)}) async-start(bf16[16,64,512]{2,1,0:T(8,128)(2,1)} %broadcast_in_dim.11), calls=%async_computation.2 | async-start | bytes 2097152 | tf_op jit(solution)/shard_map/cond/branch_1_fun/all_to_all | solution.py:25
  30.7 1.5 collective-permute-start.5
  57.1 18.9 %all-to-all-start.3 = ((bf16[16,64,512]{2,1,0:T(8,128)(2,1)}), bf16[16,64,512]{2,1,0:T(8,128)(2,1)}, u32[]{:S(2)}, u32[]{:S(2)}) async-start(bf16[16,64,512]{2,1,0:T(8,128)(2,1)} %fusion.3), calls=%async_computation.3 | async-start | bytes 2097152 | tf_op jit(solution)/shard_map/cond/branch_1_fun/all_to_all | solution.py:25
  63.1 14.4 %copy-start.14 = (f32[512]{0:T(512)S(1)}, f32[512]{0:T(512)}, u32[]{:S(2)}) copy-start(f32[512]{0:T(512)} %get-tuple-element.58) | copy-start | bytes 6148 | tf_op jit(solution)/shard_map/cond
  63.1 16.1 %copy-start.20 = (f32[4,256]{1,0:T(4,128)S(1)}, f32[4,256]{1,0:T(4,128)}, u32[]{:S(2)}) copy-start(f32[4,256]{1,0:T(4,128)} %copy-done.19) | copy-start | bytes 12292 | tf_op jit(solution)/shard_map/cond
  80.4 22.5 %copy-start.8 = (f32[4,16,256]{2,1,0:T(8,128)}, f32[4,16,256]{2,1,0:T(8,128)S(1)}, u32[]{:S(2)}) copy-start(f32[4,16,256]{2,1,0:T(8,128)S(1)} %get-tuple-element.89) | copy-start | bytes 196612
  80.4 22.5 %copy-start.10 = (f32[4,16,256]{2,1,0:T(8,128)}, f32[4,16,256]{2,1,0:T(8,128)S(1)}, u32[]{:S(2)}) copy-start(f32[4,16,256]{2,1,0:T(8,128)S(1)} %get-tuple-element.90) | copy-start | bytes 196612
  80.4 22.6 %copy-start.21 = (f32[4,256]{1,0:T(4,128)}, f32[4,256]{1,0:T(4,128)S(1)}, u32[]{:S(2)}) copy-start(f32[4,256]{1,0:T(4,128)S(1)} %get-tuple-element.92) | copy-start | bytes 12292
  80.4 22.6 %collective-permute-start.12 = (bf16[64,512]{1,0:T(8,128)(2,1)S(1)}, bf16[64,512]{1,0:T(8,128)(2,1)S(1)}, u32[]{:S(2)}, u32[]{:S(2)}) collective-permute-start(bf16[64,512]{1,0:T(8,128)(2,1)S(1)} %get-tuple-element.87), channel_id=1, source_target_pairs={{0,32},{16,48},{1,33},{17,49},{2,34},{18,50},{3,35},{19,51},{4,36}... | collective-permute-start | bytes 196616 | tf_op jit(solution)/shard_map/ppermute | solution.py:21
  105.9 17.6 %all-to-all-start.4 = ((bf16[16,72,256]{2,1,0:T(8,128)(2,1)}), bf16[16,72,256]{2,1,0:T(8,128)(2,1)}, u32[]{:S(2)}, u32[]{:S(2)}) async-start(bf16[16,72,256]{2,1,0:T(8,128)(2,1)} %pad_maximum_fusion), calls=%async_computation.4 | async-start | bytes 1179648 | tf_op jit(solution)/shard_map/all_to_all | solution.py:25
  125.7 16.0 %all-to-all-start.5 = ((bf16[16,64,256]{2,1,0:T(8,128)(2,1)}), bf16[16,64,256]{2,1,0:T(8,128)(2,1)}, u32[]{:S(2)}, u32[]{:S(2)}) async-start(bf16[16,64,256]{2,1,0:T(8,128)(2,1)} %broadcast_in_dim.31), calls=%async_computation.5 | async-start | bytes 1048576 | tf_op jit(solution)/shard_map/all_to_all | solution.py:25
  129.9 11.8 %copy-start.13 = (f32[512]{0:T(512)S(1)}, f32[512]{0:T(512)}, u32[]{:S(2)}) copy-start(f32[512]{0:T(512)} %dynamic-slice_select_fusion) | copy-start | bytes 6148
  145.6 0.7 collective-permute-start.13
  147.3 28.6 %copy-start.4 = (bf16[16,512,256]{2,1,0:T(8,128)(2,1)S(1)}, bf16[16,512,256]{2,1,0:T(8,128)(2,1)}, u32[]{:S(2)}) copy-start(bf16[16,512,256]{2,1,0:T(8,128)(2,1)} %copy-done.3) | copy-start | bytes 12582916
  177.2 0.7 collective-permute-start.14
  193.6 13.7 %all-to-all-start.9 = ((bf16[16,64,256]{2,1,0:T(8,128)(2,1)}), bf16[16,64,256]{2,1,0:T(8,128)(2,1)S(1)}, u32[]{:S(2)}, u32[]{:S(2)}) async-start(bf16[16,64,256]{2,1,0:T(8,128)(2,1)} %broadcast_in_dim.58), calls=%async_computation.9 | async-start | bytes 1048576 | tf_op jit(solution)/shard_map/all_to_all | solution.py:25
  198.8 14.7 %collective-permute-start.18 = (bf16[512,64]{0,1:T(8,128)(2,1)S(1)}, bf16[512,64]{0,1:T(8,128)(2,1)S(1)}, u32[]{:S(2)}, u32[]{:S(2)}) collective-permute-start(bf16[512,64]{0,1:T(8,128)(2,1)S(1)} %constant_dynamic-slice_fusion), channel_id=1, source_target_pairs={{0,16},{16,0},{32,48},{48,32},{64,80},{80,64},{96,112},{112,96},{1... | collective-permute-start | bytes 196616 | tf_op jit(solution)/shard_map/ppermute | solution.py:16
  210.9 12.5 %collective-permute-start.15 = (bf16[64,512]{1,0:T(8,128)(2,1)S(1)}, bf16[64,512]{1,0:T(8,128)(2,1)S(1)}, u32[]{:S(2)}, u32[]{:S(2)}) collective-permute-start(bf16[64,512]{1,0:T(8,128)(2,1)S(1)} %fusion.54), channel_id=1, source_target_pairs={{96,0},{112,16},{97,1},{113,17},{98,2},{114,18},{99,3},{115,19},{1... | collective-permute-start | bytes 196616 | tf_op jit(solution)/shard_map/ppermute | solution.py:21
  212.2 11.2 %collective-permute-start.16 = (bf16[64,512]{1,0:T(8,128)(2,1)S(1)}, bf16[64,512]{1,0:T(8,128)(2,1)S(1)}, u32[]{:S(2)}, u32[]{:S(2)}) collective-permute-start(bf16[64,512]{1,0:T(8,128)(2,1)S(1)} %fusion.54), channel_id=1, source_target_pairs={{96,32},{112,48},{97,33},{113,49},{98,34},{114,50},{99,35},{115,51... | collective-permute-start | bytes 196616 | tf_op jit(solution)/shard_map/ppermute | solution.py:21
  212.9 10.5 %collective-permute-start.17 = (bf16[64,512]{1,0:T(8,128)(2,1)S(1)}, bf16[64,512]{1,0:T(8,128)(2,1)S(1)}, u32[]{:S(2)}, u32[]{:S(2)}) collective-permute-start(bf16[64,512]{1,0:T(8,128)(2,1)S(1)} %fusion.54), channel_id=1, source_target_pairs={{96,64},{112,80},{97,65},{113,81},{98,66},{114,82},{99,67},{115,83... | collective-permute-start | bytes 196616 | tf_op jit(solution)/shard_map/ppermute | solution.py:21
  235.8 1.3 collective-permute-start.19
  (14 other events, 48.2 us)

commit v4 on v2

--- a/solution.py
+++ b/solution.py
@@ -38,37 +38,94 @@
     )()
 
 
-def terms_kernel(filt_ref, history_ref, out_ref, shifted):
+def terms_kernel(filt_ref, history_ref, out_ref):
     steps = out_ref.shape[0]
-    length = history_ref.shape[1]
+    length, requests, chan = history_ref.shape
+
+    def one_position(r, totals):
+        row = history_ref[r].astype(jnp.float32)
+        return tuple(
+            total + filt_ref[pl.ds(LEAD + r - k, 1), :] * row for k, total in enumerate(totals)
+        )
+
+    zeros = (jnp.zeros((requests, chan), jnp.float32),) * steps
+    totals = lax.fori_loop(0, length, one_position, zeros)
     for k in range(steps):
-        shifted[k] = filt_ref[LEAD - k : LEAD - k + length, :]
-
-    def one_request(b, carry):
-        rows = history_ref[b].astype(jnp.float32)
-        for k in range(steps):
-            out_ref[k, pl.ds(b, 1), :] = jnp.sum(shifted[k] * rows, axis=0, keepdims=True)
-        return carry
-
-    lax.fori_loop(0, history_ref.shape[0], one_request, 0)
+        out_ref[k] = totals[k]
 
 
 def cache_terms(filt, history, steps):
-    requests, length, chan = history.shape
+    length, requests, chan = history.shape
     padded = jnp.pad(filt[::-1].astype(jnp.float32), ((LEAD, 0), (0, 0)))
     return pl.pallas_call(
         terms_kernel,
         out_shape=jax.ShapeDtypeStruct((steps, requests, chan), jnp.float32),
         in_specs=[pl.BlockSpec(memory_space=pltpu.VMEM)] * 2,
         out_specs=pl.BlockSpec(memory_space=pltpu.VMEM),
-        scratch_shapes=[pltpu.VMEM((steps, length, chan), jnp.float32)],
-        compiler_params=pltpu.CompilerParams(vmem_limit_bytes=24 << 20),
+        compiler_params=pltpu.CompilerParams(vmem_limit_bytes=8 << 20),
         cost_estimate=pl.CostEstimate(
             flops=2 * steps * requests * length * chan,
             bytes_accessed=2 * requests * length * chan,
             transcendentals=0,
         ),
     )(padded, history)
+
+
+def stage_kernel(source_ref, out_ref, sem):
+    move = pltpu.make_async_copy(source_ref, out_ref, sem)
+    move.start()
+    move.wait()
+
+
+def stage(array):
+    return pl.pallas_call(
+        stage_kernel,
+        out_shape=jax.ShapeDtypeStruct(array.shape, array.dtype),
+        in_specs=[pl.BlockSpec(memory_space=pl.ANY)],
+        out_specs=pl.BlockSpec(memory_space=pltpu.VMEM),
+        scratch_shapes=[pltpu.SemaphoreType.DMA],
+        compiler_params=pltpu.CompilerParams(vmem_limit_bytes=8 << 20),
+    )(array)
+
+
+def pick(core, arrays, plans, like):
+    def kernel(core_ref, *refs):
+        sources, out_ref, sems = refs[:-2], refs[-2], refs[-1]
+        for c in range(CORES):
+
+            @pl.when(core_ref[0] == c)
+            def _():
+                moves = [
+                    pltpu.make_async_copy(
+                        sources[which].at[:, pl.ds(start, size)],
+                        out_ref.at[:, pl.ds(place, size)],
+                        sems.at[n],
+                    )
+                    for n, (which, start, place, size) in enumerate(plans[c])
+                ]
+                for move in moves:
+                    move.start()
+                for move in moves:
+                    move.wait()
+
+    return pl.pallas_call(
+        kernel,
+        out_shape=jax.ShapeDtypeStruct(like.shape, like.dtype),
+        in_specs=[pl.BlockSpec(memory_space=pltpu.SMEM)]
+        + [pl.BlockSpec(memory_space=pl.ANY)] * len(arrays),
+        out_specs=pl.BlockSpec(memory_space=pltpu.VMEM),
+        scratch_shapes=[pltpu.SemaphoreType.DMA((max(map(len, plans)),))],
+        compiler_params=pltpu.CompilerParams(vmem_limit_bytes=8 << 20),
+    )(core.reshape(1), *arrays)
+
+
+def even_of(core, mine, other):
+    size = mine.shape[1]
+    return pick(core, [mine, other], [[(0, 0, 0, size)], [(1, 0, 0, size)]], mine)
+
+
+def odd_of(core, mine, other):
+    return even_of(1 - core, mine, other)
 
 
 def as_row_pair(column, width):
@@ -104,20 +161,23 @@
     taps = conv_filters.shape[1]
     cols = unembed.shape[1]
 
-    ids = token_ids.reshape(steps, CORES, own).transpose(1, 0, 2).reshape(CORES, rows)
     vocab_ids = section * vocab_local + jnp.arange(vocab_local, dtype=jnp.int32)
     table_part = lax.dynamic_slice_in_dim(embed_table, group * part, part, 1)
 
     def find(half):
-        half_ids = lax.dynamic_index_in_dim(ids, half, 0, keepdims=False)
-        one_hot = (half_ids[:, None] == vocab_ids).astype(bf16)
+        ids = lax.dynamic_slice_in_dim(token_ids, half * own, own, 1)
+        one_hot = (ids[:, :, None] == vocab_ids).astype(bf16).reshape(rows, vocab_local)
         return jnp.dot(one_hot, table_part, preferred_element_type=f32).astype(bf16)
 
     on_chip = find(core) + swap_cores(find(1 - core))
     on_chip, mine, small = lax.optimization_barrier(
-        (on_chip, proj_weights[0], (norm_gains[0], unembed))
-    )
-    my_gain, unembed = small
+        (
+            on_chip,
+            proj_weights[0].reshape(groups, part, chan),
+            (norm_gains[0], unembed, conv_filters[0], conv_caches[0].transpose(1, 0, 2)),
+        )
+    )
+    my_gain, unembed, filters, history = small
 
     def pair(mine):
         other = swap_cores(mine)
@@ -128,10 +188,10 @@
     chunk = on_chip
     for source in range(1, planes):
         chunk = chunk + to_plane(on_chip, source, 0)
-    blocks, filters, history = lax.optimization_barrier(
-        (copies(chunk), conv_filters[0], conv_caches[0])
-    )
-    gathered = exchange(blocks)
+    gain_in, gain_out = pair(my_gain)
+    gain_in_all = gain_in.reshape(groups, 1, part)
+    gain_in = lax.dynamic_slice_in_dim(gain_in, group * part, part, 0)
+    gain_out = lax.dynamic_slice_in_dim(gain_out, group * part, part, 0)
 
     mask = jnp.where(block_types[0] == 1, 1.0, (jnp.arange(taps) < SHORT).astype(f32))
     filt = filters.astype(f32) * mask[:, None]
@@ -142,14 +202,7 @@
     base_in = jnp.where(core == 0, terms_kept, terms_other)
     base_out = jnp.where(core == 0, terms_other, terms_kept)
     lags_in, lags_out = pair(filt[:steps])
-    weight_in, weight_out = pair(mine.reshape(groups, part, chan))
-    gain_in, gain_out = pair(my_gain)
-    gain_in_all = gain_in.reshape(groups, 1, part)
-    gain_in = lax.dynamic_slice_in_dim(gain_in, group * part, part, 0)
-    gain_out = lax.dynamic_slice_in_dim(gain_out, group * part, part, 0)
-    head = pair(lax.dynamic_slice_in_dim(unembed, group * part, part, 0))
-    head = jnp.concatenate(head, 1)
-    head_gain = lax.dynamic_slice_in_dim(final_gain, group * part, part, 0)
+    theirs = swap_cores(mine)
 
     def convolve(signal, base, lags):
         signal = signal.astype(f32).reshape(steps, own, chan)
@@ -165,16 +218,24 @@
         z = convolve(a.astype(bf16), base_in, lags_in).astype(bf16)
         return (z.astype(f32) * convolve(z, base_out, lags_out)).astype(bf16)
 
-    def native(chunk, gathered):
-        full = gathered.astype(f32)
-        mean_square = jnp.sum(full * full, axis=(0, 2), keepdims=True) / width
-        normed = (full * lax.rsqrt(mean_square + 1e-06) * gain_in_all).astype(bf16)
-        g = gate(jnp.einsum("trk,tkc->rc", normed, weight_in, preferred_element_type=f32))
-        partial = jnp.einsum("rc,tkc->trk", g, weight_out, preferred_element_type=f32)
-        summed = jnp.sum(exchange(partial.astype(bf16)).astype(f32), axis=0)
-        return (chunk.astype(f32) + gain_out * summed).astype(bf16)
-
-    def recut(chunk, cut_in, cut_out):
+    def first_plane(chunk, mine, theirs):
+        weight_in, weight_out = even_of(core, mine, theirs), odd_of(core, mine, theirs)
+        return native_layer(chunk, weight_in, weight_out), unset(mine), unset(mine)
+
+    def second_plane(chunk, mine, theirs):
+        half = part // 2
+        plans = [[(0, 0, 0, half)], [(1, half, 0, half)]]
+        piece = exchange(pick(core, [mine, theirs], plans, mine[:, :half]))
+        plans = [[(0, 0, 0, half), (1, 0, half, half)], [(1, 0, 0, half), (0, 0, half, half)]]
+        cut_in = pick(core, [piece, swap_cores(piece)], plans, mine)
+        return chunk, cut_in, odd_of(core, mine, theirs)
+
+    def last_planes(chunk, mine, theirs):
+        cut = exchange(stage(mine))
+        other = swap_cores(cut)
+        return chunk, even_of(core, cut, other), odd_of(core, cut, other)
+
+    def project_in(chunk, cut_in):
         values = chunk.astype(f32)
         squares = jnp.sum(values * values, axis=1, keepdims=True)
         scaled = (values * gain_in).astype(bf16)
@@ -182,33 +243,42 @@
         packed = jnp.concatenate([partial.astype(bf16), copies(as_row_pair(squares, chan))], 1)
         totals = jnp.sum(exchange(packed).astype(f32), axis=0)
         square = (totals[rows] + totals[rows + 1])[:rows, None]
-        g = gate(totals[:rows] * lax.rsqrt(square / width + 1e-06))
-        whole = exchange(copies(g))
+        return gate(totals[:rows] * lax.rsqrt(square / width + 1e-06))
+
+    def project_out(chunk, g, weight_out):
+        partial = jnp.einsum("rc,tkc->trk", g, weight_out, preferred_element_type=f32)
+        summed = jnp.sum(exchange(partial.astype(bf16)).astype(f32), axis=0)
+        return (chunk.astype(f32) + gain_out * summed).astype(bf16)
+
+    def native_layer(chunk, weight_in, weight_out):
+        full = exchange(copies(chunk)).astype(f32)
+        mean_square = jnp.sum(full * full, axis=(0, 2), keepdims=True) / width
+        normed = (full * lax.rsqrt(mean_square + 1e-06) * gain_in_all).astype(bf16)
+        g = gate(jnp.einsum("trk,tkc->rc", normed, weight_in, preferred_element_type=f32))
+        return project_out(chunk, g, weight_out)
+
+    def half_cut_layer(chunk, cut_in, weight_out):
+        return project_out(chunk, project_in(chunk, cut_in), weight_out)
+
+    def cut_layer(chunk, cut_in, cut_out):
+        whole = exchange(copies(project_in(chunk, cut_in)))
         summed = jnp.einsum("trc,tkc->rk", whole, cut_out, preferred_element_type=f32)
-        return (values + gain_out * summed).astype(bf16)
-
-    def cut(mine):
-        return pair(exchange(mine))
-
-    cut_in, cut_out = lax.cond(
-        plane >= RECUT,
-        cut,
-        lambda mine: (unset(mine), unset(mine)),
-        mine.reshape(groups, part, chan),
-    )
-    chunk = lax.cond(plane == 0, native, lambda chunk, gathered: chunk, chunk, gathered)
-    for layer in range(1, planes):
+        return (chunk.astype(f32) + gain_out * summed).astype(bf16)
+
+    chunk, weight_in, weight_out = lax.switch(
+        jnp.minimum(plane, RECUT), [first_plane, second_plane, last_planes], chunk, mine, theirs
+    )
+    chunk = to_plane(chunk, 0, 1)
+    chunk, weight_in, weight_out, unembed = lax.optimization_barrier(
+        (chunk, weight_in, weight_out, unembed)
+    )
+    chunk = lax.cond(plane == 1, half_cut_layer, lambda c, a, b: c, chunk, weight_in, weight_out)
+    for layer in range(RECUT, planes):
         chunk = to_plane(chunk, layer - 1, layer)
-        if layer < RECUT:
-            chunk = lax.cond(
-                plane == layer, lambda c: native(c, exchange(copies(c))), lambda c: c, chunk
-            )
-            if layer == RECUT - 1:
-                chunk, cut_in, cut_out = lax.optimization_barrier((chunk, cut_in, cut_out))
-        else:
-            chunk = lax.cond(
-                plane == layer, recut, lambda c, cut_in, cut_out: c, chunk, cut_in, cut_out
-            )
+        chunk = cut_layer(chunk, weight_in, weight_out)
+    head = pair(lax.dynamic_slice_in_dim(unembed, group * part, part, 0))
+    head = jnp.concatenate(head, 1)
+    head_gain = lax.dynamic_slice_in_dim(final_gain, group * part, part, 0)
 
     last = planes - 1
     shared = jnp.where(plane == last, chunk, jnp.zeros_like(chunk))

time: 223 us -> 212 us (0.951)
  waiting for transfers between devices: 146 us -> 98.7 us
  matrix products: 5.19 us -> 17.2 us
  starting transfers between devices: 18.7 us -> 29.3 us
  blocking collectives: 31.9 us -> 38.7 us
  Pallas kernels: 2.03 us -> 7.16 us
  local copies, waits for them, and re-layouts: 7.58 us -> 11.5 us
  other arithmetic: 8.63 us -> 5.96 us
    ppermute x9, waiting for transfers between devices: 131 us -> 51.1 us  [to_plane(): return lax.ppermute(block, 'section', route)]
    all_to_all x1 -> x4, waiting for transfers between devices: 12 us -> 44 us  [exchange(): return lax.all_to_all(blocks, 'tensor', 0, 0)]
    dot_general x2 -> x6, matrix products: 4.62 us -> 16.6 us  [the longest x2 7.12 us: cut_layer(): jnp.einsum('trc,tkc->rk', whole, cut_out, preferred_element_type=f32)]
    all_to_all x1 -> x4, starting transfers between devices: 8.13 us -> 18.9 us  [exchange(): return lax.all_to_all(blocks, 'tensor', 0, 0)]
    all_to_all x2 -> x3, blocking collectives: 31.9 us -> 38.7 us  [exchange(): return lax.all_to_all(blocks, 'tensor', 0, 0)]
    select_n x3 -> x2, other arithmetic: 5.86 us -> 0.76 us  [pair(): odd = jnp.where(core == 0, other, mine)]
    pallas_call x0 -> x2, Pallas kernels: none -> 4.55 us  [pick(): pl.pallas_call(kernel, out_shape=jax.ShapeDtypeStruct(like.shape, like.dt...]
    cond x2 -> x8, local copies, waits for them, and re-layouts: 0.01 us -> 4.02 us
  transfers between devices with their start and end apart: 17 -> 20, of which waited for: 8 -> 9; matrix products, arithmetic and copies ran while one was open for 6% -> 4% of each run, Pallas kernels for 1% -> 3%
where the time goes in v4:
time: 212 us; the launch traced here: 210 us
  waiting for transfers between devices  98.7 us (47%)
  blocking collectives  38.7 us (18%)
  starting transfers between devices  29.3 us (14%)
  matrix products  17.2 us (8%)
  local copies, waits for them, and re-layouts  11.5 us (5%)
  Pallas kernels  7.16 us (3%)
  other arithmetic  5.96 us (3%)
    ppermute x9, waiting for transfers between devices, to_plane(): return lax.ppermute(block, 'section', route)  51.1 us
    all_to_all x4, waiting for transfers between devices, exchange(): return lax.all_to_all(blocks, 'tensor', 0, 0)  44 us
    all_to_all x3, blocking collectives, exchange(): return lax.all_to_all(blocks, 'tensor', 0, 0)  38.7 us
    all_to_all x4, starting transfers between devices, exchange(): return lax.all_to_all(blocks, 'tensor', 0, 0)  18.9 us
    ppermute x9, starting transfers between devices, to_plane(): return lax.ppermute(block, 'section', route)  9.11 us
    dot_general x2, matrix products, cut_layer(): jnp.einsum('trc,tkc->rk', whole, cut_out, preferred_element_type=f32)  7.12 us
    pallas_call x2, Pallas kernels, pick(): pl.pallas_call(kernel, out_shape=jax.ShapeDtypeStruct(like.shape, like.dt...  4.55 us
  transfers between devices with their start and end apart: 20, of which 9 were waited for; matrix products, arithmetic and copies ran while one was open for 4% of the time, Pallas kernels for 3%

profile of v4, /device:TPU:0, one launch (start us, length us, event | category | flops | bytes accessed | tf_op | source)
XLA Modules:
  0.0 209.8 jit_solution(2821907796561346886)
XLA Ops:
  3.9 1.3 collective-permute-start.3
  5.2 1.3 collective-permute-start.4
  6.5 1.3 collective-permute-start.5
  9.3 1.6 copy-done.4
  10.9 2.6 %shard_map.91 = f32[4,32,256]{2,1,0:T(8,128)S(1)} custom-call(f32[136,256]{1,0:T(8,128)S(1)} %pad.32.filt_ref, bf16[127,32,256]{2,1,0:T(8,128)(2,1)S(1)} %bitcast.497), custom_call_target="tpu_custom_call" | custom-call | flops 8323072 | bytes 2080768 | tf_op jit(solution)/shard_map/pallas_call | solution.py:60
  13.8 1.3 collective-permute-done.6
  16.8 52.9 %conditional.2 = (bf16[64,512]{1,0:T(8,128)(2,1)S(1)}, bf16[16,512,256]{2,1,0:T(8,128)(2,1)}, bf16[16,512,256]{2,1,0:T(8,128)(2,1)}) conditional(s32[]{:T(128)} %clamp.3, (bf16[64,512]{1,0:T(8,128)(2,1)S(1)}, f32[512]{0:T(512)S(1)}, s32[]{:T(128)}, bf16[16,512,256]{2,1,0:T(8,128)(2,1)}, bf16[16,512,256]{2,1,0:T(8,128)(2,1)}, ...), branch_computations={%region_0.3_spmd, %region_3.4_spmd, %region_4.5_spmd} | conditional | flops 542638144 | bytes 88304856 | solution.py:268
  17.9 8.1 %all-to-all-start.2 = ((bf16[16,64,512]{2,1,0:T(8,128)(2,1)}), bf16[16,64,512]{2,1,0:T(8,128)(2,1)S(1)}, u32[]{:S(2)}, u32[]{:S(2)}) async-start(bf16[16,64,512]{2,1,0:T(8,128)(2,1)} %broadcast_in_dim.7), calls=%async_computation.2 | async-start | bytes 2097152 | tf_op jit(solution)/shard_map/cond/branch_0_fun/all_to_all | solution.py:26
  26.1 2.4 %branch_0_fun.5 = bf16[16,512,256]{2,1,0:T(8,128)(2,1)S(1)} custom-call(s32[1]{0:T(128)} %bitcast.3.core_ref, bf16[16,512,256]{2,1,0:T(8,128)(2,1)} %get-tuple-element.65.refs_0_, bf16[16,512,256]{2,1,0:T(8,128)(2,1)} %get-tuple-element.66.refs_1_), custom_call_target="tpu_custom_call" | custom-call | tf_op jit(solution)/shard_map/cond/branch_0_fun/pallas_call | solution.py:111
  28.5 2.0 copy-done.3
  30.5 2.2 %branch_0_fun.4 = bf16[16,512,256]{2,1,0:T(8,128)(2,1)S(1)} custom-call(s32[1]{0:T(128)} %bitcast.core_ref, bf16[16,512,256]{2,1,0:T(8,128)(2,1)S(1)} %copy-done.5, bf16[16,512,256]{2,1,0:T(8,128)(2,1)} %get-tuple-element.66.refs_1_), custom_call_target="tpu_custom_call" | custom-call | tf_op jit(solution)/shard_map/cond/branch_0_fun/pallas_call | solution.py:111
  32.7 2.0 copy-done.1
  34.7 8.9 %all-to-all-done.2 = bf16[16,64,512]{2,1,0:T(8,128)(2,1)S(1)} async-done(((bf16[16,64,512]{2,1,0:T(8,128)(2,1)}), bf16[16,64,512]{2,1,0:T(8,128)(2,1)S(1)}, u32[]{:S(2)}, u32[]{:S(2)}) %all-to-all-start.2) | async-done | bytes 1048608 | tf_op jit(solution)/shard_map/cond/branch_0_fun/all_to_all | solution.py:26
  43.9 3.2 %fusion.5 = f32[64,256]{1,0:T(8,128)S(1)} fusion(bf16[16,512,256]{2,1,0:T(8,128)(2,1)} %copy-done.3, bf16[16,64,512]{2,1,0:T(8,128)(2,1)S(1)} %all-to-all-done.2, f32[16,512]{1,0:T(8,128)S(1)} %mul.241, f32[64]{0:T(128)S(1)} %add_rsqrt_fusion), kind=kOutput, calls=%fused_computation.10 | convolution fusion | flops 270565376 | bytes 5341440 | tf_op jit(solution)/shard_map/cond/branch_0_fun/trk,tkc->rc/dot_general | solution.py:257
  47.2 2.4 %fusion.3 = bf16[16,64,512]{2,1,0:T(8,128)(2,1)} fusion(bf16[16,512,256]{2,1,0:T(8,128)(2,1)S(1)} %copy-done.2, bf16[64,256,1]{1,0,2:T(8,128)(2,1)S(1)} %bitcast.504), kind=kOutput, calls=%fused_computation.7 | convolution fusion | flops 268959744 | bytes 5275648 | tf_op jit(solution)/shard_map/cond/branch_0_fun/rc,tkc->trk/dot_general | solution.py:249
  49.6 3.7 %all-to-all-start.3 = ((bf16[16,64,512]{2,1,0:T(8,128)(2,1)}), bf16[16,64,512]{2,1,0:T(8,128)(2,1)S(1)}, u32[]{:S(2)}, u32[]{:S(2)}) async-start(bf16[16,64,512]{2,1,0:T(8,128)(2,1)} %fusion.3), calls=%async_computation.3 | async-start | bytes 2097152 | tf_op jit(solution)/shard_map/cond/branch_0_fun/all_to_all | solution.py:26
  53.3 16.2 %all-to-all-done.3 = bf16[16,64,512]{2,1,0:T(8,128)(2,1)S(1)} async-done(((bf16[16,64,512]{2,1,0:T(8,128)(2,1)}), bf16[16,64,512]{2,1,0:T(8,128)(2,1)S(1)}, u32[]{:S(2)}, u32[]{:S(2)}) %all-to-all-start.3) | async-done | bytes 1048608 | tf_op jit(solution)/shard_map/cond/branch_0_fun/all_to_all | solution.py:26
  69.7 1.3 collective-permute-start.10
  71.1 1.8 collective-permute-done.10
  73.7 3.0 %fusion.79 = bf16[16,64,256]{2,1,0:T(8,128)(2,1)S(1)} fusion(bf16[16,512,256]{2,1,0:T(8,128)(2,1)} %get-tuple-element.111, bf16[64,512]{1,0:T(8,128)(2,1)S(1)} %collective-permute-done.11, f32[512]{0:T(512)S(1)} %dynamic_slice.34), kind=kOutput, calls=%fused_computation.126 | convolution fusion | flops 268795904 | bytes 4786176 | tf_op jit(solution)/shard_map/rk,tkc->trc/dot_general | solution.py:242
  77.7 3.6 %all-to-all-start.6 = ((bf16[16,72,256]{2,1,0:T(8,128)(2,1)}), bf16[16,72,256]{2,1,0:T(8,128)(2,1)S(1)}, u32[]{:S(2)}, u32[]{:S(2)}) async-start(bf16[16,72,256]{2,1,0:T(8,128)(2,1)} %pad_maximum_fusion.1), calls=%async_computation.6 | async-start | bytes 1179648 | tf_op jit(solution)/shard_map/all_to_all | solution.py:26
  81.3 10.4 %all-to-all-done.6 = bf16[16,72,256]{2,1,0:T(8,128)(2,1)S(1)} async-done(((bf16[16,72,256]{2,1,0:T(8,128)(2,1)}), bf16[16,72,256]{2,1,0:T(8,128)(2,1)S(1)}, u32[]{:S(2)}, u32[]{:S(2)}) %all-to-all-start.6) | async-done | bytes 589856 | tf_op jit(solution)/shard_map/all_to_all | solution.py:26
  92.0 13.4 %all_to_all.52 = bf16[16,64,256]{2,1,0:T(8,128)(2,1)S(1)} all-to-all(bf16[16,64,256]{2,1,0:T(8,128)(2,1)S(1)} %broadcast_in_dim.32), channel_id=1, replica_groups=mesh['section'=8,'tensor'=16] {'tensor'}, dimensions={0} | all-to-all | bytes 1048576 | tf_op jit(solution)/shard_map/all_to_all | solution.py:26
  105.5 3.6 %fusion.85 = bf16[64,512]{1,0:T(8,128)(2,1)S(1)} fusion(bf16[16,64,256]{2,1,0:T(8,128)(2,1)S(1)} %all_to_all.52, bf16[16,512,256]{2,1,0:T(8,128)(2,1)} %get-tuple-element.112, bf16[64,512]{1,0:T(8,128)(2,1)S(1)} %collective-permute-done.11, f32[512]{0:T(512)S(1)} %dynamic-slice_select_fusion), kind=kOutput, calls=%fused_computation.136 | convolution fusion | flops 268566528 | bytes 4851712 | tf_op jit(solution)/shard_map/trc,tkc->rk/dot_general | solution.py:265
  110.8 13.5 %all_to_all.53 = bf16[16,72,256]{2,1,0:T(8,128)(2,1)S(1)} all-to-all(bf16[16,72,256]{2,1,0:T(8,128)(2,1)S(1)} %pad_maximum_fusion.2), channel_id=1, replica_groups=mesh['section'=8,'tensor'=16] {'tensor'}, dimensions={0} | all-to-all | bytes 1179648 | tf_op jit(solution)/shard_map/all_to_all | solution.py:26
  125.4 3.6 %all-to-all-start.9 = ((bf16[16,64,256]{2,1,0:T(8,128)(2,1)}), bf16[16,64,256]{2,1,0:T(8,128)(2,1)S(1)}, u32[]{:S(2)}, u32[]{:S(2)}) async-start(bf16[16,64,256]{2,1,0:T(8,128)(2,1)} %broadcast_in_dim.34), calls=%async_computation.9 | async-start | bytes 1048576 | tf_op jit(solution)/shard_map/all_to_all | solution.py:26
  130.6 8.5 %all-to-all-done.9 = bf16[16,64,256]{2,1,0:T(8,128)(2,1)S(1)} async-done(((bf16[16,64,256]{2,1,0:T(8,128)(2,1)}), bf16[16,64,256]{2,1,0:T(8,128)(2,1)S(1)}, u32[]{:S(2)}, u32[]{:S(2)}) %all-to-all-start.9) | async-done | bytes 524320 | tf_op jit(solution)/shard_map/all_to_all | solution.py:26
  139.1 3.6 %fusion.86 = bf16[64,512]{1,0:T(8,128)(2,1)S(1)} fusion(bf16[16,64,256]{2,1,0:T(8,128)(2,1)S(1)} %all-to-all-done.9, bf16[16,512,256]{2,1,0:T(8,128)(2,1)} %get-tuple-element.112, bf16[64,512]{1,0:T(8,128)(2,1)S(1)} %collective-permute-done.12, f32[512]{0:T(512)S(1)} %dynamic-slice_select_fusion), kind=kOutput, calls=%fused_computation.137 | convolution fusion | flops 268566528 | bytes 4851712 | tf_op jit(solution)/shard_map/trc,tkc->rk/dot_general | solution.py:265
  142.7 1.3 collective-permute-start.13
  146.2 49.3 %collective-permute-done.13 = bf16[64,512]{1,0:T(8,128)(2,1)S(1)} collective-permute-done((bf16[64,512]{1,0:T(8,128)(2,1)S(1)}, bf16[64,512]{1,0:T(8,128)(2,1)S(1)}, u32[]{:S(2)}, u32[]{:S(2)}) %collective-permute-start.13) | collective-permute-done | bytes 65568 | tf_op jit(solution)/shard_map/ppermute | solution.py:22
  195.9 11.8 %all_to_all.54 = bf16[16,72,128]{2,1,0:T(8,128)(2,1)S(1)} all-to-all(bf16[16,72,128]{2,1,0:T(8,128)(2,1)S(1)} %broadcast_in_dim.36), channel_id=1, replica_groups=mesh['section'=8,'tensor'=16] {'tensor'}, dimensions={0} | all-to-all | bytes 589824 | tf_op jit(solution)/shard_map/all_to_all | solution.py:26
  208.0 1.2 collective-permute-done.17
  (115 shorter events, 18.3 us)
Async XLA Ops:
  0.0 1.3 copy-start
  1.5 1.3 collective-permute-start.2
  3.0 13.8 %collective-permute-start.7 = (bf16[16,512,256]{2,1,0:T(8,128)(2,1)}, bf16[16,512,256]{2,1,0:T(8,128)(2,1)}, u32[]{:S(2)}, u32[]{:S(2)}) collective-permute-start(bf16[16,512,256]{2,1,0:T(8,128)(2,1)} %bitcast.500), channel_id=1, source_target_pairs={{0,16},{16,0},{32,48},{48,32},{64,80},{80,64},{96,112},{112,96},{1... | collective-permute-start | bytes 12582920 | tf_op jit(solution)/shard_map/ppermute | solution.py:17
  3.9 12.8 %collective-permute-start.3 = (bf16[64,512]{1,0:T(8,128)(2,1)S(1)}, bf16[64,512]{1,0:T(8,128)(2,1)S(1)}, u32[]{:S(2)}, u32[]{:S(2)}) collective-permute-start(bf16[64,512]{1,0:T(8,128)(2,1)S(1)} %fusion.87), channel_id=1, source_target_pairs={{32,0},{48,16},{33,1},{49,17},{34,2},{50,18},{35,3},{51,19},{36,4}... | collective-permute-start | bytes 196616 | tf_op jit(solution)/shard_map/ppermute | solution.py:22
  5.2 11.5 %collective-permute-start.4 = (bf16[64,512]{1,0:T(8,128)(2,1)S(1)}, bf16[64,512]{1,0:T(8,128)(2,1)S(1)}, u32[]{:S(2)}, u32[]{:S(2)}) collective-permute-start(bf16[64,512]{1,0:T(8,128)(2,1)S(1)} %fusion.87), channel_id=1, source_target_pairs={{64,0},{80,16},{65,1},{81,17},{66,2},{82,18},{67,3},{83,19},{68,4}... | collective-permute-start | bytes 196616 | tf_op jit(solution)/shard_map/ppermute | solution.py:22
  6.5 10.2 %collective-permute-start.5 = (bf16[64,512]{1,0:T(8,128)(2,1)S(1)}, bf16[64,512]{1,0:T(8,128)(2,1)S(1)}, u32[]{:S(2)}, u32[]{:S(2)}) collective-permute-start(bf16[64,512]{1,0:T(8,128)(2,1)S(1)} %fusion.87), channel_id=1, source_target_pairs={{96,0},{112,16},{97,1},{113,17},{98,2},{114,18},{99,3},{115,19},{1... | collective-permute-start | bytes 196616 | tf_op jit(solution)/shard_map/ppermute | solution.py:22
  8.8 4.7 %collective-permute-start.9 = (f32[4,256]{1,0:T(4,128)S(1)}, f32[4,256]{1,0:T(4,128)S(1)}, u32[]{:S(2)}, u32[]{:S(2)}) collective-permute-start(f32[4,256]{1,0:T(4,128)S(1)} %slice.571), channel_id=1, source_target_pairs={{0,16},{16,0},{32,48},{48,32},{64,80},{80,64},{96,112},{112,96},{1... | collective-permute-start | bytes 12296 | tf_op jit(solution)/shard_map/ppermute | solution.py:17
  9.3 1.6 copy-start.4
  13.5 1.5 collective-permute-start.6
  15.0 1.7 collective-permute-start.8
  17.9 25.6 %all-to-all-start.2 = ((bf16[16,64,512]{2,1,0:T(8,128)(2,1)}), bf16[16,64,512]{2,1,0:T(8,128)(2,1)S(1)}, u32[]{:S(2)}, u32[]{:S(2)}) async-start(bf16[16,64,512]{2,1,0:T(8,128)(2,1)} %broadcast_in_dim.7), calls=%async_computation.2 | async-start | bytes 2097152 | tf_op jit(solution)/shard_map/cond/branch_0_fun/all_to_all | solution.py:26
  26.1 4.4 %copy-start.5 = (bf16[16,512,256]{2,1,0:T(8,128)(2,1)S(1)}, bf16[16,512,256]{2,1,0:T(8,128)(2,1)}, u32[]{:S(2)}) copy-start(bf16[16,512,256]{2,1,0:T(8,128)(2,1)} %get-tuple-element.65.refs_0_) | copy-start | bytes 12582916 | tf_op jit(solution)/shard_map/cond
  28.5 2.0 copy-start.3
  32.7 2.0 copy-start.1
  43.6 3.7 %copy-start.2 = (bf16[16,512,256]{2,1,0:T(8,128)(2,1)S(1)}, bf16[16,512,256]{2,1,0:T(8,128)(2,1)}, u32[]{:S(2)}) copy-start(bf16[16,512,256]{2,1,0:T(8,128)(2,1)} %copy-done.1) | copy-start | bytes 12582916 | tf_op jit(solution)/shard_map/cond
  49.6 19.9 %all-to-all-start.3 = ((bf16[16,64,512]{2,1,0:T(8,128)(2,1)}), bf16[16,64,512]{2,1,0:T(8,128)(2,1)S(1)}, u32[]{:S(2)}, u32[]{:S(2)}) async-start(bf16[16,64,512]{2,1,0:T(8,128)(2,1)} %fusion.3), calls=%async_computation.3 | async-start | bytes 2097152 | tf_op jit(solution)/shard_map/cond/branch_0_fun/all_to_all | solution.py:26
  69.7 3.2 %collective-permute-start.10 = (bf16[64,512]{1,0:T(8,128)(2,1)S(1)}, bf16[64,512]{1,0:T(8,128)(2,1)S(1)}, u32[]{:S(2)}, u32[]{:S(2)}) collective-permute-start(bf16[64,512]{1,0:T(8,128)(2,1)S(1)} %get-tuple-element.106), channel_id=1, source_target_pairs={{0,32},{16,48},{1,33},{17,49},{2,34},{18,50},{3,35},{19,51},{4,36}... | collective-permute-start | bytes 196616 | tf_op jit(solution)/shard_map/ppermute | solution.py:22
  72.9 0.7 collective-permute-start.11
  77.7 14.0 %all-to-all-start.6 = ((bf16[16,72,256]{2,1,0:T(8,128)(2,1)}), bf16[16,72,256]{2,1,0:T(8,128)(2,1)S(1)}, u32[]{:S(2)}, u32[]{:S(2)}) async-start(bf16[16,72,256]{2,1,0:T(8,128)(2,1)} %pad_maximum_fusion.1), calls=%async_computation.6 | async-start | bytes 1179648 | tf_op jit(solution)/shard_map/all_to_all | solution.py:26
  91.7 18.2 %copy-start.6 = (bf16[16,512,256]{2,1,0:T(8,128)(2,1)S(1)}, bf16[16,512,256]{2,1,0:T(8,128)(2,1)}, u32[]{:S(2)}) copy-start(bf16[16,512,256]{2,1,0:T(8,128)(2,1)} %get-tuple-element.111) | copy-start | bytes 12582916
  109.1 0.7 collective-permute-start.12
  125.4 13.7 %all-to-all-start.9 = ((bf16[16,64,256]{2,1,0:T(8,128)(2,1)}), bf16[16,64,256]{2,1,0:T(8,128)(2,1)S(1)}, u32[]{:S(2)}, u32[]{:S(2)}) async-start(bf16[16,64,256]{2,1,0:T(8,128)(2,1)} %broadcast_in_dim.34), calls=%async_computation.9 | async-start | bytes 1048576 | tf_op jit(solution)/shard_map/all_to_all | solution.py:26
  130.6 14.7 %collective-permute-start.16 = (bf16[512,64]{0,1:T(8,128)(2,1)S(1)}, bf16[512,64]{0,1:T(8,128)(2,1)S(1)}, u32[]{:S(2)}, u32[]{:S(2)}) collective-permute-start(bf16[512,64]{0,1:T(8,128)(2,1)S(1)} %constant_dynamic-slice_fusion), channel_id=1, source_target_pairs={{0,16},{16,0},{32,48},{48,32},{64,80},{80,64},{96,112},{112,96},{1... | collective-permute-start | bytes 196616 | tf_op jit(solution)/shard_map/ppermute | solution.py:17
  142.7 52.8 %collective-permute-start.13 = (bf16[64,512]{1,0:T(8,128)(2,1)S(1)}, bf16[64,512]{1,0:T(8,128)(2,1)S(1)}, u32[]{:S(2)}, u32[]{:S(2)}) collective-permute-start(bf16[64,512]{1,0:T(8,128)(2,1)S(1)} %fusion.86), channel_id=1, source_target_pairs={{96,0},{112,16},{97,1},{113,17},{98,2},{114,18},{99,3},{115,19},{1... | collective-permute-start | bytes 196616 | tf_op jit(solution)/shard_map/ppermute | solution.py:22
  144.0 51.5 %collective-permute-start.14 = (bf16[64,512]{1,0:T(8,128)(2,1)S(1)}, bf16[64,512]{1,0:T(8,128)(2,1)S(1)}, u32[]{:S(2)}, u32[]{:S(2)}) collective-permute-start(bf16[64,512]{1,0:T(8,128)(2,1)S(1)} %fusion.86), channel_id=1, source_target_pairs={{96,32},{112,48},{97,33},{113,49},{98,34},{114,50},{99,35},{115,51... | collective-permute-start | bytes 196616 | tf_op jit(solution)/shard_map/ppermute | solution.py:22
  144.6 50.9 %collective-permute-start.15 = (bf16[64,512]{1,0:T(8,128)(2,1)S(1)}, bf16[64,512]{1,0:T(8,128)(2,1)S(1)}, u32[]{:S(2)}, u32[]{:S(2)}) collective-permute-start(bf16[64,512]{1,0:T(8,128)(2,1)S(1)} %fusion.86), channel_id=1, source_target_pairs={{96,64},{112,80},{97,65},{113,81},{98,66},{114,82},{99,67},{115,83... | collective-permute-start | bytes 196616 | tf_op jit(solution)/shard_map/ppermute | solution.py:22
  207.9 1.3 collective-permute-start.17

commit v5 on v4

v5 whole, which is shorter than its diff:
```python
import functools

import jax
import jax.numpy as jnp
from jax import lax
from jax.experimental import pallas as pl
from jax.experimental.pallas import tpu as pltpu
from jax.sharding import PartitionSpec as P

SHORT = 7
CORES = 2
RECUT = 2
PARTS = 4
PIECES = 4
CORE, GROUP, KIND = range(3)
EXTRA = 16


def swap_cores(block):
    devices = range(lax.axis_size("section"))
    return lax.ppermute(block, "section", [(i, i ^ 1) for i in devices])


def to_plane(block, source, target):
    route = [(CORES * source + core, CORES * target + core) for core in range(CORES)]
    return lax.ppermute(block, "section", route)


def from_plane_behind(block, distance):
    devices = lax.axis_size("section")
    route = [(i, (i + CORES * distance) % devices) for i in range(devices)]
    return lax.ppermute(block, "section", route)


def exchange(blocks):
    return lax.all_to_all(blocks, "tensor", 0, 0)


def copies(block):
    return jnp.broadcast_to(block, (lax.axis_size("tensor"),) + block.shape)


def unset(like):
    return pl.pallas_call(
        lambda out: None,
        out_shape=jax.ShapeDtypeStruct(like.shape, like.dtype),
        out_specs=pl.BlockSpec(memory_space=pl.ANY),
    )()


def on_vmem(kernel, shapes, scratch=(), cost=0):
    def call(flags, *arrays):
        return pl.pallas_call(
            kernel,
            out_shape=shapes,
            in_specs=[pl.BlockSpec(memory_space=pltpu.SMEM)]
            + [pl.BlockSpec(memory_space=pltpu.VMEM)] * len(arrays),
            out_specs=jax.tree.map(lambda _: pl.BlockSpec(memory_space=pltpu.VMEM), shapes),
            scratch_shapes=list(scratch),
            compiler_params=pltpu.CompilerParams(vmem_limit_bytes=24 << 20),
            cost_estimate=pl.CostEstimate(
                flops=cost,
                bytes_accessed=sum(a.size * a.dtype.itemsize for a in arrays),
                transcendentals=0,
            ),
        )(flags, *arrays)

    return call


def shape(dims, dtype=jnp.bfloat16):
    return jax.ShapeDtypeStruct(dims, dtype)


def terms_kernel(flags_ref, filt_ref, history_ref, kept_ref, given_ref, taps_ref):
    steps = kept_ref.shape[0]
    own = kept_ref.shape[1] - EXTRA
    taps, chan = filt_ref.shape
    length, requests, _ = history_ref.shape
    place = lax.broadcasted_iota(jnp.int32, (taps, chan), 0)
    used = (place < SHORT) | (flags_ref[KIND] == 1)
    taps_ref[0:taps] = jnp.where(used, filt_ref[...].astype(jnp.float32), 0.0)
    taps_ref[taps:] = jnp.zeros((EXTRA, chan), jnp.float32)

    def one_position(r, totals):
        row = history_ref[r].astype(jnp.float32)
        return tuple(
            total + taps_ref[pl.ds(taps - 1 + k - r, 1), :] * row for k, total in enumerate(totals)
        )

    zeros = (jnp.zeros((requests, chan), jnp.float32),) * steps
    totals = lax.fori_loop(0, length, one_position, zeros)
    first = flags_ref[CORE] == 0
    for k in range(steps):
        low, high = totals[k][:own], totals[k][own:]
        kept_ref[k, 0:own] = jnp.where(first, low, high)
        given_ref[k, 0:own] = jnp.where(first, high, low)
        lag = jnp.broadcast_to(taps_ref[k : k + 1, :], (EXTRA, chan))
        kept_ref[k, own:] = lag
        given_ref[k, own:] = lag


def cache_terms(flags, filters, history, steps):
    taps, chan = filters.shape
    length, requests, _ = history.shape
    out = shape((steps, requests // CORES + EXTRA, chan), jnp.float32)
    scratch = [pltpu.VMEM((taps + EXTRA, chan), jnp.float32)]
    cost = 2 * steps * requests * length * chan
    return on_vmem(terms_kernel, [out, out], scratch, cost)(flags, filters, history)


def gate(flags_ref, kept_ref, received_ref, a):
    steps = kept_ref.shape[0]
    own = kept_ref.shape[1] - EXTRA
    first = flags_ref[CORE] == 0

    def convolve(even, signal):
        results = []
        for k in range(steps):
            total = None
            for lag in range(k, -1, -1):
                mine, other = kept_ref[lag], received_ref[lag]
                terms = jnp.where(first, mine, other) if even else jnp.where(first, other, mine)
                if lag == k:
                    mine, other = kept_ref[k], received_ref[k]
                    base = jnp.where(first, mine, other) if even else jnp.where(first, other, mine)
                    total = base[:own]
                total = total + terms[own : own + 1] * signal[k - lag]
            results.append(total)
        return results

    a = a.astype(jnp.bfloat16).astype(jnp.float32)
    z = convolve(True, [a[k * own : (k + 1) * own] for k in range(steps)])
    z = [part.astype(jnp.bfloat16).astype(jnp.float32) for part in z]
    mixed = convolve(False, z)
    return jnp.concatenate([x * y for x, y in zip(z, mixed)], 0).astype(jnp.bfloat16)


def dot(x, y):
    return jnp.dot(x, y, preferred_element_type=jnp.float32)


def dot_turned(x, y):
    return lax.dot_general(x, y, (((1,), (1,)), ((), ())), preferred_element_type=jnp.float32)


def gain_part(flags_ref, mine_ref, other_ref, even, start, size):
    mine, other = mine_ref[:, pl.ds(start, size)], other_ref[:, pl.ds(start, size)]
    first = flags_ref[CORE] == 0
    return jnp.where(first, mine, other) if even else jnp.where(first, other, mine)


def spread_kernel(flags_ref, *refs):
    parts, (sum_ref, out_ref) = refs[:PARTS], refs[-2:]
    total = parts[0][...].astype(jnp.float32)
    for part_ref in parts[1:]:
        total = total + part_ref[...].astype(jnp.float32)
    total = total.astype(jnp.bfloat16)
    sum_ref[...] = total
    for t in range(out_ref.shape[0]):
        out_ref[t] = total


def native_kernel(
    flags_ref,
    full_ref,
    gain_ref,
    gain2_ref,
    kept_ref,
    received_ref,
    mine_ref,
    other_ref,
    out_ref,
    in_buffer,
    back_buffer,
    sems,
):
    groups, rows, part = full_ref.shape
    chan = mine_ref.shape[2]

    def moves(source_ref, buffer_ref, first):
        size = groups // PIECES
        return [
            pltpu.make_async_copy(
                source_ref.at[pl.ds(n * size, size)],
                buffer_ref.at[pl.ds(n * size, size)],
                sems.at[first + n],
            )
            for n in range(PIECES)
        ]

    for core in range(CORES):
        in_ref, back_ref = (mine_ref, other_ref) if core == 0 else (other_ref, mine_ref)

        @pl.when(flags_ref[CORE] == core)
        def _():
            ahead = moves(in_ref, in_buffer, 0)
            after = moves(back_ref, back_buffer, PIECES)
            for move in ahead:
                move.start()
            squares = jnp.zeros((rows, 1), jnp.float32)
            for t in range(groups):
                values = full_ref[t].astype(jnp.float32)
                squares = squares + jnp.sum(values * values, axis=1, keepdims=True)
            scale = lax.rsqrt(squares / (groups * part) + 1e-06)
            a = jnp.zeros((rows, chan), jnp.float32)
            for t in range(groups):
                gain = gain_part(flags_ref, gain_ref, gain2_ref, True, t * part, part)
                normed = full_ref[t].astype(jnp.float32) * scale * gain
                if t % (groups // PIECES) == 0:
                    ahead[t // (groups // PIECES)].wait()
                if t == 0:
                    for move in after:
                        move.start()
                a = a + dot(normed.astype(jnp.bfloat16), in_buffer[t])
            g = gate(flags_ref, kept_ref, received_ref, a)
            for t in range(groups):
                if t % (groups // PIECES) == 0:
                    after[t // (groups // PIECES)].wait()
                out_ref[t] = dot_turned(g, back_buffer[t]).astype(jnp.bfloat16)


def residual_kernel(flags_ref, arrived_ref, chunk_ref, gain_ref, gain2_ref, out_ref):
    groups, rows, part = arrived_ref.shape
    start = pl.multiple_of(flags_ref[GROUP] * part, part)
    gain = gain_part(flags_ref, gain_ref, gain2_ref, False, start, part)
    summed = arrived_ref[0].astype(jnp.float32)
    for t in range(1, groups):
        summed = summed + arrived_ref[t].astype(jnp.float32)
    out_ref[...] = (chunk_ref[...].astype(jnp.float32) + gain * summed).astype(jnp.bfloat16)


def in_kernel(flags_ref, chunk_ref, gain_ref, gain2_ref, cut_ref, out_ref):
    groups, part, chan = cut_ref.shape
    rows = chunk_ref.shape[0]
    start = pl.multiple_of(flags_ref[GROUP] * part, part)
    gain = gain_part(flags_ref, gain_ref, gain2_ref, True, start, part)
    values = chunk_ref[...].astype(jnp.float32)
    scaled = (values * gain).astype(jnp.bfloat16)
    column = jnp.sum(values * values, axis=1, keepdims=True)
    diagonal = lax.broadcasted_iota(jnp.int32, (rows, chan), 0) == lax.broadcasted_iota(
        jnp.int32, (rows, chan), 1
    )
    row = jnp.sum(jnp.where(diagonal, column, 0.0), axis=0, keepdims=True)
    high = row.astype(jnp.bfloat16).astype(jnp.float32)
    below = lax.broadcasted_iota(jnp.int32, (EXTRA, chan), 0)
    pair = jnp.where(below == 0, high, jnp.where(below == 1, row - high, 0.0))
    pair = pair.astype(jnp.bfloat16)
    for t in range(groups):
        out_ref[t, 0:rows] = dot(scaled, cut_ref[t]).astype(jnp.bfloat16)
        out_ref[t, rows:] = pair


def gated(flags_ref, arrived_ref, kept_ref, received_ref, width):
    groups, rows, chan = arrived_ref.shape
    rows = rows - EXTRA
    totals = arrived_ref[0].astype(jnp.float32)
    for t in range(1, groups):
        totals = totals + arrived_ref[t].astype(jnp.float32)
    row = totals[rows : rows + 1] + totals[rows + 1 : rows + 2]
    diagonal = lax.broadcasted_iota(jnp.int32, (rows, chan), 0) == lax.broadcasted_iota(
        jnp.int32, (rows, chan), 1
    )
    squares = jnp.sum(jnp.where(diagonal, row, 0.0), axis=1, keepdims=True)
    return gate(
        flags_ref, kept_ref, received_ref, totals[:rows] * lax.rsqrt(squares / width + 1e-06)
    )


def gate_kernel(flags_ref, arrived_ref, kept_ref, received_ref, out_ref, *, width):
    g = gated(flags_ref, arrived_ref, kept_ref, received_ref, width)
    for t in range(out_ref.shape[0]):
        out_ref[t] = g


def gate_out_kernel(flags_ref, arrived_ref, kept_ref, received_ref, back_ref, out_ref, *, width):
    g = gated(flags_ref, arrived_ref, kept_ref, received_ref, width)
    for t in range(out_ref.shape[0]):
        out_ref[t] = dot_turned(g, back_ref[t]).astype(jnp.bfloat16)


def out_kernel(flags_ref, whole_ref, chunk_ref, gain_ref, gain2_ref, cut_ref, out_ref):
    groups, part, chan = cut_ref.shape
    start = pl.multiple_of(flags_ref[GROUP] * part, part)
    gain = gain_part(flags_ref, gain_ref, gain2_ref, False, start, part)
    summed = dot_turned(whole_ref[0], cut_ref[0])
    for t in range(1, groups):
        summed = summed + dot_turned(whole_ref[t], cut_ref[t])
    out_ref[...] = (chunk_ref[...].astype(jnp.float32) + gain * summed).astype(jnp.bfloat16)


def stage_kernel(source_ref, out_ref, sem):
    move = pltpu.make_async_copy(source_ref, out_ref, sem)
    move.start()
    move.wait()


def stage(array):
    return pl.pallas_call(
        stage_kernel,
        out_shape=jax.ShapeDtypeStruct(array.shape, array.dtype),
        in_specs=[pl.BlockSpec(memory_space=pl.ANY)],
        out_specs=pl.BlockSpec(memory_space=pltpu.VMEM),
        scratch_shapes=[pltpu.SemaphoreType.DMA],
        compiler_params=pltpu.CompilerParams(vmem_limit_bytes=8 << 20),
    )(array)


def pick(core, arrays, plans, like):
    def kernel(core_ref, *refs):
        sources, out_ref, sems = refs[:-2], refs[-2], refs[-1]
        for c in range(CORES):

            @pl.when(core_ref[0] == c)
            def _():
                moves = [
                    pltpu.make_async_copy(
                        sources[which].at[:, pl.ds(start, size)],
                        out_ref.at[:, pl.ds(place, size)],
                        sems.at[n],
                    )
                    for n, (which, start, place, size) in enumerate(plans[c])
                ]
                for move in moves:
                    move.start()
                for move in moves:
                    move.wait()

    return pl.pallas_call(
        kernel,
        out_shape=jax.ShapeDtypeStruct(like.shape, like.dtype),
        in_specs=[pl.BlockSpec(memory_space=pltpu.SMEM)]
        + [pl.BlockSpec(memory_space=pl.ANY)] * len(arrays),
        out_specs=pl.BlockSpec(memory_space=pltpu.VMEM),
        scratch_shapes=[pltpu.SemaphoreType.DMA((max(map(len, plans)),))],
        compiler_params=pltpu.CompilerParams(vmem_limit_bytes=8 << 20),
    )(core.reshape(1), *arrays)


def even_of(core, mine, other):
    size = mine.shape[1]
    return pick(core, [mine, other], [[(0, 0, 0, size)], [(1, 0, 0, size)]], mine)


def odd_of(core, mine, other):
    return even_of(1 - core, mine, other)


def as_row_pair(column, width):
    row = jnp.pad(column.reshape(1, -1), ((0, 0), (0, width - column.shape[0])))
    high = row.astype(jnp.bfloat16)
    low = (row - high.astype(jnp.float32)).astype(jnp.bfloat16)
    return jnp.pad(jnp.concatenate([high, low], 0), ((0, EXTRA - 2), (0, 0)))


def on_device(
    token_ids,
    block_types,
    embed_table,
    proj_weights,
    norm_gains,
    conv_filters,
    conv_caches,
    final_gain,
    unembed,
):
    f32, bf16 = jnp.float32, jnp.bfloat16
    planes = lax.axis_size("section") // CORES
    section = lax.axis_index("section")
    plane, core = section // CORES, section % CORES
    groups = lax.axis_size("tensor")
    group = lax.axis_index("tensor")
    steps, requests = token_ids.shape
    own = requests // CORES
    rows = steps * own
    vocab_local, width = embed_table.shape
    part = width // groups
    chan = proj_weights.shape[2]
    cols = unembed.shape[1]

    vocab_ids = section * vocab_local + jnp.arange(vocab_local, dtype=jnp.int32)
    table_part = lax.dynamic_slice_in_dim(embed_table, group * part, part, 1)

    def find(half):
        ids = lax.dynamic_slice_in_dim(token_ids, half * own, own, 1)
        one_hot = (ids[:, :, None] == vocab_ids).astype(bf16).reshape(rows, vocab_local)
        return jnp.dot(one_hot, table_part, preferred_element_type=f32).astype(bf16)

    on_chip = find(core) + swap_cores(find(1 - core))
    flags = jnp.stack([core, group, block_types[0]]).astype(jnp.int32)
    on_chip, flags, mine, gains, filters, history, unembed = lax.optimization_barrier(
        (
            on_chip,
            flags,
            proj_weights[0].reshape(groups, part, chan),
            norm_gains,
            conv_filters[0],
            conv_caches[0].transpose(1, 0, 2),
            unembed,
        )
    )
    theirs, gains2 = swap_cores(mine), swap_cores(gains)

    arriving = [from_plane_behind(on_chip, distance) for distance in range(1, planes)]

    work = 2 * rows * width * chan
    wide = shape((groups, rows, part))
    packed_shape = shape((groups, rows + EXTRA, chan))

    def prepare_terms(filters, history):
        kept, given = cache_terms(flags, filters, history, steps)
        return kept, swap_cores(given)

    def add_exchanged(chunk, blocks):
        return on_vmem(residual_kernel, shape((rows, part)))(
            flags, exchange(blocks), chunk, gains, gains2
        )

    def project_in(chunk, cut_in):
        kernel = on_vmem(in_kernel, packed_shape, cost=work)
        return exchange(kernel(flags, chunk, gains, gains2, cut_in))

    def first_plane(on_chip, arriving, mine, theirs, filters, history):
        chunk, blocks = on_vmem(spread_kernel, [shape((rows, part)), wide])(
            flags, on_chip, *arriving
        )
        blocks, filters, history, mine, theirs = lax.optimization_barrier(
            (blocks, filters, history, mine, theirs)
        )
        full = exchange(blocks)
        kept, received = prepare_terms(filters, history)
        blocks = pl.pallas_call(
            native_kernel,
            out_shape=wide,
            in_specs=[pl.BlockSpec(memory_space=pltpu.SMEM)]
            + [pl.BlockSpec(memory_space=pltpu.VMEM)] * 5
            + [pl.BlockSpec(memory_space=pl.ANY)] * 2,
            out_specs=pl.BlockSpec(memory_space=pltpu.VMEM),
            scratch_shapes=[pltpu.VMEM(mine.shape, bf16)] * 2
            + [pltpu.SemaphoreType.DMA((2 * PIECES,))],
            compiler_params=pltpu.CompilerParams(vmem_limit_bytes=24 << 20),
        )(flags, full, gains, gains2, kept, received, mine, theirs)
        return add_exchanged(chunk, blocks), unset(mine), unset(mine), unset(kept), unset(kept)

    def second_plane(chunk, arriving, mine, theirs, filters, history):
        half = part // 2
        plans = [[(0, 0, 0, half)], [(1, half, 0, half)]]
        piece = exchange(pick(core, [mine, theirs], plans, mine[:, :half]))
        plans = [[(0, 0, 0, half), (1, 0, half, half)], [(1, 0, 0, half), (0, 0, half, half)]]
        cut_in = pick(core, [piece, swap_cores(piece)], plans, mine)
        return chunk, cut_in, odd_of(core, mine, theirs), *prepare_terms(filters, history)

    def last_planes(chunk, arriving, mine, theirs, filters, history):
        cut = exchange(stage(mine))
        other = swap_cores(cut)
        weights = even_of(core, cut, other), odd_of(core, cut, other)
        return chunk, *weights, *prepare_terms(filters, history)

    def half_cut_layer(chunk, cut_in, weight_out, kept, received):
        arrived = project_in(chunk, cut_in)
        kernel = functools.partial(gate_out_kernel, width=width)
        kernel = on_vmem(kernel, wide, cost=work)
        return add_exchanged(chunk, kernel(flags, arrived, kept, received, weight_out))

    def cut_layer(chunk, cut_in, cut_out, kept, received):
        arrived = project_in(chunk, cut_in)
        kernel = on_vmem(functools.partial(gate_kernel, width=width), shape((groups, rows, chan)))
        whole = exchange(kernel(flags, arrived, kept, received))
        return on_vmem(out_kernel, shape((rows, part)), cost=work)(
            flags, whole, chunk, gains, gains2, cut_out
        )

    chunk, *held = lax.switch(
        jnp.minimum(plane, RECUT),
        [first_plane, second_plane, last_planes],
        on_chip,
        arriving,
        mine,
        theirs,
        filters,
        history,
    )
    chunk, unembed, final_gain = lax.optimization_barrier((chunk, unembed, final_gain))
    other_head = swap_cores(lax.dynamic_slice_in_dim(unembed, group * part, part, 0))
    my_head = lax.dynamic_slice_in_dim(unembed, group * part, part, 0)
    head = jnp.where(
        core == 0,
        jnp.concatenate([my_head, other_head], 1),
        jnp.concatenate([other_head, my_head], 1),
    )
    head_gain = lax.dynamic_slice_in_dim(final_gain, group * part, part, 0)
    chunk = to_plane(chunk, 0, 1)
    chunk, held, head, head_gain = lax.optimization_barrier((chunk, held, head, head_gain))
    chunk = lax.cond(plane == 1, half_cut_layer, lambda c, *held: c, chunk, *held)
    staged = stage(lax.optimization_barrier((chunk, held[0]))[1])
    for layer in range(RECUT, planes):
        chunk = to_plane(chunk, layer - 1, layer)
        if layer == RECUT:
            chunk, staged = lax.optimization_barrier((chunk, staged))
        first = staged if layer == RECUT else held[0]
        chunk = cut_layer(chunk, first, *held[1:])
    last = planes - 1
    shared = jnp.where(plane == last, chunk, jnp.zeros_like(chunk))
    for target in range(last):
        shared = shared + to_plane(chunk, last, target)
    shared = shared.astype(f32)
    squares = jnp.sum(shared * shared, axis=1, keepdims=True)
    scores = jnp.dot((shared * head_gain).astype(bf16), head, preferred_element_type=f32)
    packed = jnp.concatenate([scores.astype(bf16), as_row_pair(squares, CORES * cols)], 0)
    totals = jnp.sum(exchange(copies(packed)).astype(f32), axis=0)
    square = (totals[rows] + totals[rows + 1])[:rows, None]
    logits = totals[:rows] * lax.rsqrt(square / width + 1e-06)
    kept = jnp.where(core == 0, logits[:, :cols], logits[:, cols:])
    other = swap_cores(jnp.where(core == 0, logits[:, cols:], logits[:, :cols]))
    both = jnp.where(core == 0, jnp.stack([kept, other]), jnp.stack([other, kept]))
    return both.reshape(CORES, steps, own, cols).transpose(1, 0, 2, 3).reshape(steps, requests, cols)


def solution(mesh):
    placed = (
        P(),
        P("section"),
        P("section", None),
        P("section", None, "tensor"),
        P("section", None),
        P("section", None, "tensor"),
        P("section", None, None, "tensor"),
        P(),
        P(None, "section"),
    )
    return jax.shard_map(
        on_device, mesh=mesh, in_specs=placed, out_specs=P(None, None, "section"), check_vma=False
    )
```

time: 212 us -> 208 us (0.981)
  blocking collectives: 38.7 us -> 70 us
  Pallas kernels: 7.16 us -> 25.2 us
  matrix products: 17.2 us -> 0.57 us
  waiting for transfers between devices: 98.7 us -> 82.1 us
  local copies, waits for them, and re-layouts: 11.5 us -> 3.65 us
  starting transfers between devices: 29.3 us -> 23.3 us
  other arithmetic: 5.96 us -> 0.49 us
    all_to_all x3 -> x5, blocking collectives: 38.7 us -> 70 us  [exchange(): return lax.all_to_all(blocks, 'tensor', 0, 0)]
    pallas_call x3 -> x11, Pallas kernels: 7.16 us -> 25.2 us  [the longest x9 16.4 us: call(): pl.pallas_call(kernel, out_shape=shapes, in_specs=[pl.BlockSpec(memory_sp...]
    all_to_all x4 -> x2, waiting for transfers between devices: 44 us -> 27 us  [exchange(): return lax.all_to_all(blocks, 'tensor', 0, 0)]
    dot_general x6 -> x0, matrix products: 16.6 us -> none  [the longest x2 7.12 us: cut_layer(): jnp.einsum('trc,tkc->rk', whole, cut_out, preferred_element_type=f32)]
    all_to_all x4 -> x2, starting transfers between devices: 18.9 us -> 11.7 us  [exchange(): return lax.all_to_all(blocks, 'tensor', 0, 0)]
    ppermute x0 -> x3, starting transfers between devices: none -> 5.74 us  [from_plane_behind(): return lax.ppermute(block, 'section', route)]
    cond x8 -> x2, local copies, waits for them, and re-layouts: 4.02 us -> 0.01 us
    ppermute x9 -> x6, starting transfers between devices: 9.11 us -> 5.35 us  [to_plane(): return lax.ppermute(block, 'section', route)]
  transfers between devices with their start and end apart: 20 -> 17, of which waited for: 9 -> 10; matrix products, arithmetic and copies ran while one was open for 4% -> 0% of each run, Pallas kernels for 3% -> 3%
where the time goes in v5:
time: 208 us; the launch traced here: 206 us
  waiting for transfers between devices  82.1 us (39%)
  blocking collectives  70 us (34%)
  Pallas kernels  25.2 us (12%)
  starting transfers between devices  23.3 us (11%)
  local copies, waits for them, and re-layouts  3.65 us (2%)
    all_to_all x5, blocking collectives, exchange(): return lax.all_to_all(blocks, 'tensor', 0, 0)  70 us
    ppermute x6, waiting for transfers between devices, to_plane(): return lax.ppermute(block, 'section', route)  49.3 us
    all_to_all x2, waiting for transfers between devices, exchange(): return lax.all_to_all(blocks, 'tensor', 0, 0)  27 us
    pallas_call x9, Pallas kernels, call(): pl.pallas_call(kernel, out_shape=shapes, in_specs=[pl.BlockSpec(memory_sp...  16.4 us
    all_to_all x2, starting transfers between devices, exchange(): return lax.all_to_all(blocks, 'tensor', 0, 0)  11.7 us
    pallas_call x1, Pallas kernels, first_plane(): pl.pallas_call(native_kernel, out_shape=wide, in_specs=[pl.BlockSpec(memo...  6.59 us
    ppermute x3, starting transfers between devices, from_plane_behind(): return lax.ppermute(block, 'section', route)  5.74 us
    ppermute x6, starting transfers between devices, to_plane(): return lax.ppermute(block, 'section', route)  5.35 us
  transfers between devices with their start and end apart: 17, of which 10 were waited for; matrix products, arithmetic and copies ran while one was open for 0% of the time, Pallas kernels for 3%

profile of v5, /device:TPU:0, one launch (start us, length us, event | category | flops | bytes accessed | tf_op | source)
XLA Modules:
  0.0 206.3 jit_solution(3153633684036739984)
XLA Ops:
  0.0 0.9 constant_dynamic-slice_fusion.2
  3.2 1.6 collective-permute-start.6
  4.8 2.7 %collective-permute-start.7 = (bf16[64,512]{1,0:T(8,128)(2,1)S(1)}, bf16[64,512]{1,0:T(8,128)(2,1)S(1)}, u32[]{:S(2)}, u32[]{:S(2)}) collective-permute-start(bf16[64,512]{1,0:T(8,128)(2,1)S(1)} %fusion), channel_id=1, source_target_pairs={{0,64},{16,80},{32,96},{48,112},{64,0},{80,16},{96,32},{112,48},{1... | collective-permute-start | bytes 196616 | tf_op jit(solution)/shard_map/ppermute | solution.py:32
  7.5 1.4 collective-permute-start.8
  9.0 1.6 collective-permute-done.9
  11.8 54.5 %conditional.2 = (bf16[64,512]{1,0:T(8,128)(2,1)}, bf16[16,512,256]{2,1,0:T(8,128)(2,1)}, bf16[16,512,256]{2,1,0:T(8,128)(2,1)}, f32[4,32,256]{2,1,0:T(8,128)S(1)}, f32[4,32,256]{2,1,0:T(8,128)}) conditional(s32[]{:T(128)} %clamp.3, (s32[3]{0:T(128)S(1)}, bf16[64,512]{1,0:T(8,128)(2,1)S(1)}, bf16[64,512]{1,0:T(8,128)(2,1)S(1)}, ...), branch_computations={%region_0.1_spmd, %region_1.2_spmd, %region_2.3_spmd} | conditional | flops 8323073 | bytes 36552892 | solution.py:473
  11.8 1.7 branch_0_fun.8
  13.5 8.0 %all-to-all-start = ((bf16[16,64,512]{2,1,0:T(8,128)(2,1)}), bf16[16,64,512]{2,1,0:T(8,128)(2,1)S(1)}, u32[]{:S(2)}, u32[]{:S(2)}) async-start(bf16[16,64,512]{2,1,0:T(8,128)(2,1)} %get-tuple-element.83), calls=%async_computation | async-start | bytes 2097152 | tf_op jit(solution)/shard_map/cond/branch_0_fun/all_to_all | solution.py:36
  21.5 4.7 %branch_0_fun.9 = (f32[4,32,256]{2,1,0:T(8,128)S(1)}, f32[4,32,256]{2,1,0:T(8,128)S(1)}) custom-call(s32[3]{0:T(128)S(1)} %get-tuple-element.73.flags_ref, bf16[128,256]{1,0:T(8,128)(2,1)} %get-tuple-element.86.filt_ref, bf16[127,32,256]{2,1,0:T(8,128)(2,1)} %get-tuple-element.87.history_ref), custom_call_target="tpu_custom_call" | custom-call | flops 8323072 | bytes 2146304 | tf_op jit(solution)/shard_map/cond/branch_0_fun/pallas_call | solution.py:53
  26.3 1.3 collective-permute-done.received_ref
  27.6 10.5 %all-to-all-done.full_ref = bf16[16,64,512]{2,1,0:T(8,128)(2,1)S(1)} async-done(((bf16[16,64,512]{2,1,0:T(8,128)(2,1)}), bf16[16,64,512]{2,1,0:T(8,128)(2,1)S(1)}, u32[]{:S(2)}, u32[]{:S(2)}) %all-to-all-start) | async-done | bytes 1048608 | tf_op jit(solution)/shard_map/cond/branch_0_fun/all_to_all | solution.py:36
  38.1 6.6 %branch_0_fun.10 = bf16[16,64,512]{2,1,0:T(8,128)(2,1)} custom-call(s32[3]{0:T(128)S(1)} %get-tuple-element.73.flags_ref, bf16[16,64,512]{2,1,0:T(8,128)(2,1)S(1)} %all-to-all-done.full_ref, f32[1,8192]{1,0:T(1,128)S(1)} %copy-done.7, f32[1,8192]{1,0:T(1,128)S(1)} %get-tuple-element.85.gain2_ref, f32[4,32,256]{2,1,0:T(8,128)S(1)} %get-tuple-element.88.kept_ref, ...), custom_call_target="tpu_custom_call" | custom-call | tf_op jit(solution)/shard_map/cond/branch_0_fun/pallas_call | solution.py:432
  44.7 3.7 %all-to-all-start.1 = ((bf16[16,64,512]{2,1,0:T(8,128)(2,1)}), bf16[16,64,512]{2,1,0:T(8,128)(2,1)S(1)}, u32[]{:S(2)}, u32[]{:S(2)}) async-start(bf16[16,64,512]{2,1,0:T(8,128)(2,1)} %branch_0_fun.10), calls=%async_computation.1 | async-start | bytes 2097152 | tf_op jit(solution)/shard_map/cond/branch_0_fun/all_to_all | solution.py:36
  48.4 16.6 %all-to-all-done.1.arrived_ref = bf16[16,64,512]{2,1,0:T(8,128)(2,1)S(1)} async-done(((bf16[16,64,512]{2,1,0:T(8,128)(2,1)}), bf16[16,64,512]{2,1,0:T(8,128)(2,1)S(1)}, u32[]{:S(2)}, u32[]{:S(2)}) %all-to-all-start.1) | async-done | bytes 1048608 | tf_op jit(solution)/shard_map/cond/branch_0_fun/all_to_all | solution.py:36
  65.0 1.3 branch_0_fun.11
  67.2 1.3 collective-permute-start.11
  69.3 1.8 collective-permute-done.11
  71.9 2.2 %shard_map.91.cut_ref = bf16[16,512,256]{2,1,0:T(8,128)(2,1)S(1)} custom-call(bf16[16,512,256]{2,1,0:T(8,128)(2,1)} %get-tuple-element.163.source_ref.cut_ref), custom_call_target="tpu_custom_call" | custom-call | tf_op jit(solution)/shard_map/pallas_call | solution.py:299
  74.1 1.4 shard_map.92
  75.5 16.2 %all_to_all.53.arrived_ref = bf16[16,80,256]{2,1,0:T(8,128)(2,1)S(1)} all-to-all(bf16[16,80,256]{2,1,0:T(8,128)(2,1)S(1)} %shard_map.92), channel_id=1, replica_groups=mesh['section'=8,'tensor'=16] {'tensor'}, dimensions={0} | all-to-all | bytes 1310720 | tf_op jit(solution)/shard_map/all_to_all | solution.py:36
  91.7 1.1 shard_map.93
  92.7 14.1 %all_to_all.54.whole_ref = bf16[16,64,256]{2,1,0:T(8,128)(2,1)S(1)} all-to-all(bf16[16,64,256]{2,1,0:T(8,128)(2,1)S(1)} %shard_map.93), channel_id=1, replica_groups=mesh['section'=8,'tensor'=16] {'tensor'}, dimensions={0} | all-to-all | bytes 1048576 | tf_op jit(solution)/shard_map/all_to_all | solution.py:36
  106.9 1.9 shard_map.94
  109.5 1.4 shard_map.95
  110.9 14.5 %all_to_all.55.arrived_ref = bf16[16,80,256]{2,1,0:T(8,128)(2,1)S(1)} all-to-all(bf16[16,80,256]{2,1,0:T(8,128)(2,1)S(1)} %shard_map.95), channel_id=1, replica_groups=mesh['section'=8,'tensor'=16] {'tensor'}, dimensions={0} | all-to-all | bytes 1310720 | tf_op jit(solution)/shard_map/all_to_all | solution.py:36
  125.4 1.1 shard_map.96
  126.5 13.2 %all_to_all.56.whole_ref = bf16[16,64,256]{2,1,0:T(8,128)(2,1)S(1)} all-to-all(bf16[16,64,256]{2,1,0:T(8,128)(2,1)S(1)} %shard_map.96), channel_id=1, replica_groups=mesh['section'=8,'tensor'=16] {'tensor'}, dimensions={0} | all-to-all | bytes 1048576 | tf_op jit(solution)/shard_map/all_to_all | solution.py:36
  139.7 1.9 shard_map.97
  141.6 1.3 collective-permute-start.15
  144.3 47.5 %collective-permute-done.15 = bf16[64,512]{1,0:T(8,128)(2,1)S(1)} collective-permute-done((bf16[64,512]{1,0:T(8,128)(2,1)S(1)}, bf16[64,512]{1,0:T(8,128)(2,1)S(1)}, u32[]{:S(2)}, u32[]{:S(2)}) %collective-permute-start.15) | collective-permute-done | bytes 65568 | tf_op jit(solution)/shard_map/ppermute | solution.py:26
  192.2 12.0 %all_to_all.57 = bf16[16,80,128]{2,1,0:T(8,128)(2,1)S(1)} all-to-all(bf16[16,80,128]{2,1,0:T(8,128)(2,1)S(1)} %broadcast_in_dim.5), channel_id=1, replica_groups=mesh['section'=8,'tensor'=16] {'tensor'}, dimensions={0} | all-to-all | bytes 655360 | tf_op jit(solution)/shard_map/all_to_all | solution.py:36
  204.5 1.2 collective-permute-done.18
  (58 shorter events, 8.8 us)
Async XLA Ops:
  0.0 1.3 copy-start
  1.5 1.3 collective-permute-start.5
  3.0 7.6 %collective-permute-start.9 = (bf16[16,512,256]{2,1,0:T(8,128)(2,1)}, bf16[16,512,256]{2,1,0:T(8,128)(2,1)}, u32[]{:S(2)}, u32[]{:S(2)}) collective-permute-start(bf16[16,512,256]{2,1,0:T(8,128)(2,1)} %bitcast.20), channel_id=1, source_target_pairs={{0,16},{16,0},{32,48},{48,32},{64,80},{80,64},{96,112},{112,96},{1... | collective-permute-start | bytes 12582920 | tf_op jit(solution)/shard_map/ppermute | solution.py:21
  3.2 7.3 %collective-permute-start.6 = (bf16[64,512]{1,0:T(8,128)(2,1)S(1)}, bf16[64,512]{1,0:T(8,128)(2,1)S(1)}, u32[]{:S(2)}, u32[]{:S(2)}) collective-permute-start(bf16[64,512]{1,0:T(8,128)(2,1)S(1)} %fusion), channel_id=1, source_target_pairs={{0,32},{16,48},{32,64},{48,80},{64,96},{80,112},{96,0},{112,16},{1... | collective-permute-start | bytes 196616 | tf_op jit(solution)/shard_map/ppermute | solution.py:32
  4.8 6.5 %collective-permute-start.7 = (bf16[64,512]{1,0:T(8,128)(2,1)S(1)}, bf16[64,512]{1,0:T(8,128)(2,1)S(1)}, u32[]{:S(2)}, u32[]{:S(2)}) collective-permute-start(bf16[64,512]{1,0:T(8,128)(2,1)S(1)} %fusion), channel_id=1, source_target_pairs={{0,64},{16,80},{32,96},{48,112},{64,0},{80,16},{96,32},{112,48},{1... | collective-permute-start | bytes 196616 | tf_op jit(solution)/shard_map/ppermute | solution.py:32
  7.5 4.3 %collective-permute-start.8 = (bf16[64,512]{1,0:T(8,128)(2,1)S(1)}, bf16[64,512]{1,0:T(8,128)(2,1)S(1)}, u32[]{:S(2)}, u32[]{:S(2)}) collective-permute-start(bf16[64,512]{1,0:T(8,128)(2,1)S(1)} %fusion), channel_id=1, source_target_pairs={{0,96},{16,112},{32,0},{48,16},{64,32},{80,48},{96,64},{112,80},{1... | collective-permute-start | bytes 196616 | tf_op jit(solution)/shard_map/ppermute | solution.py:32
  9.0 1.6 collective-permute-start.10
  11.8 26.3 %copy-start.7 = (f32[1,8192]{1,0:T(1,128)S(1)}, f32[1,8192]{1,0:T(1,128)}, u32[]{:S(2)}) copy-start(f32[1,8192]{1,0:T(1,128)} %get-tuple-element.84.gain_ref) | copy-start | bytes 98308 | tf_op jit(solution)/shard_map/cond
  13.5 24.6 %all-to-all-start = ((bf16[16,64,512]{2,1,0:T(8,128)(2,1)}), bf16[16,64,512]{2,1,0:T(8,128)(2,1)S(1)}, u32[]{:S(2)}, u32[]{:S(2)}) async-start(bf16[16,64,512]{2,1,0:T(8,128)(2,1)} %get-tuple-element.83), calls=%async_computation | async-start | bytes 2097152 | tf_op jit(solution)/shard_map/cond/branch_0_fun/all_to_all | solution.py:36
  26.2 1.4 collective-permute-start
  44.7 20.3 %all-to-all-start.1 = ((bf16[16,64,512]{2,1,0:T(8,128)(2,1)}), bf16[16,64,512]{2,1,0:T(8,128)(2,1)S(1)}, u32[]{:S(2)}, u32[]{:S(2)}) async-start(bf16[16,64,512]{2,1,0:T(8,128)(2,1)} %branch_0_fun.10), calls=%async_computation.1 | async-start | bytes 2097152 | tf_op jit(solution)/shard_map/cond/branch_0_fun/all_to_all | solution.py:36
  67.2 2.1 collective-permute-start.12
  67.2 3.9 %collective-permute-start.11 = (bf16[64,512]{1,0:T(8,128)(2,1)}, bf16[64,512]{1,0:T(8,128)(2,1)S(1)}, u32[]{:S(2)}, u32[]{:S(2)}) collective-permute-start(bf16[64,512]{1,0:T(8,128)(2,1)} %get-tuple-element.151), channel_id=1, source_target_pairs={{0,32},{16,48},{1,33},{17,49},{2,34},{18,50},{3,35},{19,51},{4,36}... | collective-permute-start | bytes 196616 | tf_op jit(solution)/shard_map/ppermute | solution.py:26
  71.1 3.0 %copy-start.6 = (f32[1,8192]{1,0:T(1,128)S(1)}, f32[1,8192]{1,0:T(1,128)}, u32[]{:S(2)}) copy-start(f32[1,8192]{1,0:T(1,128)} %gain_ref.3) | copy-start | bytes 98308
  71.1 3.0 %collective-permute-start.13 = (bf16[64,512]{1,0:T(8,128)(2,1)S(1)}, bf16[64,512]{1,0:T(8,128)(2,1)S(1)}, u32[]{:S(2)}, u32[]{:S(2)}) collective-permute-start(bf16[64,512]{1,0:T(8,128)(2,1)S(1)} %get-tuple-element.189), channel_id=1, source_target_pairs={{32,64},{48,80},{33,65},{49,81},{34,66},{50,82},{35,67},{51,83},{3... | collective-permute-start | bytes 196616 | tf_op jit(solution)/shard_map/ppermute | solution.py:26
  74.1 32.8 %copy-start.2 = (bf16[16,512,256]{2,1,0:T(8,128)(2,1)S(1)}, bf16[16,512,256]{2,1,0:T(8,128)(2,1)}, u32[]{:S(2)}) copy-start(bf16[16,512,256]{2,1,0:T(8,128)(2,1)} %get-tuple-element.162.cut_ref) | copy-start | bytes 12582916
  75.5 34.0 %copy-start.1 = (bf16[16,512,256]{2,1,0:T(8,128)(2,1)S(1)}, bf16[16,512,256]{2,1,0:T(8,128)(2,1)}, u32[]{:S(2)}) copy-start(bf16[16,512,256]{2,1,0:T(8,128)(2,1)} %get-tuple-element.163.source_ref.cut_ref) | copy-start | bytes 12582916
  108.8 0.7 collective-permute-start.14
  141.6 50.2 %collective-permute-start.15 = (bf16[64,512]{1,0:T(8,128)(2,1)S(1)}, bf16[64,512]{1,0:T(8,128)(2,1)S(1)}, u32[]{:S(2)}, u32[]{:S(2)}) collective-permute-start(bf16[64,512]{1,0:T(8,128)(2,1)S(1)} %shard_map.97), channel_id=1, source_target_pairs={{96,0},{112,16},{97,1},{113,17},{98,2},{114,18},{99,3},{115,19},{1... | collective-permute-start | bytes 196616 | tf_op jit(solution)/shard_map/ppermute | solution.py:26
  142.9 48.9 %collective-permute-start.16 = (bf16[64,512]{1,0:T(8,128)(2,1)S(1)}, bf16[64,512]{1,0:T(8,128)(2,1)S(1)}, u32[]{:S(2)}, u32[]{:S(2)}) collective-permute-start(bf16[64,512]{1,0:T(8,128)(2,1)S(1)} %shard_map.97), channel_id=1, source_target_pairs={{96,32},{112,48},{97,33},{113,49},{98,34},{114,50},{99,35},{115,51... | collective-permute-start | bytes 196616 | tf_op jit(solution)/shard_map/ppermute | solution.py:26
  143.6 48.2 %collective-permute-start.17 = (bf16[64,512]{1,0:T(8,128)(2,1)S(1)}, bf16[64,512]{1,0:T(8,128)(2,1)S(1)}, u32[]{:S(2)}, u32[]{:S(2)}) collective-permute-start(bf16[64,512]{1,0:T(8,128)(2,1)S(1)} %shard_map.97), channel_id=1, source_target_pairs={{96,64},{112,80},{97,65},{113,81},{98,66},{114,82},{99,67},{115,83... | collective-permute-start | bytes 196616 | tf_op jit(solution)/shard_map/ppermute | solution.py:26
  204.4 1.3 collective-permute-start.18

commit v6 on v5

--- a/solution.py
+++ b/solution.py
@@ -251,7 +251,7 @@
         out_ref[t, rows:] = pair
 
 
-def gated(flags_ref, arrived_ref, kept_ref, received_ref, width):
+def rescaled(arrived_ref, width):
     groups, rows, chan = arrived_ref.shape
     rows = rows - EXTRA
     totals = arrived_ref[0].astype(jnp.float32)
@@ -262,21 +262,51 @@
         jnp.int32, (rows, chan), 1
     )
     squares = jnp.sum(jnp.where(diagonal, row, 0.0), axis=1, keepdims=True)
-    return gate(
-        flags_ref, kept_ref, received_ref, totals[:rows] * lax.rsqrt(squares / width + 1e-06)
-    )
+    return totals[:rows] * lax.rsqrt(squares / width + 1e-06)
 
 
 def gate_kernel(flags_ref, arrived_ref, kept_ref, received_ref, out_ref, *, width):
-    g = gated(flags_ref, arrived_ref, kept_ref, received_ref, width)
+    g = gate(flags_ref, kept_ref, received_ref, rescaled(arrived_ref, width))
     for t in range(out_ref.shape[0]):
         out_ref[t] = g
 
 
-def gate_out_kernel(flags_ref, arrived_ref, kept_ref, received_ref, back_ref, out_ref, *, width):
-    g = gated(flags_ref, arrived_ref, kept_ref, received_ref, width)
-    for t in range(out_ref.shape[0]):
-        out_ref[t] = dot_turned(g, back_ref[t]).astype(jnp.bfloat16)
+def gate_out_kernel(
+    flags_ref,
+    arrived_ref,
+    kept_ref,
+    received_ref,
+    back_ref,
+    out_ref,
+    kept,
+    received,
+    buffer,
+    sems,
+    *,
+    width,
+):
+    groups = out_ref.shape[0]
+    size = groups // PIECES
+    terms = [
+        pltpu.make_async_copy(kept_ref, kept, sems.at[PIECES]),
+        pltpu.make_async_copy(received_ref, received, sems.at[PIECES + 1]),
+    ]
+    moves = [
+        pltpu.make_async_copy(
+            back_ref.at[pl.ds(n * size, size)], buffer.at[pl.ds(n * size, size)], sems.at[n]
+        )
+        for n in range(PIECES)
+    ]
+    for move in terms + moves:
+        move.start()
+    a = rescaled(arrived_ref, width)
+    for move in terms:
+        move.wait()
+    g = gate(flags_ref, kept, received, a)
+    for t in range(groups):
+        if t % size == 0:
+            moves[t // size].wait()
+        out_ref[t] = dot_turned(g, buffer[t]).astype(jnp.bfloat16)
 
 
 def out_kernel(flags_ref, whole_ref, chunk_ref, gain_ref, gain2_ref, cut_ref, out_ref):
@@ -388,7 +418,7 @@
 
     on_chip = find(core) + swap_cores(find(1 - core))
     flags = jnp.stack([core, group, block_types[0]]).astype(jnp.int32)
-    on_chip, flags, mine, gains, filters, history, unembed = lax.optimization_barrier(
+    on_chip, flags, mine, gains, filters, history, (unembed, final_gain) = lax.optimization_barrier(
         (
             on_chip,
             flags,
@@ -396,12 +426,15 @@
             norm_gains,
             conv_filters[0],
             conv_caches[0].transpose(1, 0, 2),
-            unembed,
+            (unembed, final_gain),
         )
     )
     theirs, gains2 = swap_cores(mine), swap_cores(gains)
 
     arriving = [from_plane_behind(on_chip, distance) for distance in range(1, planes)]
+    my_head = lax.dynamic_slice_in_dim(unembed, group * part, part, 0)
+    head_gain = lax.dynamic_slice_in_dim(final_gain, group * part, part, 0)
+    arriving, my_head, head_gain = lax.optimization_barrier((arriving, my_head, head_gain))
 
     work = 2 * rows * width * chan
     wide = shape((groups, rows, part))
@@ -416,9 +449,8 @@
             flags, exchange(blocks), chunk, gains, gains2
         )
 
-    def project_in(chunk, cut_in):
-        kernel = on_vmem(in_kernel, packed_shape, cost=work)
-        return exchange(kernel(flags, chunk, gains, gains2, cut_in))
+    def pack_partials(chunk, cut_in):
+        return on_vmem(in_kernel, packed_shape, cost=work)(flags, chunk, gains, gains2, cut_in)
 
     def first_plane(on_chip, arriving, mine, theirs, filters, history):
         chunk, blocks = on_vmem(spread_kernel, [shape((rows, part)), wide])(
@@ -456,14 +488,27 @@
         weights = even_of(core, cut, other), odd_of(core, cut, other)
         return chunk, *weights, *prepare_terms(filters, history)
 
-    def half_cut_layer(chunk, cut_in, weight_out, kept, received):
-        arrived = project_in(chunk, cut_in)
-        kernel = functools.partial(gate_out_kernel, width=width)
-        kernel = on_vmem(kernel, wide, cost=work)
-        return add_exchanged(chunk, kernel(flags, arrived, kept, received, weight_out))
+    def half_cut_layer(chunk, packed, weight_out, kept, received):
+        arrived = exchange(packed)
+        blocks = pl.pallas_call(
+            functools.partial(gate_out_kernel, width=width),
+            out_shape=wide,
+            in_specs=[pl.BlockSpec(memory_space=pltpu.SMEM)]
+            + [pl.BlockSpec(memory_space=pltpu.VMEM)]
+            + [pl.BlockSpec(memory_space=pl.ANY)] * 3,
+            out_specs=pl.BlockSpec(memory_space=pltpu.VMEM),
+            scratch_shapes=[
+                pltpu.VMEM(kept.shape, f32),
+                pltpu.VMEM(kept.shape, f32),
+                pltpu.VMEM(weight_out.shape, bf16),
+                pltpu.SemaphoreType.DMA((PIECES + 2,)),
+            ],
+            compiler_params=pltpu.CompilerParams(vmem_limit_bytes=24 << 20),
+        )(flags, arrived, kept, received, weight_out)
+        return add_exchanged(chunk, blocks)
 
     def cut_layer(chunk, cut_in, cut_out, kept, received):
-        arrived = project_in(chunk, cut_in)
+        arrived = exchange(pack_partials(chunk, cut_in))
         kernel = on_vmem(functools.partial(gate_kernel, width=width), shape((groups, rows, chan)))
         whole = exchange(kernel(flags, arrived, kept, received))
         return on_vmem(out_kernel, shape((rows, part)), cost=work)(
@@ -480,18 +525,13 @@
         filters,
         history,
     )
-    chunk, unembed, final_gain = lax.optimization_barrier((chunk, unembed, final_gain))
-    other_head = swap_cores(lax.dynamic_slice_in_dim(unembed, group * part, part, 0))
-    my_head = lax.dynamic_slice_in_dim(unembed, group * part, part, 0)
-    head = jnp.where(
-        core == 0,
-        jnp.concatenate([my_head, other_head], 1),
-        jnp.concatenate([other_head, my_head], 1),
-    )
-    head_gain = lax.dynamic_slice_in_dim(final_gain, group * part, part, 0)
+    staged = stage(lax.optimization_barrier((chunk, held[0]))[1])
     chunk = to_plane(chunk, 0, 1)
-    chunk, held, head, head_gain = lax.optimization_barrier((chunk, held, head, head_gain))
-    chunk = lax.cond(plane == 1, half_cut_layer, lambda c, *held: c, chunk, *held)
+    chunk, staged, held = lax.optimization_barrier((chunk, staged, held))
+    packed = pack_partials(chunk, staged)
+    chunk = lax.cond(
+        plane == 1, half_cut_layer, lambda c, packed, *held: c, chunk, packed, *held[1:]
+    )
     staged = stage(lax.optimization_barrier((chunk, held[0]))[1])
     for layer in range(RECUT, planes):
         chunk = to_plane(chunk, layer - 1, layer)
@@ -499,10 +539,17 @@
             chunk, staged = lax.optimization_barrier((chunk, staged))
         first = staged if layer == RECUT else held[0]
         chunk = cut_layer(chunk, first, *held[1:])
+
     last = planes - 1
     shared = jnp.where(plane == last, chunk, jnp.zeros_like(chunk))
     for target in range(last):
         shared = shared + to_plane(chunk, last, target)
+    other_head = swap_cores(my_head)
+    head = jnp.where(
+        core == 0,
+        jnp.concatenate([my_head, other_head], 1),
+        jnp.concatenate([other_head, my_head], 1),
+    )
     shared = shared.astype(f32)
     squares = jnp.sum(shared * shared, axis=1, keepdims=True)
     scores = jnp.dot((shared * head_gain).astype(bf16), head, preferred_element_type=f32)

time: 208 us -> 207 us (level)
  Pallas kernels: 25.2 us -> 28.8 us
  waiting for transfers between devices: 82.1 us -> 78.6 us
  blocking collectives: 70 us -> 67.9 us
    ppermute x6, waiting for transfers between devices: 49.3 us -> 46.6 us  [to_plane(): return lax.ppermute(block, 'section', route)]
    pallas_call x1 -> x2, Pallas kernels: 2.2 us -> 4.4 us  [stage(): pl.pallas_call(stage_kernel, out_shape=jax.ShapeDtypeStruct(array.shape,...]
    all_to_all x5, blocking collectives: 70 us -> 67.9 us  [exchange(): return lax.all_to_all(blocks, 'tensor', 0, 0)]
    pallas_call x9 -> x10, Pallas kernels: 16.4 us -> 17.8 us  [call(): pl.pallas_call(kernel, out_shape=shapes, in_specs=[pl.BlockSpec(memory_sp...]
  transfers between devices with their start and end apart: 17 -> 17, of which waited for: 10 -> 8; matrix products, arithmetic and copies ran while one was open for 0% -> 1% of each run, Pallas kernels for 3% -> 4%
where the time goes in v6:
time: 207 us; the launch traced here: 205 us
  waiting for transfers between devices  78.6 us (38%)
  blocking collectives  67.9 us (33%)
  Pallas kernels  28.8 us (14%)
  starting transfers between devices  23.4 us (11%)
  local copies, waits for them, and re-layouts  4.28 us (2%)
    all_to_all x5, blocking collectives, exchange(): return lax.all_to_all(blocks, 'tensor', 0, 0)  67.9 us
    ppermute x6, waiting for transfers between devices, to_plane(): return lax.ppermute(block, 'section', route)  46.6 us
    all_to_all x2, waiting for transfers between devices, exchange(): return lax.all_to_all(blocks, 'tensor', 0, 0)  28.5 us
    pallas_call x10, Pallas kernels, call(): pl.pallas_call(kernel, out_shape=shapes, in_specs=[pl.BlockSpec(memory_sp...  17.8 us
    all_to_all x2, starting transfers between devices, exchange(): return lax.all_to_all(blocks, 'tensor', 0, 0)  11.7 us
    pallas_call x1, Pallas kernels, first_plane(): pl.pallas_call(native_kernel, out_shape=wide, in_specs=[pl.BlockSpec(memo...  6.59 us
    ppermute x3, starting transfers between devices, from_plane_behind(): return lax.ppermute(block, 'section', route)  5.74 us
    ppermute x6, starting transfers between devices, to_plane(): return lax.ppermute(block, 'section', route)  5.41 us
  transfers between devices with their start and end apart: 17, of which 8 were waited for; matrix products, arithmetic and copies ran while one was open for 1% of the time, Pallas kernels for 4%

profile of v6, /device:TPU:0, one launch (start us, length us, event | category | flops | bytes accessed | tf_op | source)
XLA Modules:
  0.0 205.1 jit_solution(12062196879839937890)
XLA Ops:
  3.2 1.6 collective-permute-start.6
  4.8 2.7 %collective-permute-start.7 = (bf16[64,512]{1,0:T(8,128)(2,1)S(1)}, bf16[64,512]{1,0:T(8,128)(2,1)S(1)}, u32[]{:S(2)}, u32[]{:S(2)}) collective-permute-start(bf16[64,512]{1,0:T(8,128)(2,1)S(1)} %fusion), channel_id=1, source_target_pairs={{0,64},{16,80},{32,96},{48,112},{64,0},{80,16},{96,32},{112,48},{1... | collective-permute-start | bytes 196616 | tf_op jit(solution)/shard_map/ppermute | solution.py:32
  7.5 1.4 collective-permute-start.8
  9.0 1.5 constant_dynamic-slice_fusion
  11.8 56.0 %conditional.2 = (bf16[64,512]{1,0:T(8,128)(2,1)}, bf16[16,512,256]{2,1,0:T(8,128)(2,1)}, bf16[16,512,256]{2,1,0:T(8,128)(2,1)}, f32[4,32,256]{2,1,0:T(8,128)S(1)}, f32[4,32,256]{2,1,0:T(8,128)}) conditional(s32[]{:T(128)} %clamp.3, (s32[3]{0:T(128)S(1)}, bf16[64,512]{1,0:T(8,128)(2,1)S(1)}, bf16[64,512]{1,0:T(8,128)(2,1)S(1)}, ...), branch_computations={%region_0.1_spmd, %region_1.2_spmd, %region_2.3_spmd} | conditional | flops 8323073 | bytes 36552892 | solution.py:518
  11.8 1.7 branch_0_fun.8
  13.5 8.0 %all-to-all-start = ((bf16[16,64,512]{2,1,0:T(8,128)(2,1)}), bf16[16,64,512]{2,1,0:T(8,128)(2,1)S(1)}, u32[]{:S(2)}, u32[]{:S(2)}) async-start(bf16[16,64,512]{2,1,0:T(8,128)(2,1)} %get-tuple-element.83), calls=%async_computation | async-start | bytes 2097152 | tf_op jit(solution)/shard_map/cond/branch_0_fun/all_to_all | solution.py:36
  21.6 4.7 %branch_0_fun.9 = (f32[4,32,256]{2,1,0:T(8,128)S(1)}, f32[4,32,256]{2,1,0:T(8,128)S(1)}) custom-call(s32[3]{0:T(128)S(1)} %get-tuple-element.73.flags_ref, bf16[128,256]{1,0:T(8,128)(2,1)} %get-tuple-element.86.filt_ref, bf16[127,32,256]{2,1,0:T(8,128)(2,1)} %get-tuple-element.87.history_ref), custom_call_target="tpu_custom_call" | custom-call | flops 8323072 | bytes 2146304 | tf_op jit(solution)/shard_map/cond/branch_0_fun/pallas_call | solution.py:53
  26.3 1.3 collective-permute-done.received_ref
  27.7 11.7 %all-to-all-done.full_ref = bf16[16,64,512]{2,1,0:T(8,128)(2,1)S(1)} async-done(((bf16[16,64,512]{2,1,0:T(8,128)(2,1)}), bf16[16,64,512]{2,1,0:T(8,128)(2,1)S(1)}, u32[]{:S(2)}, u32[]{:S(2)}) %all-to-all-start) | async-done | bytes 1048608 | tf_op jit(solution)/shard_map/cond/branch_0_fun/all_to_all | solution.py:36
  39.3 6.6 %branch_0_fun.10 = bf16[16,64,512]{2,1,0:T(8,128)(2,1)} custom-call(s32[3]{0:T(128)S(1)} %get-tuple-element.73.flags_ref, bf16[16,64,512]{2,1,0:T(8,128)(2,1)S(1)} %all-to-all-done.full_ref, f32[1,8192]{1,0:T(1,128)S(1)} %copy-done.6, f32[1,8192]{1,0:T(1,128)S(1)} %get-tuple-element.85.gain2_ref, f32[4,32,256]{2,1,0:T(8,128)S(1)} %get-tuple-element.88.kept_ref, ...), custom_call_target="tpu_custom_call" | custom-call | tf_op jit(solution)/shard_map/cond/branch_0_fun/pallas_call | solution.py:464
  45.9 3.7 %all-to-all-start.1 = ((bf16[16,64,512]{2,1,0:T(8,128)(2,1)}), bf16[16,64,512]{2,1,0:T(8,128)(2,1)S(1)}, u32[]{:S(2)}, u32[]{:S(2)}) async-start(bf16[16,64,512]{2,1,0:T(8,128)(2,1)} %branch_0_fun.10), calls=%async_computation.1 | async-start | bytes 2097152 | tf_op jit(solution)/shard_map/cond/branch_0_fun/all_to_all | solution.py:36
  49.6 16.8 %all-to-all-done.1.arrived_ref = bf16[16,64,512]{2,1,0:T(8,128)(2,1)S(1)} async-done(((bf16[16,64,512]{2,1,0:T(8,128)(2,1)}), bf16[16,64,512]{2,1,0:T(8,128)(2,1)S(1)}, u32[]{:S(2)}, u32[]{:S(2)}) %all-to-all-start.1) | async-done | bytes 1048608 | tf_op jit(solution)/shard_map/cond/branch_0_fun/all_to_all | solution.py:36
  66.5 1.3 branch_0_fun.11
  67.8 1.3 collective-permute-start.11
  69.1 2.2 %shard_map.91.cut_ref = bf16[16,512,256]{2,1,0:T(8,128)(2,1)S(1)} custom-call(bf16[16,512,256]{2,1,0:T(8,128)(2,1)} %get-tuple-element.169.source_ref.cut_ref), custom_call_target="tpu_custom_call" | custom-call | tf_op jit(solution)/shard_map/pallas_call | solution.py:329
  71.3 1.4 shard_map.92
  73.6 2.2 %shard_map.93.cut_ref = bf16[16,512,256]{2,1,0:T(8,128)(2,1)S(1)} custom-call(bf16[16,512,256]{2,1,0:T(8,128)(2,1)} %get-tuple-element.169.source_ref.cut_ref), custom_call_target="tpu_custom_call" | custom-call | tf_op jit(solution)/shard_map/pallas_call | solution.py:329
  75.8 1.4 shard_map.94
  77.2 15.5 %all_to_all.52.arrived_ref = bf16[16,80,256]{2,1,0:T(8,128)(2,1)S(1)} all-to-all(bf16[16,80,256]{2,1,0:T(8,128)(2,1)S(1)} %shard_map.94), channel_id=1, replica_groups=mesh['section'=8,'tensor'=16] {'tensor'}, dimensions={0} | all-to-all | bytes 1310720 | tf_op jit(solution)/shard_map/all_to_all | solution.py:36
  92.7 1.1 shard_map.95
  93.8 13.2 %all_to_all.53.whole_ref = bf16[16,64,256]{2,1,0:T(8,128)(2,1)S(1)} all-to-all(bf16[16,64,256]{2,1,0:T(8,128)(2,1)S(1)} %shard_map.95), channel_id=1, replica_groups=mesh['section'=8,'tensor'=16] {'tensor'}, dimensions={0} | all-to-all | bytes 1048576 | tf_op jit(solution)/shard_map/all_to_all | solution.py:36
  107.0 1.9 shard_map.96
  109.6 1.4 shard_map.97
  111.0 13.9 %all_to_all.54.arrived_ref = bf16[16,80,256]{2,1,0:T(8,128)(2,1)S(1)} all-to-all(bf16[16,80,256]{2,1,0:T(8,128)(2,1)S(1)} %shard_map.97), channel_id=1, replica_groups=mesh['section'=8,'tensor'=16] {'tensor'}, dimensions={0} | all-to-all | bytes 1310720 | tf_op jit(solution)/shard_map/all_to_all | solution.py:36
  124.9 1.1 shard_map.98
  126.0 13.3 %all_to_all.55.whole_ref = bf16[16,64,256]{2,1,0:T(8,128)(2,1)S(1)} all-to-all(bf16[16,64,256]{2,1,0:T(8,128)(2,1)S(1)} %shard_map.98), channel_id=1, replica_groups=mesh['section'=8,'tensor'=16] {'tensor'}, dimensions={0} | all-to-all | bytes 1048576 | tf_op jit(solution)/shard_map/all_to_all | solution.py:36
  139.3 1.9 shard_map.99
  141.2 1.3 collective-permute-start.14
  143.9 46.6 %collective-permute-done.14 = bf16[64,512]{1,0:T(8,128)(2,1)S(1)} collective-permute-done((bf16[64,512]{1,0:T(8,128)(2,1)S(1)}, bf16[64,512]{1,0:T(8,128)(2,1)S(1)}, u32[]{:S(2)}, u32[]{:S(2)}) %collective-permute-start.14) | collective-permute-done | bytes 65568 | tf_op jit(solution)/shard_map/ppermute | solution.py:26
  191.0 12.0 %all_to_all.56 = bf16[16,80,128]{2,1,0:T(8,128)(2,1)S(1)} all-to-all(bf16[16,80,128]{2,1,0:T(8,128)(2,1)S(1)} %broadcast_in_dim.5), channel_id=1, replica_groups=mesh['section'=8,'tensor'=16] {'tensor'}, dimensions={0} | all-to-all | bytes 655360 | tf_op jit(solution)/shard_map/all_to_all | solution.py:36
  203.2 1.2 collective-permute-done.18
  (61 shorter events, 8.3 us)
Async XLA Ops:
  0.0 1.3 copy-start
  1.5 1.3 collective-permute-start.5
  3.0 8.8 %collective-permute-start.9 = (bf16[16,512,256]{2,1,0:T(8,128)(2,1)}, bf16[16,512,256]{2,1,0:T(8,128)(2,1)}, u32[]{:S(2)}, u32[]{:S(2)}) collective-permute-start(bf16[16,512,256]{2,1,0:T(8,128)(2,1)} %bitcast.19), channel_id=1, source_target_pairs={{0,16},{16,0},{32,48},{48,32},{64,80},{80,64},{96,112},{112,96},{1... | collective-permute-start | bytes 12582920 | tf_op jit(solution)/shard_map/ppermute | solution.py:21
  3.2 8.0 %collective-permute-start.6 = (bf16[64,512]{1,0:T(8,128)(2,1)S(1)}, bf16[64,512]{1,0:T(8,128)(2,1)S(1)}, u32[]{:S(2)}, u32[]{:S(2)}) collective-permute-start(bf16[64,512]{1,0:T(8,128)(2,1)S(1)} %fusion), channel_id=1, source_target_pairs={{0,32},{16,48},{32,64},{48,80},{64,96},{80,112},{96,0},{112,16},{1... | collective-permute-start | bytes 196616 | tf_op jit(solution)/shard_map/ppermute | solution.py:32
  4.8 6.5 %collective-permute-start.7 = (bf16[64,512]{1,0:T(8,128)(2,1)S(1)}, bf16[64,512]{1,0:T(8,128)(2,1)S(1)}, u32[]{:S(2)}, u32[]{:S(2)}) collective-permute-start(bf16[64,512]{1,0:T(8,128)(2,1)S(1)} %fusion), channel_id=1, source_target_pairs={{0,64},{16,80},{32,96},{48,112},{64,0},{80,16},{96,32},{112,48},{1... | collective-permute-start | bytes 196616 | tf_op jit(solution)/shard_map/ppermute | solution.py:32
  7.5 4.3 %collective-permute-start.8 = (bf16[64,512]{1,0:T(8,128)(2,1)S(1)}, bf16[64,512]{1,0:T(8,128)(2,1)S(1)}, u32[]{:S(2)}, u32[]{:S(2)}) collective-permute-start(bf16[64,512]{1,0:T(8,128)(2,1)S(1)} %fusion), channel_id=1, source_target_pairs={{0,96},{16,112},{32,0},{48,16},{64,32},{80,48},{96,64},{112,80},{1... | collective-permute-start | bytes 196616 | tf_op jit(solution)/shard_map/ppermute | solution.py:32
  9.0 2.8 %collective-permute-start.10 = (f32[1,8192]{1,0:T(1,128)}, f32[1,8192]{1,0:T(1,128)S(1)}, u32[]{:S(2)}, u32[]{:S(2)}) collective-permute-start(f32[1,8192]{1,0:T(1,128)} %gain_ref.4), channel_id=1, source_target_pairs={{0,16},{16,0},{32,48},{48,32},{64,80},{80,64},{96,112},{112,96},{1... | collective-permute-start | bytes 98312 | tf_op jit(solution)/shard_map/ppermute | solution.py:21
  11.8 27.5 %copy-start.6 = (f32[1,8192]{1,0:T(1,128)S(1)}, f32[1,8192]{1,0:T(1,128)}, u32[]{:S(2)}) copy-start(f32[1,8192]{1,0:T(1,128)} %get-tuple-element.84.gain_ref) | copy-start | bytes 98308 | tf_op jit(solution)/shard_map/cond
  13.5 25.8 %all-to-all-start = ((bf16[16,64,512]{2,1,0:T(8,128)(2,1)}), bf16[16,64,512]{2,1,0:T(8,128)(2,1)S(1)}, u32[]{:S(2)}, u32[]{:S(2)}) async-start(bf16[16,64,512]{2,1,0:T(8,128)(2,1)} %get-tuple-element.83), calls=%async_computation | async-start | bytes 2097152 | tf_op jit(solution)/shard_map/cond/branch_0_fun/all_to_all | solution.py:36
  26.2 1.4 collective-permute-start
  45.9 20.5 %all-to-all-start.1 = ((bf16[16,64,512]{2,1,0:T(8,128)(2,1)}), bf16[16,64,512]{2,1,0:T(8,128)(2,1)S(1)}, u32[]{:S(2)}, u32[]{:S(2)}) async-start(bf16[16,64,512]{2,1,0:T(8,128)(2,1)} %branch_0_fun.10), calls=%async_computation.1 | async-start | bytes 2097152 | tf_op jit(solution)/shard_map/cond/branch_0_fun/all_to_all | solution.py:36
  67.8 3.5 %collective-permute-start.11 = (bf16[64,512]{1,0:T(8,128)(2,1)}, bf16[64,512]{1,0:T(8,128)(2,1)S(1)}, u32[]{:S(2)}, u32[]{:S(2)}) collective-permute-start(bf16[64,512]{1,0:T(8,128)(2,1)} %get-tuple-element.157), channel_id=1, source_target_pairs={{0,32},{16,48},{1,33},{17,49},{2,34},{18,50},{3,35},{19,51},{4,36}... | collective-permute-start | bytes 196616 | tf_op jit(solution)/shard_map/ppermute | solution.py:26
  69.1 2.2 %copy-start.5 = (f32[1,8192]{1,0:T(1,128)S(1)}, f32[1,8192]{1,0:T(1,128)}, u32[]{:S(2)}) copy-start(f32[1,8192]{1,0:T(1,128)} %gain_ref.4) | copy-start | bytes 98308
  72.7 3.1 %collective-permute-start.12 = (bf16[64,512]{1,0:T(8,128)(2,1)S(1)}, bf16[64,512]{1,0:T(8,128)(2,1)S(1)}, u32[]{:S(2)}, u32[]{:S(2)}) collective-permute-start(bf16[64,512]{1,0:T(8,128)(2,1)S(1)} %get-tuple-element.195), channel_id=1, source_target_pairs={{32,64},{48,80},{33,65},{49,81},{34,66},{50,82},{35,67},{51,83},{3... | collective-permute-start | bytes 196616 | tf_op jit(solution)/shard_map/ppermute | solution.py:26
  75.8 31.2 %copy-start.2 = (bf16[16,512,256]{2,1,0:T(8,128)(2,1)S(1)}, bf16[16,512,256]{2,1,0:T(8,128)(2,1)}, u32[]{:S(2)}) copy-start(bf16[16,512,256]{2,1,0:T(8,128)(2,1)} %get-tuple-element.167.cut_ref) | copy-start | bytes 12582916
  77.2 32.4 %copy-start.1 = (bf16[16,512,256]{2,1,0:T(8,128)(2,1)S(1)}, bf16[16,512,256]{2,1,0:T(8,128)(2,1)}, u32[]{:S(2)}) copy-start(bf16[16,512,256]{2,1,0:T(8,128)(2,1)} %get-tuple-element.169.source_ref.cut_ref) | copy-start | bytes 12582916
  108.9 0.7 collective-permute-start.13
  111.0 32.9 %copy-start.9 = (bf16[512,64]{0,1:T(8,128)(2,1)S(1)}, bf16[512,64]{0,1:T(8,128)(2,1)}, u32[]{:S(2)}) copy-start(bf16[512,64]{0,1:T(8,128)(2,1)} %constant_dynamic-slice_fusion) | copy-start | bytes 196612
  141.2 49.3 %collective-permute-start.14 = (bf16[64,512]{1,0:T(8,128)(2,1)S(1)}, bf16[64,512]{1,0:T(8,128)(2,1)S(1)}, u32[]{:S(2)}, u32[]{:S(2)}) collective-permute-start(bf16[64,512]{1,0:T(8,128)(2,1)S(1)} %shard_map.99), channel_id=1, source_target_pairs={{96,0},{112,16},{97,1},{113,17},{98,2},{114,18},{99,3},{115,19},{1... | collective-permute-start | bytes 196616 | tf_op jit(solution)/shard_map/ppermute | solution.py:26
  142.5 48.0 %collective-permute-start.15 = (bf16[64,512]{1,0:T(8,128)(2,1)S(1)}, bf16[64,512]{1,0:T(8,128)(2,1)S(1)}, u32[]{:S(2)}, u32[]{:S(2)}) collective-permute-start(bf16[64,512]{1,0:T(8,128)(2,1)S(1)} %shard_map.99), channel_id=1, source_target_pairs={{96,32},{112,48},{97,33},{113,49},{98,34},{114,50},{99,35},{115,51... | collective-permute-start | bytes 196616 | tf_op jit(solution)/shard_map/ppermute | solution.py:26
  143.1 47.4 %collective-permute-start.16 = (bf16[64,512]{1,0:T(8,128)(2,1)S(1)}, bf16[64,512]{1,0:T(8,128)(2,1)S(1)}, u32[]{:S(2)}, u32[]{:S(2)}) collective-permute-start(bf16[64,512]{1,0:T(8,128)(2,1)S(1)} %shard_map.99), channel_id=1, source_target_pairs={{96,64},{112,80},{97,65},{113,81},{98,66},{114,82},{99,67},{115,83... | collective-permute-start | bytes 196616 | tf_op jit(solution)/shard_map/ppermute | solution.py:26
  143.8 46.9 %collective-permute-start.17 = (bf16[512,64]{0,1:T(8,128)(2,1)S(1)}, bf16[512,64]{0,1:T(8,128)(2,1)S(1)}, u32[]{:S(2)}, u32[]{:S(2)}) collective-permute-start(bf16[512,64]{0,1:T(8,128)(2,1)S(1)} %copy-done.9), channel_id=1, source_target_pairs={{0,16},{16,0},{32,48},{48,32},{64,80},{80,64},{96,112},{112,96},{1... | collective-permute-start | bytes 196616 | tf_op jit(solution)/shard_map/ppermute | solution.py:21
  203.2 1.3 collective-permute-start.18

commit v7 on v6

--- a/solution.py
+++ b/solution.py
@@ -559,8 +559,9 @@
     logits = totals[:rows] * lax.rsqrt(square / width + 1e-06)
     kept = jnp.where(core == 0, logits[:, :cols], logits[:, cols:])
     other = swap_cores(jnp.where(core == 0, logits[:, cols:], logits[:, :cols]))
-    both = jnp.where(core == 0, jnp.stack([kept, other]), jnp.stack([other, kept]))
-    return both.reshape(CORES, steps, own, cols).transpose(1, 0, 2, 3).reshape(steps, requests, cols)
+    kept, other = kept.reshape(steps, own, cols), other.reshape(steps, own, cols)
+    first, second = jnp.where(core == 0, kept, other), jnp.where(core == 0, other, kept)
+    return jnp.concatenate([first, second], 1)
 
 
 def solution(mesh):

time: 207 us -> 207 us (level)
  no operation moved by 1% of the time
where the time goes in v7:
time: 207 us; the launch traced here: 205 us
  waiting for transfers between devices  78.6 us (38%)
  blocking collectives  67.9 us (33%)
  Pallas kernels  28.8 us (14%)
  starting transfers between devices  23.4 us (11%)
  local copies, waits for them, and re-layouts  3.65 us (2%)
    all_to_all x5, blocking collectives, exchange(): return lax.all_to_all(blocks, 'tensor', 0, 0)  67.9 us
    ppermute x6, waiting for transfers between devices, to_plane(): return lax.ppermute(block, 'section', route)  46.6 us
    all_to_all x2, waiting for transfers between devices, exchange(): return lax.all_to_all(blocks, 'tensor', 0, 0)  28.5 us
    pallas_call x10, Pallas kernels, call(): pl.pallas_call(kernel, out_shape=shapes, in_specs=[pl.BlockSpec(memory_sp...  17.8 us
    all_to_all x2, starting transfers between devices, exchange(): return lax.all_to_all(blocks, 'tensor', 0, 0)  11.7 us
    pallas_call x1, Pallas kernels, first_plane(): pl.pallas_call(native_kernel, out_shape=wide, in_specs=[pl.BlockSpec(memo...  6.59 us
    ppermute x3, starting transfers between devices, from_plane_behind(): return lax.ppermute(block, 'section', route)  5.74 us
    ppermute x6, starting transfers between devices, to_plane(): return lax.ppermute(block, 'section', route)  5.41 us
  transfers between devices with their start and end apart: 17, of which 8 were waited for; matrix products, arithmetic and copies ran while one was open for 1% of the time, Pallas kernels for 4%

profile of v7, /device:TPU:0, one launch (start us, length us, event | category | flops | bytes accessed | tf_op | source)
XLA Modules:
  0.0 205.1 jit_solution(390632471874159276)
XLA Ops:
  3.2 1.6 collective-permute-start.6
  4.8 2.7 %collective-permute-start.7 = (bf16[64,512]{1,0:T(8,128)(2,1)S(1)}, bf16[64,512]{1,0:T(8,128)(2,1)S(1)}, u32[]{:S(2)}, u32[]{:S(2)}) collective-permute-start(bf16[64,512]{1,0:T(8,128)(2,1)S(1)} %fusion), channel_id=1, source_target_pairs={{0,64},{16,80},{32,96},{48,112},{64,0},{80,16},{96,32},{112,48},{1... | collective-permute-start | bytes 196616 | tf_op jit(solution)/shard_map/ppermute | solution.py:32
  7.5 1.4 collective-permute-start.8
  9.0 1.5 constant_dynamic-slice_fusion
  11.8 56.0 %conditional.2 = (bf16[64,512]{1,0:T(8,128)(2,1)}, bf16[16,512,256]{2,1,0:T(8,128)(2,1)}, bf16[16,512,256]{2,1,0:T(8,128)(2,1)}, f32[4,32,256]{2,1,0:T(8,128)S(1)}, f32[4,32,256]{2,1,0:T(8,128)}) conditional(s32[]{:T(128)} %clamp.3, (s32[3]{0:T(128)S(1)}, bf16[64,512]{1,0:T(8,128)(2,1)S(1)}, bf16[64,512]{1,0:T(8,128)(2,1)S(1)}, ...), branch_computations={%region_0.1_spmd, %region_1.2_spmd, %region_2.3_spmd} | conditional | flops 8323073 | bytes 36552892 | solution.py:518
  11.8 1.7 branch_0_fun.8
  13.5 8.0 %all-to-all-start = ((bf16[16,64,512]{2,1,0:T(8,128)(2,1)}), bf16[16,64,512]{2,1,0:T(8,128)(2,1)S(1)}, u32[]{:S(2)}, u32[]{:S(2)}) async-start(bf16[16,64,512]{2,1,0:T(8,128)(2,1)} %get-tuple-element.83), calls=%async_computation | async-start | bytes 2097152 | tf_op jit(solution)/shard_map/cond/branch_0_fun/all_to_all | solution.py:36
  21.6 4.7 %branch_0_fun.9 = (f32[4,32,256]{2,1,0:T(8,128)S(1)}, f32[4,32,256]{2,1,0:T(8,128)S(1)}) custom-call(s32[3]{0:T(128)S(1)} %get-tuple-element.73.flags_ref, bf16[128,256]{1,0:T(8,128)(2,1)} %get-tuple-element.86.filt_ref, bf16[127,32,256]{2,1,0:T(8,128)(2,1)} %get-tuple-element.87.history_ref), custom_call_target="tpu_custom_call" | custom-call | flops 8323072 | bytes 2146304 | tf_op jit(solution)/shard_map/cond/branch_0_fun/pallas_call | solution.py:53
  26.3 1.3 collective-permute-done.received_ref
  27.7 11.7 %all-to-all-done.full_ref = bf16[16,64,512]{2,1,0:T(8,128)(2,1)S(1)} async-done(((bf16[16,64,512]{2,1,0:T(8,128)(2,1)}), bf16[16,64,512]{2,1,0:T(8,128)(2,1)S(1)}, u32[]{:S(2)}, u32[]{:S(2)}) %all-to-all-start) | async-done | bytes 1048608 | tf_op jit(solution)/shard_map/cond/branch_0_fun/all_to_all | solution.py:36
  39.3 6.6 %branch_0_fun.10 = bf16[16,64,512]{2,1,0:T(8,128)(2,1)} custom-call(s32[3]{0:T(128)S(1)} %get-tuple-element.73.flags_ref, bf16[16,64,512]{2,1,0:T(8,128)(2,1)S(1)} %all-to-all-done.full_ref, f32[1,8192]{1,0:T(1,128)S(1)} %copy-done.6, f32[1,8192]{1,0:T(1,128)S(1)} %get-tuple-element.85.gain2_ref, f32[4,32,256]{2,1,0:T(8,128)S(1)} %get-tuple-element.88.kept_ref, ...), custom_call_target="tpu_custom_call" | custom-call | tf_op jit(solution)/shard_map/cond/branch_0_fun/pallas_call | solution.py:464
  45.9 3.7 %all-to-all-start.1 = ((bf16[16,64,512]{2,1,0:T(8,128)(2,1)}), bf16[16,64,512]{2,1,0:T(8,128)(2,1)S(1)}, u32[]{:S(2)}, u32[]{:S(2)}) async-start(bf16[16,64,512]{2,1,0:T(8,128)(2,1)} %branch_0_fun.10), calls=%async_computation.1 | async-start | bytes 2097152 | tf_op jit(solution)/shard_map/cond/branch_0_fun/all_to_all | solution.py:36
  49.6 16.8 %all-to-all-done.1.arrived_ref = bf16[16,64,512]{2,1,0:T(8,128)(2,1)S(1)} async-done(((bf16[16,64,512]{2,1,0:T(8,128)(2,1)}), bf16[16,64,512]{2,1,0:T(8,128)(2,1)S(1)}, u32[]{:S(2)}, u32[]{:S(2)}) %all-to-all-start.1) | async-done | bytes 1048608 | tf_op jit(solution)/shard_map/cond/branch_0_fun/all_to_all | solution.py:36
  66.5 1.3 branch_0_fun.11
  67.8 1.3 collective-permute-start.11
  69.1 2.2 %shard_map.91.cut_ref = bf16[16,512,256]{2,1,0:T(8,128)(2,1)S(1)} custom-call(bf16[16,512,256]{2,1,0:T(8,128)(2,1)} %get-tuple-element.169.source_ref.cut_ref), custom_call_target="tpu_custom_call" | custom-call | tf_op jit(solution)/shard_map/pallas_call | solution.py:329
  71.3 1.4 shard_map.92
  73.6 2.2 %shard_map.93.cut_ref = bf16[16,512,256]{2,1,0:T(8,128)(2,1)S(1)} custom-call(bf16[16,512,256]{2,1,0:T(8,128)(2,1)} %get-tuple-element.169.source_ref.cut_ref), custom_call_target="tpu_custom_call" | custom-call | tf_op jit(solution)/shard_map/pallas_call | solution.py:329
  75.8 1.4 shard_map.94
  77.2 15.5 %all_to_all.52.arrived_ref = bf16[16,80,256]{2,1,0:T(8,128)(2,1)S(1)} all-to-all(bf16[16,80,256]{2,1,0:T(8,128)(2,1)S(1)} %shard_map.94), channel_id=1, replica_groups=mesh['section'=8,'tensor'=16] {'tensor'}, dimensions={0} | all-to-all | bytes 1310720 | tf_op jit(solution)/shard_map/all_to_all | solution.py:36
  92.7 1.1 shard_map.95
  93.8 13.2 %all_to_all.53.whole_ref = bf16[16,64,256]{2,1,0:T(8,128)(2,1)S(1)} all-to-all(bf16[16,64,256]{2,1,0:T(8,128)(2,1)S(1)} %shard_map.95), channel_id=1, replica_groups=mesh['section'=8,'tensor'=16] {'tensor'}, dimensions={0} | all-to-all | bytes 1048576 | tf_op jit(solution)/shard_map/all_to_all | solution.py:36
  107.0 1.9 shard_map.96
  109.6 1.4 shard_map.97
  111.0 13.9 %all_to_all.54.arrived_ref = bf16[16,80,256]{2,1,0:T(8,128)(2,1)S(1)} all-to-all(bf16[16,80,256]{2,1,0:T(8,128)(2,1)S(1)} %shard_map.97), channel_id=1, replica_groups=mesh['section'=8,'tensor'=16] {'tensor'}, dimensions={0} | all-to-all | bytes 1310720 | tf_op jit(solution)/shard_map/all_to_all | solution.py:36
  124.9 1.1 shard_map.98
  126.0 13.3 %all_to_all.55.whole_ref = bf16[16,64,256]{2,1,0:T(8,128)(2,1)S(1)} all-to-all(bf16[16,64,256]{2,1,0:T(8,128)(2,1)S(1)} %shard_map.98), channel_id=1, replica_groups=mesh['section'=8,'tensor'=16] {'tensor'}, dimensions={0} | all-to-all | bytes 1048576 | tf_op jit(solution)/shard_map/all_to_all | solution.py:36
  139.3 1.9 shard_map.99
  141.2 1.3 collective-permute-start.14
  143.9 46.6 %collective-permute-done.14 = bf16[64,512]{1,0:T(8,128)(2,1)S(1)} collective-permute-done((bf16[64,512]{1,0:T(8,128)(2,1)S(1)}, bf16[64,512]{1,0:T(8,128)(2,1)S(1)}, u32[]{:S(2)}, u32[]{:S(2)}) %collective-permute-start.14) | collective-permute-done | bytes 65568 | tf_op jit(solution)/shard_map/ppermute | solution.py:26
  191.0 12.0 %all_to_all.56 = bf16[16,80,128]{2,1,0:T(8,128)(2,1)S(1)} all-to-all(bf16[16,80,128]{2,1,0:T(8,128)(2,1)S(1)} %broadcast_in_dim.5), channel_id=1, replica_groups=mesh['section'=8,'tensor'=16] {'tensor'}, dimensions={0} | all-to-all | bytes 655360 | tf_op jit(solution)/shard_map/all_to_all | solution.py:36
  203.2 1.2 collective-permute-done.18
  (61 shorter events, 8.3 us)
Async XLA Ops:
  0.0 1.3 copy-start
  1.5 1.3 collective-permute-start.5
  3.0 8.8 %collective-permute-start.9 = (bf16[16,512,256]{2,1,0:T(8,128)(2,1)}, bf16[16,512,256]{2,1,0:T(8,128)(2,1)}, u32[]{:S(2)}, u32[]{:S(2)}) collective-permute-start(bf16[16,512,256]{2,1,0:T(8,128)(2,1)} %bitcast.16), channel_id=1, source_target_pairs={{0,16},{16,0},{32,48},{48,32},{64,80},{80,64},{96,112},{112,96},{1... | collective-permute-start | bytes 12582920 | tf_op jit(solution)/shard_map/ppermute | solution.py:21
  3.2 8.0 %collective-permute-start.6 = (bf16[64,512]{1,0:T(8,128)(2,1)S(1)}, bf16[64,512]{1,0:T(8,128)(2,1)S(1)}, u32[]{:S(2)}, u32[]{:S(2)}) collective-permute-start(bf16[64,512]{1,0:T(8,128)(2,1)S(1)} %fusion), channel_id=1, source_target_pairs={{0,32},{16,48},{32,64},{48,80},{64,96},{80,112},{96,0},{112,16},{1... | collective-permute-start | bytes 196616 | tf_op jit(solution)/shard_map/ppermute | solution.py:32
  4.8 6.5 %collective-permute-start.7 = (bf16[64,512]{1,0:T(8,128)(2,1)S(1)}, bf16[64,512]{1,0:T(8,128)(2,1)S(1)}, u32[]{:S(2)}, u32[]{:S(2)}) collective-permute-start(bf16[64,512]{1,0:T(8,128)(2,1)S(1)} %fusion), channel_id=1, source_target_pairs={{0,64},{16,80},{32,96},{48,112},{64,0},{80,16},{96,32},{112,48},{1... | collective-permute-start | bytes 196616 | tf_op jit(solution)/shard_map/ppermute | solution.py:32
  7.5 4.3 %collective-permute-start.8 = (bf16[64,512]{1,0:T(8,128)(2,1)S(1)}, bf16[64,512]{1,0:T(8,128)(2,1)S(1)}, u32[]{:S(2)}, u32[]{:S(2)}) collective-permute-start(bf16[64,512]{1,0:T(8,128)(2,1)S(1)} %fusion), channel_id=1, source_target_pairs={{0,96},{16,112},{32,0},{48,16},{64,32},{80,48},{96,64},{112,80},{1... | collective-permute-start | bytes 196616 | tf_op jit(solution)/shard_map/ppermute | solution.py:32
  9.0 2.8 %collective-permute-start.10 = (f32[1,8192]{1,0:T(1,128)}, f32[1,8192]{1,0:T(1,128)S(1)}, u32[]{:S(2)}, u32[]{:S(2)}) collective-permute-start(f32[1,8192]{1,0:T(1,128)} %gain_ref.4), channel_id=1, source_target_pairs={{0,16},{16,0},{32,48},{48,32},{64,80},{80,64},{96,112},{112,96},{1... | collective-permute-start | bytes 98312 | tf_op jit(solution)/shard_map/ppermute | solution.py:21
  11.8 27.5 %copy-start.6 = (f32[1,8192]{1,0:T(1,128)S(1)}, f32[1,8192]{1,0:T(1,128)}, u32[]{:S(2)}) copy-start(f32[1,8192]{1,0:T(1,128)} %get-tuple-element.84.gain_ref) | copy-start | bytes 98308 | tf_op jit(solution)/shard_map/cond
  13.5 25.8 %all-to-all-start = ((bf16[16,64,512]{2,1,0:T(8,128)(2,1)}), bf16[16,64,512]{2,1,0:T(8,128)(2,1)S(1)}, u32[]{:S(2)}, u32[]{:S(2)}) async-start(bf16[16,64,512]{2,1,0:T(8,128)(2,1)} %get-tuple-element.83), calls=%async_computation | async-start | bytes 2097152 | tf_op jit(solution)/shard_map/cond/branch_0_fun/all_to_all | solution.py:36
  26.2 1.4 collective-permute-start
  45.9 20.5 %all-to-all-start.1 = ((bf16[16,64,512]{2,1,0:T(8,128)(2,1)}), bf16[16,64,512]{2,1,0:T(8,128)(2,1)S(1)}, u32[]{:S(2)}, u32[]{:S(2)}) async-start(bf16[16,64,512]{2,1,0:T(8,128)(2,1)} %branch_0_fun.10), calls=%async_computation.1 | async-start | bytes 2097152 | tf_op jit(solution)/shard_map/cond/branch_0_fun/all_to_all | solution.py:36
  67.8 3.5 %collective-permute-start.11 = (bf16[64,512]{1,0:T(8,128)(2,1)}, bf16[64,512]{1,0:T(8,128)(2,1)S(1)}, u32[]{:S(2)}, u32[]{:S(2)}) collective-permute-start(bf16[64,512]{1,0:T(8,128)(2,1)} %get-tuple-element.157), channel_id=1, source_target_pairs={{0,32},{16,48},{1,33},{17,49},{2,34},{18,50},{3,35},{19,51},{4,36}... | collective-permute-start | bytes 196616 | tf_op jit(solution)/shard_map/ppermute | solution.py:26
  69.1 2.2 %copy-start.5 = (f32[1,8192]{1,0:T(1,128)S(1)}, f32[1,8192]{1,0:T(1,128)}, u32[]{:S(2)}) copy-start(f32[1,8192]{1,0:T(1,128)} %gain_ref.4) | copy-start | bytes 98308
  72.7 3.1 %collective-permute-start.12 = (bf16[64,512]{1,0:T(8,128)(2,1)S(1)}, bf16[64,512]{1,0:T(8,128)(2,1)S(1)}, u32[]{:S(2)}, u32[]{:S(2)}) collective-permute-start(bf16[64,512]{1,0:T(8,128)(2,1)S(1)} %get-tuple-element.195), channel_id=1, source_target_pairs={{32,64},{48,80},{33,65},{49,81},{34,66},{50,82},{35,67},{51,83},{3... | collective-permute-start | bytes 196616 | tf_op jit(solution)/shard_map/ppermute | solution.py:26
  75.8 31.2 %copy-start.2 = (bf16[16,512,256]{2,1,0:T(8,128)(2,1)S(1)}, bf16[16,512,256]{2,1,0:T(8,128)(2,1)}, u32[]{:S(2)}) copy-start(bf16[16,512,256]{2,1,0:T(8,128)(2,1)} %get-tuple-element.167.cut_ref) | copy-start | bytes 12582916
  77.2 32.4 %copy-start.1 = (bf16[16,512,256]{2,1,0:T(8,128)(2,1)S(1)}, bf16[16,512,256]{2,1,0:T(8,128)(2,1)}, u32[]{:S(2)}) copy-start(bf16[16,512,256]{2,1,0:T(8,128)(2,1)} %get-tuple-element.169.source_ref.cut_ref) | copy-start | bytes 12582916
  108.9 0.7 collective-permute-start.13
  111.0 32.9 %copy-start.9 = (bf16[512,64]{0,1:T(8,128)(2,1)S(1)}, bf16[512,64]{0,1:T(8,128)(2,1)}, u32[]{:S(2)}) copy-start(bf16[512,64]{0,1:T(8,128)(2,1)} %constant_dynamic-slice_fusion) | copy-start | bytes 196612
  141.2 49.3 %collective-permute-start.14 = (bf16[64,512]{1,0:T(8,128)(2,1)S(1)}, bf16[64,512]{1,0:T(8,128)(2,1)S(1)}, u32[]{:S(2)}, u32[]{:S(2)}) collective-permute-start(bf16[64,512]{1,0:T(8,128)(2,1)S(1)} %shard_map.99), channel_id=1, source_target_pairs={{96,0},{112,16},{97,1},{113,17},{98,2},{114,18},{99,3},{115,19},{1... | collective-permute-start | bytes 196616 | tf_op jit(solution)/shard_map/ppermute | solution.py:26
  142.5 48.0 %collective-permute-start.15 = (bf16[64,512]{1,0:T(8,128)(2,1)S(1)}, bf16[64,512]{1,0:T(8,128)(2,1)S(1)}, u32[]{:S(2)}, u32[]{:S(2)}) collective-permute-start(bf16[64,512]{1,0:T(8,128)(2,1)S(1)} %shard_map.99), channel_id=1, source_target_pairs={{96,32},{112,48},{97,33},{113,49},{98,34},{114,50},{99,35},{115,51... | collective-permute-start | bytes 196616 | tf_op jit(solution)/shard_map/ppermute | solution.py:26
  143.1 47.4 %collective-permute-start.16 = (bf16[64,512]{1,0:T(8,128)(2,1)S(1)}, bf16[64,512]{1,0:T(8,128)(2,1)S(1)}, u32[]{:S(2)}, u32[]{:S(2)}) collective-permute-start(bf16[64,512]{1,0:T(8,128)(2,1)S(1)} %shard_map.99), channel_id=1, source_target_pairs={{96,64},{112,80},{97,65},{113,81},{98,66},{114,82},{99,67},{115,83... | collective-permute-start | bytes 196616 | tf_op jit(solution)/shard_map/ppermute | solution.py:26
  143.8 46.9 %collective-permute-start.17 = (bf16[512,64]{0,1:T(8,128)(2,1)S(1)}, bf16[512,64]{0,1:T(8,128)(2,1)S(1)}, u32[]{:S(2)}, u32[]{:S(2)}) collective-permute-start(bf16[512,64]{0,1:T(8,128)(2,1)S(1)} %copy-done.9), channel_id=1, source_target_pairs={{0,16},{16,0},{32,48},{48,32},{64,80},{80,64},{96,112},{112,96},{1... | collective-permute-start | bytes 196616 | tf_op jit(solution)/shard_map/ppermute | solution.py:21
  203.2 1.2 collective-permute-start.18
